TPU v7x, 32 devices: a whole 2x2x4 slice. The times are simulated.
32 devices in a mesh: dp: 8 (over z, y), seq: 4 (over x, core).
Axes of the slice: x: 2, y: 2, z: 4, core: 2. Of those that a mesh axis runs over, the one named last changes fastest.
Arguments:
- char_ids: int32 [16384], P(('dp', 'seq')), may hold values from 0 to 255
- char_table: bfloat16 [1024, 256], P(('dp', 'seq')), may hold values from -6 to 6
- attn_gain: bfloat16 [1024], P(('dp', 'seq')), may hold values from 0.5 to 1.5
- query_weight: bfloat16 [1024, 1024], P(('dp', 'seq')), may hold values from -0.1875 to 0.1875
- key_weight: bfloat16 [1024, 1024], P(('dp', 'seq')), may hold values from -0.1875 to 0.1875
- value_weight: bfloat16 [1024, 1024], P(('dp', 'seq')), may hold values from -0.1875 to 0.1875
- out_weight: bfloat16 [1024, 1024], P(('dp', 'seq')), may hold values from -1 to 1
- state_key_weight: bfloat16 [1024, 1024], P(('dp', 'seq')), may hold values from -0.1875 to 0.1875
- state_value_weight: bfloat16 [1024, 1024], P(('dp', 'seq')), may hold values from -0.1875 to 0.1875
- update_weight: bfloat16 [1024, 1024], P(('dp', 'seq')), may hold values from -1 to 1
- state_query: bfloat16 [1024, 512], P(('dp', 'seq')), may hold values from -6 to 6
- state_init: bfloat16 [1024, 512], P(('dp', 'seq')), may hold values from -6 to 6
- gate_bias: bfloat16 [1024], P(('dp', 'seq')), may hold values from -1 to 6
- position_table: bfloat16 [8, 512], replicated, may hold values from -5 to 5
- mlp_gain: bfloat16 [1024], P(('dp', 'seq')), may hold values from 0.5 to 1.5
- up_weight: bfloat16 [1024, 4096], P(('dp', 'seq')), may hold values from -0.1875 to 0.1875
- up_bias: bfloat16 [4096], P(('dp', 'seq')), may hold values from -3 to 3
- down_weight: bfloat16 [4096, 1024], P(('dp', 'seq')), may hold values from -0.09375 to 0.09375
- down_bias: bfloat16 [1024], P(('dp', 'seq')), may hold values from -3 to 3
- out_grad: bfloat16 [16384, 1024], P(('dp', 'seq')), may hold values from -6 to 6
Outputs:
- output: bfloat16 [16384, 1024], P(('dp', 'seq'))
- embedded_grad: float32 [16384, 1024], P(('dp', 'seq'))
- char_table_grad: float32 [1024, 256], P(('dp', 'seq'))
- attn_gain_grad: float32 [1024], P(('dp', 'seq'))
- query_weight_grad: float32 [1024, 1024], P(('dp', 'seq'))
- key_weight_grad: float32 [1024, 1024], P(('dp', 'seq'))
- value_weight_grad: float32 [1024, 1024], P(('dp', 'seq'))
- out_weight_grad: float32 [1024, 1024], P(('dp', 'seq'))
- state_key_matrix_gradient: float32 [1024, 1024], P(('dp', 'seq'))
- state_value_weight_grad: float32 [1024, 1024], P(('dp', 'seq'))
- update_weight_grad: float32 [1024, 1024], P(('dp', 'seq'))
- state_query_grad: float32 [1024, 512], P(('dp', 'seq'))
- state_init_grad: float32 [1024, 512], P(('dp', 'seq'))
- gate_bias_grad: float32 [1024], P(('dp', 'seq'))
- position_table_grad: float32 [8, 512], replicated
- mlp_gain_grad: float32 [1024], P(('dp', 'seq'))
- up_weight_grad: float32 [1024, 4096], P(('dp', 'seq'))
- up_bias_grad: float32 [4096], P(('dp', 'seq'))
- down_weight_grad: float32 [4096, 1024], P(('dp', 'seq'))
- down_bias_grad: float32 [1024], P(('dp', 'seq'))
All inputs are finite; a program needn't handle non-finite values.
Results may differ from a plain program's by a relative error of at most 0.03.
Values may be sent and summed in bfloat16 or wider, within the bound.
No kernel may reach another device: no remote copies, remote signals or barrier semaphores. Data moves between devices by JAX's collectives and lax.ppermute only.
A program may use at most 320 MiB of HBM per device.

v0:
```python
import jax
import jax.numpy as jnp
from jax import lax
from jax.sharding import PartitionSpec as P

D = 1024
HEADS = 8
HD = 128
NSTATE = 512
VOCAB = 256
BLK = 512


def from_behind(block, axis, distance):
    devices = range(lax.axis_size(axis))
    route = [(i - distance, i) for i in devices if i - distance in devices]
    return lax.ppermute(block, axis, route)


def entering(shard, axis, combine, identity, reverse):
    devices, mine = (lax.axis_size(axis), lax.axis_index(axis))
    everything = jax.tree.map(
        lambda part, kind: lax.all_gather(part.astype(kind), axis),
        shard,
        (jnp.bfloat16, jnp.bfloat16),
    )
    start = jax.tree.map(
        lambda part, zero: jnp.broadcast_to(jnp.asarray(zero, part.dtype), part.shape),
        shard,
        identity,
    )

    def turn(k, before):
        at = devices - 1 - k if reverse else k
        reached = at > mine if reverse else at < mine
        new = combine(
            before, jax.tree.map(lambda part, own: part[at].astype(own.dtype), everything, shard)
        )
        return jax.tree.map(lambda a, b: jnp.where(reached, a, b), new, before)

    return lax.fori_loop(0, devices, turn, start)


def matrix_product(left_side, right_side):
    return jnp.dot(left_side, right_side, preferred_element_type=jnp.float32)


def matrix_product_transposed_left(left_side, right_side):
    return lax.dot_general(
        left_side, right_side, (((0,), (0,)), ((), ())), preferred_element_type=jnp.float32
    )


def matrix_product_transposed_right(left_side, right_side):
    return lax.dot_general(
        left_side, right_side, (((1,), (1,)), ((), ())), preferred_element_type=jnp.float32
    )


def rms_norm(values, scale_gain):
    return values * lax.rsqrt(jnp.mean(values * values, -1, keepdims=True) + 1e-06) * scale_gain


def softmax_rows(scores):
    shifted = scores - jnp.max(scores, -1, keepdims=True)
    powers = jnp.exp(shifted)
    return powers / jnp.sum(powers, -1, keepdims=True)


def position_bias(bias_table):
    heads = bias_table.shape[0]
    width = bias_table.shape[1]
    base_row = jnp.concatenate(
        [
            jnp.zeros((heads, 1), jnp.float32),
            jnp.flip(bias_table, 1),
            jnp.zeros((heads, width), jnp.float32),
        ],
        1,
    )
    repeated = jnp.broadcast_to(base_row[:, None, :], (heads, width, 2 * width + 1)).reshape(
        heads, -1
    )
    skewed = repeated[:, : width * 2 * width].reshape(heads, width, 2 * width)
    padding = jnp.zeros((heads, width, NSTATE), jnp.float32)
    return jnp.concatenate([skewed, padding], 2)


def diagonal_sums(token_grads):
    heads = token_grads.shape[0]
    width = token_grads.shape[1]
    flat = token_grads.reshape(heads, -1)
    flat = jnp.concatenate([flat, jnp.zeros((heads, width), jnp.float32)], 1)
    skewed = flat.reshape(heads, width, 2 * width + 1)
    return jnp.flip(jnp.sum(skewed[:, :, 1 : width + 1], 1), 1)


def position_mask(is_first):
    row_pos = jnp.arange(BLK)[:, None]
    col_pos = jnp.arange(2 * BLK)[None, :]
    distance = row_pos - col_pos + BLK
    allowed = (distance >= 0) & (distance < BLK) & ((col_pos >= BLK) | jnp.logical_not(is_first))
    return jnp.concatenate([allowed, jnp.ones((BLK, NSTATE), jnp.bool_)], 1)


def combine(earlier_pair, later_pair):
    return (earlier_pair[0] * later_pair[0], later_pair[0] * earlier_pair[1] + later_pair[1])


def attention_scores(query_heads, keys_all, pos_bias, allowed):
    raw_scores = jnp.einsum(
        "ihd,jhd->hij", query_heads, keys_all, preferred_element_type=jnp.float32
    )
    return jnp.where(allowed[None], raw_scores * HD ** (-0.5) + pos_bias, -1e30)


def shards(
    char_ids,
    char_table,
    attn_gain,
    query_weight,
    key_weight,
    value_weight,
    out_weight,
    state_key_weight,
    state_value_weight,
    update_weight,
    state_query,
    state_init,
    gate_bias,
    position_table,
    mlp_gain,
    up_weight,
    up_bias,
    down_weight,
    down_bias,
    out_grad,
):
    attn_shards = (
        char_table,
        attn_gain,
        query_weight,
        key_weight,
        value_weight,
        out_weight,
        state_key_weight,
        state_value_weight,
        update_weight,
        state_query,
        state_init,
        gate_bias,
    )
    mlp_shards = (mlp_gain, up_weight, up_bias, down_weight, down_bias)
    attn_full = (
        lax.all_gather(attn_shards[0], ("dp", "seq"), axis=0, tiled=True),
        lax.all_gather(attn_shards[1], ("dp", "seq"), axis=0, tiled=True),
        lax.all_gather(attn_shards[2], ("dp", "seq"), axis=0, tiled=True),
        lax.all_gather(attn_shards[3], ("dp", "seq"), axis=0, tiled=True),
        lax.all_gather(attn_shards[4], ("dp", "seq"), axis=0, tiled=True),
        lax.all_gather(attn_shards[5], ("dp", "seq"), axis=0, tiled=True),
        lax.all_gather(attn_shards[6], ("dp", "seq"), axis=0, tiled=True),
        lax.all_gather(attn_shards[7], ("dp", "seq"), axis=0, tiled=True),
        lax.all_gather(attn_shards[8], ("dp", "seq"), axis=0, tiled=True),
        lax.all_gather(attn_shards[9], ("dp", "seq"), axis=0, tiled=True),
        lax.all_gather(attn_shards[10], ("dp", "seq"), axis=0, tiled=True),
        lax.all_gather(attn_shards[11], ("dp", "seq"), axis=0, tiled=True),
    )
    (
        table_full,
        gain_attn,
        query_full,
        key_full,
        value_full,
        out_full,
        state_key_complete,
        svalue_full,
        update_full,
        squery_full,
        sinit_full,
        gbias_full,
    ) = attn_full
    count_of_rows = char_ids.shape[0]
    score_scale = HD ** (-0.5)
    is_first = lax.axis_index("seq") == 0
    one_hot = (char_ids[:, None] == jnp.arange(VOCAB)[None, :]).astype(jnp.bfloat16)
    embedded = matrix_product_transposed_right(one_hot, table_full)
    normed, norm_back = jax.vjp(rms_norm, embedded, gain_attn.astype(jnp.float32))
    normed_low = normed.astype(jnp.bfloat16)
    query_now = matrix_product(normed_low, query_full).astype(jnp.bfloat16)
    key_now = matrix_product(normed_low, key_full).astype(jnp.bfloat16)
    value_now = matrix_product(normed_low, value_full).astype(jnp.bfloat16)
    previous = from_behind(jnp.stack([key_now, value_now]), "seq", 1)
    keep_gate = jax.nn.sigmoid(gbias_full.astype(jnp.float32))
    key_heads = key_now.reshape(count_of_rows, HEADS, HD)
    value_heads = value_now.reshape(count_of_rows, HEADS, HD)
    squery_heads = squery_full.reshape(HEADS, HD, NSTATE)
    state_raw = jnp.einsum(
        "hds,jhd->hsj", squery_heads, key_heads, preferred_element_type=jnp.float32
    )
    state_probs = softmax_rows(state_raw * score_scale)
    state_probs_low = state_probs.astype(jnp.bfloat16)
    state_mix = jnp.einsum(
        "hsj,jhd->shd", state_probs_low, value_heads, preferred_element_type=jnp.float32
    )
    state_mix = state_mix.reshape(NSTATE, D).astype(jnp.bfloat16)
    update = matrix_product(state_mix, update_full)
    unit_gain = jnp.ones_like(keep_gate)
    zero_state = jnp.zeros_like(update)
    prefix_gain, prefix_sum = entering(
        (keep_gate, (1.0 - keep_gate) * update), "seq", combine, (unit_gain, zero_state), False
    )
    state_prev = prefix_gain * jnp.transpose(sinit_full.astype(jnp.float32)) + prefix_sum
    state_reduced_precision = state_prev.astype(jnp.bfloat16)
    recurrent_state_key = matrix_product(state_reduced_precision, state_key_complete).astype(
        jnp.bfloat16
    )
    state_value = matrix_product(state_reduced_precision, svalue_full).astype(jnp.bfloat16)
    keys_all = jnp.concatenate([previous[0], key_now, recurrent_state_key], 0).reshape(
        2 * count_of_rows + NSTATE, HEADS, HD
    )
    values_all = jnp.concatenate([previous[1], value_now, state_value], 0).reshape(
        2 * count_of_rows + NSTATE, HEADS, HD
    )
    pos_bias = position_bias(position_table.astype(jnp.float32))
    allowed = position_mask(is_first)
    query_heads = query_now.reshape(count_of_rows, HEADS, HD)
    scores = attention_scores(query_heads, keys_all, pos_bias, allowed)
    row_max = jnp.max(scores, -1, keepdims=True)
    log_total = row_max + jnp.log(jnp.sum(jnp.exp(scores - row_max), -1, keepdims=True))
    attn_probs = jnp.exp(scores - log_total)
    attn_mixed = jnp.einsum(
        "hij,jhd->ihd",
        attn_probs.astype(jnp.bfloat16),
        values_all,
        preferred_element_type=jnp.float32,
    )
    attn_mixed = attn_mixed.reshape(count_of_rows, D).astype(jnp.bfloat16)
    hidden = embedded + matrix_product(attn_mixed, out_full)
    mlp_full = (
        lax.all_gather(mlp_shards[0], ("dp", "seq"), axis=0, tiled=True),
        lax.all_gather(mlp_shards[1], ("dp", "seq"), axis=0, tiled=True),
        lax.all_gather(mlp_shards[2], ("dp", "seq"), axis=0, tiled=True),
        lax.all_gather(mlp_shards[3], ("dp", "seq"), axis=0, tiled=True),
        lax.all_gather(mlp_shards[4], ("dp", "seq"), axis=0, tiled=True),
    )
    gain_mlp, up_full, upbias_full, down_full, downbias_full = mlp_full
    normed_mlp, norm_mlp_back = jax.vjp(rms_norm, hidden, gain_mlp.astype(jnp.float32))
    normed_mlp_low = normed_mlp.astype(jnp.bfloat16)
    up_pre = matrix_product(normed_mlp_low, up_full) + upbias_full.astype(jnp.float32)
    activation, gelu_back = jax.vjp(jax.nn.gelu, up_pre)
    activation_low = activation.astype(jnp.bfloat16)
    output = hidden + matrix_product(activation_low, down_full) + downbias_full.astype(jnp.float32)
    mlp_back = (
        lax.all_gather(mlp_shards[0], ("dp", "seq"), axis=0, tiled=True),
        lax.all_gather(mlp_shards[1], ("dp", "seq"), axis=0, tiled=True),
        lax.all_gather(mlp_shards[2], ("dp", "seq"), axis=0, tiled=True),
        lax.all_gather(mlp_shards[3], ("dp", "seq"), axis=0, tiled=True),
        lax.all_gather(mlp_shards[4], ("dp", "seq"), axis=0, tiled=True),
    )
    up_back = mlp_back[1]
    down_back = mlp_back[3]
    grad_out = out_grad.astype(jnp.float32)
    grad_down = grad_out.astype(jnp.bfloat16)
    down_bias_grad = jnp.sum(grad_out, 0)
    down_weight_grad = matrix_product_transposed_left(activation_low, grad_down)
    (grad_up_pre,) = gelu_back(matrix_product_transposed_right(grad_down, down_back))
    grad_up = grad_up_pre.astype(jnp.bfloat16)
    up_bias_grad = jnp.sum(grad_up.astype(jnp.float32), 0)
    up_weight_grad = matrix_product_transposed_left(normed_mlp_low, grad_up)
    grad_hidden_norm, mlp_gain_grad = norm_mlp_back(
        matrix_product_transposed_right(grad_up, up_back)
    )
    grad_hidden = grad_out + grad_hidden_norm
    mlp_grads = (
        lax.psum_scatter(mlp_gain_grad, ("dp", "seq"), scatter_dimension=0, tiled=True),
        lax.psum_scatter(up_weight_grad, ("dp", "seq"), scatter_dimension=0, tiled=True),
        lax.psum_scatter(up_bias_grad, ("dp", "seq"), scatter_dimension=0, tiled=True),
        lax.psum_scatter(down_weight_grad, ("dp", "seq"), scatter_dimension=0, tiled=True),
        lax.psum_scatter(down_bias_grad, ("dp", "seq"), scatter_dimension=0, tiled=True),
    )
    attn_back = (
        lax.all_gather(attn_shards[0], ("dp", "seq"), axis=0, tiled=True),
        lax.all_gather(attn_shards[1], ("dp", "seq"), axis=0, tiled=True),
        lax.all_gather(attn_shards[2], ("dp", "seq"), axis=0, tiled=True),
        lax.all_gather(attn_shards[3], ("dp", "seq"), axis=0, tiled=True),
        lax.all_gather(attn_shards[4], ("dp", "seq"), axis=0, tiled=True),
        lax.all_gather(attn_shards[5], ("dp", "seq"), axis=0, tiled=True),
        lax.all_gather(attn_shards[6], ("dp", "seq"), axis=0, tiled=True),
        lax.all_gather(attn_shards[7], ("dp", "seq"), axis=0, tiled=True),
        lax.all_gather(attn_shards[8], ("dp", "seq"), axis=0, tiled=True),
        lax.all_gather(attn_shards[9], ("dp", "seq"), axis=0, tiled=True),
        lax.all_gather(attn_shards[10], ("dp", "seq"), axis=0, tiled=True),
        lax.all_gather(attn_shards[11], ("dp", "seq"), axis=0, tiled=True),
    )
    (
        table_back,
        gain_back,
        query_back,
        key_back,
        value_back,
        out_back,
        state_key_backward,
        state_value_backward,
        update_back,
        squery_back,
        sinit_back,
        gbias_back,
    ) = attn_back
    grad_branch = grad_hidden.astype(jnp.bfloat16)
    out_weight_grad = matrix_product_transposed_left(attn_mixed, grad_branch)
    grad_mixed = (
        matrix_product_transposed_right(grad_branch, out_back)
        .astype(jnp.bfloat16)
        .reshape(count_of_rows, HEADS, HD)
    )
    scores = attention_scores(query_heads, keys_all, pos_bias, allowed)
    attn_probs = jnp.exp(scores - log_total)
    grad_values_all = jnp.einsum(
        "hij,ihd->jhd",
        attn_probs.astype(jnp.bfloat16),
        grad_mixed,
        preferred_element_type=jnp.float32,
    ).reshape(-1, D)
    grad_probs = jnp.einsum(
        "ihd,jhd->hij", grad_mixed, values_all, preferred_element_type=jnp.float32
    )
    grad_scores = attn_probs * (grad_probs - jnp.sum(attn_probs * grad_probs, -1, keepdims=True))
    grad_scores_low = grad_scores.astype(jnp.bfloat16)
    table_grad_local = diagonal_sums(grad_scores_low[:, :, : 2 * count_of_rows].astype(jnp.float32))
    grad_query = jnp.einsum(
        "hij,jhd->ihd", grad_scores_low, keys_all, preferred_element_type=jnp.float32
    )
    grad_query = (grad_query * score_scale).reshape(count_of_rows, D).astype(jnp.bfloat16)
    every_key_gradient = jnp.einsum(
        "hij,ihd->jhd", grad_scores_low, query_heads, preferred_element_type=jnp.float32
    )
    every_key_gradient = (every_key_gradient * score_scale).reshape(-1, D)
    grad_key_prev = every_key_gradient[:count_of_rows]
    grad_key_local = every_key_gradient[count_of_rows : 2 * count_of_rows]
    state_key_gradient = every_key_gradient[2 * count_of_rows :].astype(jnp.bfloat16)
    grad_value_prev = grad_values_all[:count_of_rows]
    grad_value_local = grad_values_all[count_of_rows : 2 * count_of_rows]
    state_value_gradient = grad_values_all[2 * count_of_rows :].astype(jnp.bfloat16)
    from_next = from_behind(
        jnp.stack([grad_key_prev, grad_value_prev]).astype(jnp.bfloat16), "seq", -1
    ).astype(jnp.float32)
    state_key_matrix_gradient = matrix_product_transposed_left(
        state_reduced_precision, state_key_gradient
    )
    state_value_weight_grad = matrix_product_transposed_left(
        state_reduced_precision, state_value_gradient
    )
    readout_gradient = matrix_product_transposed_right(
        state_key_gradient, state_key_backward
    ) + matrix_product_transposed_right(state_value_gradient, state_value_backward)
    later_gain, after_grad = entering(
        (keep_gate, readout_gradient), "seq", combine, (unit_gain, zero_state), True
    )
    gate_term = jnp.sum(after_grad * (state_prev - update), 0)
    gate_bias_grad = gate_term * keep_gate * (1.0 - keep_gate)
    state_init_grad = jnp.transpose(
        jnp.where(is_first, readout_gradient + keep_gate * after_grad, 0.0)
    )
    grad_update = ((1.0 - keep_gate) * after_grad).astype(jnp.bfloat16)
    update_weight_grad = matrix_product_transposed_left(state_mix, grad_update)
    grad_smix = (
        matrix_product_transposed_right(grad_update, update_back)
        .astype(jnp.bfloat16)
        .reshape(NSTATE, HEADS, HD)
    )
    grad_value_state = jnp.einsum(
        "hsj,shd->jhd", state_probs_low, grad_smix, preferred_element_type=jnp.float32
    ).reshape(count_of_rows, D)
    grad_sprobs = jnp.einsum(
        "shd,jhd->hsj", grad_smix, value_heads, preferred_element_type=jnp.float32
    )
    grad_sscores = state_probs * (
        grad_sprobs - jnp.sum(state_probs * grad_sprobs, -1, keepdims=True)
    )
    grad_sscores = grad_sscores.astype(jnp.bfloat16)
    state_query_grad = jnp.einsum(
        "hsj,jhd->hds", grad_sscores, key_heads, preferred_element_type=jnp.float32
    )
    state_query_grad = (state_query_grad * score_scale).reshape(D, NSTATE)
    grad_key_state = jnp.einsum(
        "hsj,hds->jhd",
        grad_sscores,
        squery_back.reshape(HEADS, HD, NSTATE),
        preferred_element_type=jnp.float32,
    )
    grad_key_state = (grad_key_state * score_scale).reshape(count_of_rows, D)
    grad_key = (grad_key_local + grad_key_state + from_next[0]).astype(jnp.bfloat16)
    grad_value = (grad_value_local + grad_value_state + from_next[1]).astype(jnp.bfloat16)
    query_weight_grad = matrix_product_transposed_left(normed_low, grad_query)
    key_weight_grad = matrix_product_transposed_left(normed_low, grad_key)
    value_weight_grad = matrix_product_transposed_left(normed_low, grad_value)
    grad_normed = (
        matrix_product_transposed_right(grad_query, query_back)
        + matrix_product_transposed_right(grad_key, key_back)
        + matrix_product_transposed_right(grad_value, value_back)
    )
    grad_embedded_norm, attn_gain_grad = norm_back(grad_normed)
    embedded_grad = grad_hidden + grad_embedded_norm
    char_table_grad = lax.dot_general(
        embedded_grad,
        one_hot.astype(jnp.float32),
        (((0,), (0,)), ((), ())),
        precision=lax.Precision.HIGHEST,
        preferred_element_type=jnp.float32,
    )
    attn_grads = (
        lax.psum_scatter(char_table_grad, ("dp", "seq"), scatter_dimension=0, tiled=True),
        lax.psum_scatter(attn_gain_grad, ("dp", "seq"), scatter_dimension=0, tiled=True),
        lax.psum_scatter(query_weight_grad, ("dp", "seq"), scatter_dimension=0, tiled=True),
        lax.psum_scatter(key_weight_grad, ("dp", "seq"), scatter_dimension=0, tiled=True),
        lax.psum_scatter(value_weight_grad, ("dp", "seq"), scatter_dimension=0, tiled=True),
        lax.psum_scatter(out_weight_grad, ("dp", "seq"), scatter_dimension=0, tiled=True),
        lax.psum_scatter(state_key_matrix_gradient, ("dp", "seq"), scatter_dimension=0, tiled=True),
        lax.psum_scatter(state_value_weight_grad, ("dp", "seq"), scatter_dimension=0, tiled=True),
        lax.psum_scatter(update_weight_grad, ("dp", "seq"), scatter_dimension=0, tiled=True),
        lax.psum_scatter(state_query_grad, ("dp", "seq"), scatter_dimension=0, tiled=True),
        lax.psum_scatter(state_init_grad, ("dp", "seq"), scatter_dimension=0, tiled=True),
        lax.psum_scatter(gate_bias_grad, ("dp", "seq"), scatter_dimension=0, tiled=True),
    )
    position_table_grad = lax.psum(table_grad_local, ("dp", "seq"))
    return (
        (output.astype(jnp.bfloat16), embedded_grad)
        + tuple(attn_grads)
        + (position_table_grad,)
        + tuple(mlp_grads)
    )


def solution(mesh):
    return jax.shard_map(
        shards,
        mesh=mesh,
        in_specs=(
            P(("dp", "seq")),
            P(("dp", "seq"), None),
            P(("dp", "seq")),
            P(("dp", "seq"), None),
            P(("dp", "seq"), None),
            P(("dp", "seq"), None),
            P(("dp", "seq"), None),
            P(("dp", "seq"), None),
            P(("dp", "seq"), None),
            P(("dp", "seq"), None),
            P(("dp", "seq"), None),
            P(("dp", "seq"), None),
            P(("dp", "seq")),
            P(),
            P(("dp", "seq")),
            P(("dp", "seq"), None),
            P(("dp", "seq")),
            P(("dp", "seq"), None),
            P(("dp", "seq")),
            P(("dp", "seq"), None),
        ),
        out_specs=(
            P(("dp", "seq"), None),
            P(("dp", "seq"), None),
            P(("dp", "seq"), None),
            P(("dp", "seq")),
            P(("dp", "seq"), None),
            P(("dp", "seq"), None),
            P(("dp", "seq"), None),
            P(("dp", "seq"), None),
            P(("dp", "seq"), None),
            P(("dp", "seq"), None),
            P(("dp", "seq"), None),
            P(("dp", "seq"), None),
            P(("dp", "seq"), None),
            P(("dp", "seq")),
            P(),
            P(("dp", "seq")),
            P(("dp", "seq"), None),
            P(("dp", "seq")),
            P(("dp", "seq"), None),
            P(("dp", "seq")),
        ),
        check_vma=False,
    )
```

profile of v0, /device:TPU:0, one launch (start us, length us, event | category | flops | bytes accessed | tf_op | source)
XLA Modules:
  0.0 2607.7 jit_solution(7938494973926946877)
XLA Ops:
  14.6 42.2 %all-reduce.13 = (bf16[1024]{0:T(1024)(128)(2,1)S(1)}, bf16[1024]{0:T(1024)(128)(2,1)S(1)}, bf16[1024]{0:T(1024)(128)(2,1)}, bf16[1024]{0:T(1024)(128)(2,1)S(1)}) all-reduce(bf16[1024]{0:T(1024)(128)(2,1)S(1)} %dynamic-update-slice, bf16[1024]{0:T(1024)(128)(2,1)S(1)} %dynamic-update-slice.1, ...), channel_id=1, replica_groups=mesh['dp'=8,'seq'=4] {'dp','seq'}, use_global_device_ids=true, to_apply=%add.3 | all-reduce | flops 4096 | bytes 16384
  56.8 42.7 %all_gather.81 = bf16[1024,256]{1,0:T(8,128)(2,1)S(1)} all-gather(bf16[32,256]{1,0:T(8,128)(2,1)} %param.25), channel_id=1, replica_groups=mesh['dp'=8,'seq'=4] {'dp','seq'}, dimensions={0}, use_global_device_ids=true | all-gather | bytes 540672 | tf_op jit(solution)/shard_map/all_gather | solution.py:155
  106.8 21.6 all-gather.18.cloned.1.call-done
  131.5 52.2 %all-gather.22.cloned.1.call-done = bf16[1024,512]{1,0:T(8,128)(2,1)} async-done(((bf16[32,512]{1,0:T(8,128)(2,1)}), bf16[1024,512]{1,0:T(8,128)(2,1)}) %all-gather.22.cloned.1.call-update) | async-done | bytes 1048592 | tf_op jit(solution)/shard_map/all_gather | solution.py:164
  201.2 40.6 %all-gather.24.cloned.1.call-done = bf16[1024,1024]{1,0:T(8,128)(2,1)} async-done(((bf16[32,1024]{1,0:T(8,128)(2,1)}), bf16[1024,1024]{1,0:T(8,128)(2,1)}) %all-gather.24.cloned.1.call-update) | async-done | bytes 2097168 | tf_op jit(solution)/shard_map/all_gather | solution.py:163
  260.3 59.9 %all-gather.3 = bf16[32,1,128]{2,1,0:T(2,128)(2,1)S(1)} all-gather(bf16[1,1,128]{2,1,0:T(2,128)(2,1)S(1)} %bitcast.242), channel_id=1, replica_groups=mesh['dp'=8,'seq'=4] {'dp','seq'}, dimensions={0}, use_global_device_ids=true | all-gather | bytes 8448 | tf_op jit(solution)/shard_map/all_gather | solution.py:242
  328.0 25.3 reshape.218
  376.0 18.8 copy.143
  426.4 23.1 all-gather.28.cloned.1.call-done
  456.0 51.7 %all-gather.32.cloned.1.call-done = bf16[1024,1024]{1,0:T(8,128)(2,1)} async-done(((bf16[32,1024]{1,0:T(8,128)(2,1)}), bf16[1024,1024]{1,0:T(8,128)(2,1)}) %all-gather.32.cloned.1.call-update) | async-done | bytes 2097168 | tf_op jit(solution)/shard_map/all_gather | solution.py:161
  570.2 74.7 %all-gather.36.cloned.1.call-done = bf16[1024,4096]{1,0:T(8,128)(2,1)} async-done(((bf16[32,4096]{1,0:T(8,128)(2,1)}), bf16[1024,4096]{1,0:T(8,128)(2,1)}) %all-gather.36.cloned.1.call-update) | async-done | bytes 8388624 | tf_op jit(solution)/shard_map/all_gather | solution.py:241
  656.9 66.8 %all-gather.38.cloned.1.call-done = bf16[4096,1024]{1,0:T(8,128)(2,1)} async-done(((bf16[128,1024]{1,0:T(8,128)(2,1)}), bf16[4096,1024]{1,0:T(8,128)(2,1)}) %all-gather.38.cloned.1.call-update) | async-done | bytes 8388624 | tf_op jit(solution)/shard_map/all_gather | solution.py:243
  986.5 19.5 reshape.220
  1041.8 66.4 %all-reduce.12 = (f32[1024]{0:T(1024)S(1)}, f32[1024]{0:T(1024)S(1)}, f32[8,512]{1,0:T(8,128)}, f32[1024]{0:T(1024)S(1)}, f32[4096]{0:T(1024)S(1)}, /*index=5*/f32[1024]{0:T(1024)S(1)}) all-reduce(f32[1024]{0:T(1024)S(1)} %get-tuple-element.366, ...), channel_id=6, replica_groups=mesh['dp'=8,'seq'=4] {'dp','seq'}, use_global_device_ids=true, to_apply=%region_16.17.clone | all-reduce | flops 12288 | bytes 98304
  1129.0 139.7 %reduce-scatter.17.cloned.1.call-done = f32[32,1024]{1,0:T(8,128)} async-done(((f32[1024,1024]{1,0:T(8,128)}), f32[32,1024]{1,0:T(8,128)}) %reduce-scatter.17.cloned.1.call-update) | async-done | bytes 131088 | tf_op jit(solution)/shard_map/reduce_scatter | solution.py:414
  1268.6 139.5 %reduce-scatter.25.cloned.1.call-done = f32[32,1024]{1,0:T(8,128)} async-done(((f32[1024,1024]{1,0:T(8,128)}), f32[32,1024]{1,0:T(8,128)}) %reduce-scatter.25.cloned.1.call-update) | async-done | bytes 131088 | tf_op jit(solution)/shard_map/reduce_scatter | solution.py:418
  1408.2 133.9 %reduce-scatter.15.cloned.1.call-done = f32[32,256]{1,0:T(8,128)} async-done(((f32[1024,256]{1,0:T(8,128)}), f32[32,256]{1,0:T(8,128)}) %reduce-scatter.15.cloned.1.call-update) | async-done | bytes 32784 | tf_op jit(solution)/shard_map/reduce_scatter | solution.py:412
  1542.1 135.2 %reduce-scatter.37.cloned.1.call-done = f32[32,512]{1,0:T(8,128)} async-done(((f32[1024,512]{1,0:T(8,128)}), f32[32,512]{1,0:T(8,128)}) %reduce-scatter.37.cloned.1.call-update) | async-done | bytes 65552
  1677.3 135.0 %reduce-scatter.31.cloned.1.call-done = f32[32,512]{1,0:T(8,128)} async-done(((f32[1024,512]{1,0:T(8,128)}), f32[32,512]{1,0:T(8,128)}) %reduce-scatter.31.cloned.1.call-update) | async-done | bytes 65552 | tf_op jit(solution)/shard_map/reduce_scatter | solution.py:421
  1812.3 139.9 %reduce-scatter.29.cloned.1.call-done = f32[32,1024]{1,0:T(8,128)} async-done(((f32[1024,1024]{1,0:T(8,128)}), f32[32,1024]{1,0:T(8,128)}) %reduce-scatter.29.cloned.1.call-update) | async-done | bytes 131088 | tf_op jit(solution)/shard_map/reduce_scatter | solution.py:420
  1952.2 139.7 %reduce-scatter.21.cloned.1.call-done = f32[32,1024]{1,0:T(8,128)} async-done(((f32[1024,1024]{1,0:T(8,128)}), f32[32,1024]{1,0:T(8,128)}) %reduce-scatter.21.cloned.1.call-update) | async-done | bytes 131088 | tf_op jit(solution)/shard_map/reduce_scatter | solution.py:416
  2091.9 139.7 %reduce-scatter.19.cloned.1.call-done = f32[32,1024]{1,0:T(8,128)} async-done(((f32[1024,1024]{1,0:T(8,128)}), f32[32,1024]{1,0:T(8,128)}) %reduce-scatter.19.cloned.1.call-update) | async-done | bytes 131088 | tf_op jit(solution)/shard_map/reduce_scatter | solution.py:415
  2231.6 181.5 %reduce-scatter.35.cloned.1.call-done = f32[128,1024]{1,0:T(8,128)} async-done(((f32[4096,1024]{1,0:T(8,128)}), f32[128,1024]{1,0:T(8,128)}) %reduce-scatter.35.cloned.1.call-update) | async-done | bytes 524304 | tf_op jit(solution)/shard_map/reduce_scatter | solution.py:278
  2413.1 187.7 %reduce-scatter.33.cloned.1.call-done = f32[32,4096]{1,0:T(8,128)} async-done(((f32[1024,4096]{1,0:T(8,128)}), f32[32,4096]{1,0:T(8,128)}) %reduce-scatter.33.cloned.1.call-update) | async-done | bytes 524304 | tf_op jit(solution)/shard_map/reduce_scatter | solution.py:276
  (380 shorter events, 535.5 us)
Async XLA Ops:
  8.7 175.1 %all-gather.22.cloned.1.call-start = ((), (), s32[]{:S(2)}) async-start(), calls=%async_computation.14 | async-start | bytes 1081344 | tf_op jit(solution)/shard_map/all_gather | solution.py:164
  9.4 232.4 %all-gather.24.cloned.1.call-start = ((), (), s32[]{:S(2)}) async-start(), calls=%async_computation.15 | async-start | bytes 2162688 | tf_op jit(solution)/shard_map/all_gather | solution.py:163
  10.0 386.0 %all-gather.26.cloned.1.call-start = ((), (), s32[]{:S(2)}) async-start(), calls=%async_computation.16 | async-start | bytes 1081344 | tf_op jit(solution)/shard_map/all_gather | solution.py:165
  10.6 387.7 %all-gather.30.cloned.1.call-start = ((), (), s32[]{:S(2)}) async-start(), calls=%async_computation.18 | async-start | bytes 2162688 | tf_op jit(solution)/shard_map/all_gather | solution.py:157
  11.1 402.8 %all-gather.40.cloned.1.call-start = ((), (), s32[]{:S(2)}) async-start(), calls=%async_computation.34 | async-start | bytes 5242880 | tf_op jit(solution)/shard_map/all_gather | solution.py:23
  246.5 203.0 %all-gather.28.cloned.1.call-start = ((), (), s32[]{:S(2)}) async-start(), calls=%async_computation.17 | async-start | bytes 2162688 | tf_op jit(solution)/shard_map/all_gather | solution.py:162
  247.2 260.4 %all-gather.32.cloned.1.call-start = ((), (), s32[]{:S(2)}) async-start(), calls=%async_computation.19 | async-start | bytes 2162688 | tf_op jit(solution)/shard_map/all_gather | solution.py:161
  248.0 317.7 %all-gather.34.cloned.1.call-start = ((), (), s32[]{:S(2)}) async-start(), calls=%async_computation.20 | async-start | bytes 2162688 | tf_op jit(solution)/shard_map/all_gather | solution.py:160
  248.6 396.3 %all-gather.36.cloned.1.call-start = ((), (), s32[]{:S(2)}) async-start(), calls=%async_computation.21 | async-start | bytes 8650752 | tf_op jit(solution)/shard_map/all_gather | solution.py:241
  249.3 474.4 %all-gather.38.cloned.1.call-start = ((), (), s32[]{:S(2)}) async-start(), calls=%async_computation.22 | async-start | bytes 8650752 | tf_op jit(solution)/shard_map/all_gather | solution.py:243
  249.9 601.9 %all-gather.42.cloned.1.call-start = ((), (), s32[]{:S(2)}) async-start(), calls=%async_computation.35 | async-start | bytes 5242880 | tf_op jit(solution)/shard_map/all_gather | solution.py:23
  251.4 153.3 %collective-permute-start = (bf16[2,512,1024]{2,1,0:T(8,128)(2,1)}, bf16[2,512,1024]{2,1,0:T(8,128)(2,1)}, u32[]{:S(2)}, u32[]{:S(2)}) collective-permute-start(bf16[2,512,1024]{2,1,0:T(8,128)(2,1)} %pad_maximum_fusion.1), channel_id=1, source_target_pairs={{0,1},{1,2},{2,3},{4,5},{5,6},{6,7},{8,9},{9,10},{10,11},{12,13},{... | collective-permute-start | bytes 6291464 | tf_op jit(solution)/shard_map/ppermute | solution.py:17
  811.4 299.7 %reduce-scatter.23.cloned.1.call-start = ((), (), s32[]{:S(2)}) async-start(), calls=%async_computation.27 | async-start | bytes 4325376 | tf_op jit(solution)/shard_map/reduce_scatter | solution.py:417
  814.8 314.2 %reduce-scatter.27.cloned.1.call-start = ((), (), s32[]{:S(2)}) async-start(), calls=%async_computation.29 | async-start | bytes 4325376 | tf_op jit(solution)/shard_map/reduce_scatter | solution.py:419
  819.9 448.8 %reduce-scatter.17.cloned.1.call-start = ((), (), s32[]{:S(2)}) async-start(), calls=%async_computation.24 | async-start | bytes 4325376 | tf_op jit(solution)/shard_map/reduce_scatter | solution.py:414
  834.2 574.0 %reduce-scatter.25.cloned.1.call-start = ((), (), s32[]{:S(2)}) async-start(), calls=%async_computation.28 | async-start | bytes 4325376 | tf_op jit(solution)/shard_map/reduce_scatter | solution.py:418
  842.1 700.0 %reduce-scatter.15.cloned.1.call-start = ((), (), s32[]{:S(2)}) async-start(), calls=%async_computation.23 | async-start | bytes 1081344 | tf_op jit(solution)/shard_map/reduce_scatter | solution.py:412
  902.2 775.1 %reduce-scatter.37.cloned.1.call-start = ((), (), s32[]{:S(2)}) async-start(), calls=%async_computation.36 | async-start | bytes 2162688
  910.7 901.6 %reduce-scatter.31.cloned.1.call-start = ((), (), s32[]{:S(2)}) async-start(), calls=%async_computation.31 | async-start | bytes 2162688 | tf_op jit(solution)/shard_map/reduce_scatter | solution.py:421
  915.3 1036.9 %reduce-scatter.29.cloned.1.call-start = ((), (), s32[]{:S(2)}) async-start(), calls=%async_computation.30 | async-start | bytes 4325376 | tf_op jit(solution)/shard_map/reduce_scatter | solution.py:420
  919.9 1171.9 %reduce-scatter.21.cloned.1.call-start = ((), (), s32[]{:S(2)}) async-start(), calls=%async_computation.26 | async-start | bytes 4325376 | tf_op jit(solution)/shard_map/reduce_scatter | solution.py:416
  924.7 1306.8 %reduce-scatter.19.cloned.1.call-start = ((), (), s32[]{:S(2)}) async-start(), calls=%async_computation.25 | async-start | bytes 4325376 | tf_op jit(solution)/shard_map/reduce_scatter | solution.py:415
  929.2 1483.8 %reduce-scatter.35.cloned.1.call-start = ((), (), s32[]{:S(2)}) async-start(), calls=%async_computation.33 | async-start | bytes 17301504 | tf_op jit(solution)/shard_map/reduce_scatter | solution.py:278
  946.0 1654.7 %reduce-scatter.33.cloned.1.call-start = ((), (), s32[]{:S(2)}) async-start(), calls=%async_computation.32 | async-start | bytes 17301504 | tf_op jit(solution)/shard_map/reduce_scatter | solution.py:276
  (94 other events, 2775.3 us)
Sparse Core Ops, SparseCore 0:
  10.9 59.2 all-gather.19
  73.0 55.2 all-gather.17
  131.2 52.4 all-gather.21
  186.5 55.3 all-gather.23
  244.6 52.6 all-gather.25
  300.0 55.3 all-gather.29
  356.9 33.3 all-gather.39
  393.1 56.3 all-gather.27
  452.4 55.2 all-gather.31
  510.4 55.2 all-gather.33
  568.5 76.2 all-gather.35
  647.6 76.0 all-gather.37
  847.6 141.7 reduce-scatter.22
  992.0 136.9 reduce-scatter.26
  1131.7 136.9 reduce-scatter.16
  1271.3 136.7 reduce-scatter.24
  1410.8 131.2 reduce-scatter.14
  1545.0 132.2 reduce-scatter.36
  1680.0 132.2 reduce-scatter.30
  1815.3 136.8 reduce-scatter.28
  1955.1 136.6 reduce-scatter.20
  2094.8 136.7 reduce-scatter.18
  2234.4 178.6 reduce-scatter.34
  2416.0 184.6 reduce-scatter.32
  (1 shorter events, 33.2 us)
where the time goes:
time: 2620 us; the launch traced here: 2610 us
  waiting for transfers between devices  1840 us (70%)
  matrix products  251 us (10%)
  blocking collectives  216 us (8%)
  local copies, waits for them, and re-layouts  196 us (7%)
  other arithmetic  79.9 us (3%)
    reduce_scatter x1, waiting for transfers between devices, shards(): lax.psum_scatter(up_weight_grad, ('dp', 'seq'), scatter_dimension=0, tile...  188 us
    reduce_scatter x1, waiting for transfers between devices, shards(): lax.psum_scatter(down_weight_grad, ('dp', 'seq'), scatter_dimension=0, ti...  181 us
    unnamed x26, waiting for transfers between devices  142 us
    reduce_scatter x1, waiting for transfers between devices, shards(): lax.psum_scatter(update_weight_grad, ('dp', 'seq'), scatter_dimension=0,...  140 us
    reduce_scatter x1, waiting for transfers between devices, shards(): lax.psum_scatter(key_weight_grad, ('dp', 'seq'), scatter_dimension=0, til...  140 us
    reduce_scatter x1, waiting for transfers between devices, shards(): lax.psum_scatter(value_weight_grad, ('dp', 'seq'), scatter_dimension=0, t...  140 us
    reduce_scatter x1, waiting for transfers between devices, shards(): lax.psum_scatter(query_weight_grad, ('dp', 'seq'), scatter_dimension=0, t...  140 us
    reduce_scatter x1, waiting for transfers between devices, shards(): lax.psum_scatter(state_key_matrix_gradient, ('dp', 'seq'), scatter_dimens...  140 us
  transfers between devices with their start and end apart: 27, of which 19 were waited for; matrix products, arithmetic and copies ran while one was open for 16% of the time, Pallas kernels for 0%

commit v1 on v0

--- a/solution.py
+++ b/solution.py
@@ -1,6 +1,10 @@
+import functools
+
 import jax
 import jax.numpy as jnp
 from jax import lax
+from jax.experimental import pallas as pl
+from jax.experimental.pallas import tpu as pltpu
 from jax.sharding import PartitionSpec as P
 
 D = 1024
@@ -9,7 +13,173 @@
 NSTATE = 512
 VOCAB = 256
 BLK = 512
-
+AX = ("dp", "seq")
+VEC = 128
+
+
+def f32(v):
+    return v.astype(jnp.float32)
+
+
+def low(v):
+    return v.astype(jnp.bfloat16)
+
+
+def route(move):
+    pairs = []
+    for z in range(4):
+        for y in range(2):
+            for x in range(2):
+                for c in range(2):
+                    tz, ty, tx, tc = move(z, y, x, c)
+                    pairs.append((z * 8 + y * 4 + x * 2 + c, tz * 8 + ty * 4 + tx * 2 + tc))
+    return pairs
+
+
+A_ROUTE = route(lambda z, y, x, c: (z, y, 1 - x, c) if c == 0 else (z, 1 - y, x, c))
+B_ROUTE = route(lambda z, y, x, c: (z, 1 - y, x, c) if c == 0 else (z, y, 1 - x, c))
+CORE_ROUTE = route(lambda z, y, x, c: (z, y, x, 1 - c))
+X_ROUTE = route(lambda z, y, x, c: (z, y, 1 - x, c))
+Z_ROUTE = {k: route(lambda z, y, x, c, k=k: ((z + k) % 4, y, x, c)) for k in (1, 2, 3)}
+
+
+def place():
+    d, s = lax.axis_index("dp"), lax.axis_index("seq")
+    return d // 2, d % 2, s // 2, s % 2
+
+
+def send(v, pairs):
+    return lax.ppermute(v, AX, pairs)
+
+
+def stack_z(shard, *others):
+    def body(*refs):
+        z = lax.axis_index("dp") // 2
+        for i, src in enumerate(refs[:4]):
+            refs[4][lax.rem(z + 4 - i, 4)] = src[...]
+
+    return pl.pallas_call(
+        body, out_shape=jax.ShapeDtypeStruct((4,) + shard.shape, shard.dtype), name="stack_z"
+    )(shard, *others)
+
+
+def assemble(pieces, layout):
+    rows, width = pieces[0].shape[1:]
+
+    def body(*refs):
+        ins, outs = refs[:8], refs[8:]
+        y = lax.rem(lax.axis_index("dp"), 2)
+        s = lax.axis_index("seq")
+        x, c = s // 2, lax.rem(s, 2)
+        for i, src in enumerate(ins):
+            core = c if i < 4 else 1 - c
+            flip_x = (0, 1 - core, core, 1)[i % 4]
+            flip_y = (0, core, 1 - core, 1)[i % 4]
+            tx, ty = lax.rem(x + flip_x, 2), lax.rem(y + flip_y, 2)
+            for (first, w, folds), out in zip(layout, outs):
+                for q in range(folds):
+                    out[0, ty, tx, core, q * rows : (q + 1) * rows, :] = src[
+                        0, :, first + q * w : first + (q + 1) * w
+                    ]
+
+    full = pl.pallas_call(
+        body,
+        out_shape=[
+            jax.ShapeDtypeStruct((4, 2, 2, 2, rows * n, w), pieces[0].dtype) for _, w, n in layout
+        ],
+        grid=(4,),
+        in_specs=[pl.BlockSpec((1, rows, width), lambda z: (z, 0, 0))] * 8,
+        out_specs=[
+            pl.BlockSpec((1, 2, 2, 2, rows * n, w), lambda z: (z, 0, 0, 0, 0, 0))
+            for _, w, n in layout
+        ],
+        compiler_params=pltpu.CompilerParams(vmem_limit_bytes=40 * 2**20),
+        name="assemble",
+    )(*pieces)
+    return [o.reshape(32 * rows * n, w) for o, (_, w, n) in zip(full, layout)]
+
+
+def gather(shard, layout, after=None):
+    if after is not None:
+        shard, _ = lax.optimization_barrier((shard, after))
+    others = [send(shard, Z_ROUTE[k]) for k in (1, 2, 3)]
+    p = stack_z(shard, *others)
+    pa, pb, qp = send(p, A_ROUTE), send(p, B_ROUTE), send(p, CORE_ROUTE)
+    pd, qa, qb = send(pa, B_ROUTE), send(pa, CORE_ROUTE), send(pb, CORE_ROUTE)
+    qd = send(pd, CORE_ROUTE)
+    return assemble((p, pa, pb, pd, qp, qa, qb, qd), layout), p
+
+
+def scatter(grad):
+    total, width = grad.shape
+    rows = total // 32
+    z, y, x, c = place()
+    parts = low(grad).reshape(4, 2, 2, 2, rows, width)
+
+    def pick(a, i, axis):
+        return lax.dynamic_index_in_dim(a, i, axis, keepdims=False)
+
+    keep = pick(parts, c, 3)
+    got = send(pick(parts, 1 - c, 3), CORE_ROUTE)
+
+    def part(ty, tx):
+        at = [
+            lax.dynamic_slice(a, (0, ty, tx, 0, 0), (4, 1, 1, rows, width)) for a in (keep, got)
+        ]
+        return (f32(at[0]) + f32(at[1])).reshape(4, rows, width)
+
+    ax, ay = jnp.where(c == 0, 1 - x, x), jnp.where(c == 0, y, 1 - y)
+    bx, by = jnp.where(c == 0, x, 1 - x), jnp.where(c == 0, 1 - y, y)
+    across = send(low(part(1 - y, 1 - x)), B_ROUTE)
+    from_b = send(low(part(by, bx)), B_ROUTE)
+    from_a = send(low(part(ay, ax) + f32(across)), A_ROUTE)
+    own = part(y, x) + f32(from_a) + f32(from_b)
+    rest = [send(low(pick(own, (z + k) % 4, 0)), Z_ROUTE[k]) for k in (1, 2, 3)]
+    return pick(own, z, 0) + f32(rest[0]) + f32(rest[1]) + f32(rest[2])
+
+
+def gather_any(shard, layout, after=None):
+    rows = shard.shape[0]
+    full = lax.all_gather(shard, AX, axis=0, tiled=True)
+    outs = []
+    for first, w, folds in layout:
+        part = full[:, first : first + w * folds]
+        if folds > 1:
+            part = part.reshape(-1, rows, folds, w).transpose(0, 2, 1, 3).reshape(-1, w)
+        outs.append(part)
+    return outs, full
+
+
+def scatter_any(grad):
+    return lax.psum_scatter(f32(grad), AX, scatter_dimension=0, tiled=True)
+
+
+def earlier_sum(keep_gate, mine, start):
+    z, y, x, c = place()
+    sibling = send(mine, CORE_ROUTE)
+    first = jnp.where(c == 0, f32(mine), f32(sibling))
+    second = jnp.where(c == 0, f32(sibling), f32(mine))
+    chip = low(keep_gate * first + second)
+    half = NSTATE // 2
+    near = send(lax.dynamic_slice(chip, (c * half, 0), (half, D)), X_ROUTE)
+    far = send(near, CORE_ROUTE)
+    other = jnp.concatenate([jnp.where(c == 0, near, far), jnp.where(c == 0, far, near)], 0)
+    before = jnp.where(x == 0, start, keep_gate * keep_gate * start + f32(other))
+    return jnp.where(c == 0, before, keep_gate * before + f32(sibling))
+
+
+def later_sum(keep_gate, mine):
+    z, y, x, c = place()
+    sibling = send(mine, CORE_ROUTE)
+    first = jnp.where(c == 0, f32(mine), f32(sibling))
+    second = jnp.where(c == 0, f32(sibling), f32(mine))
+    chip = low(first + keep_gate * second)
+    half = NSTATE // 2
+    near = send(lax.dynamic_slice(chip, (c * half, 0), (half, D)), X_ROUTE)
+    far = send(near, CORE_ROUTE)
+    other = jnp.concatenate([jnp.where(c == 0, near, far), jnp.where(c == 0, far, near)], 0)
+    after = jnp.where(x == 0, f32(other), 0.0)
+    return jnp.where(c == 0, f32(sibling) + keep_gate * after, after)
 
 def from_behind(block, axis, distance):
     devices = range(lax.axis_size(axis))
@@ -115,6 +285,7 @@
 
 
 def shards(
+    fast,
     char_ids,
     char_table,
     attn_gain,
@@ -136,49 +307,42 @@
     down_bias,
     out_grad,
 ):
-    attn_shards = (
-        char_table,
-        attn_gain,
-        query_weight,
-        key_weight,
-        value_weight,
-        out_weight,
-        state_key_weight,
-        state_value_weight,
-        update_weight,
-        state_query,
-        state_init,
-        gate_bias,
-    )
-    mlp_shards = (mlp_gain, up_weight, up_bias, down_weight, down_bias)
-    attn_full = (
-        lax.all_gather(attn_shards[0], ("dp", "seq"), axis=0, tiled=True),
-        lax.all_gather(attn_shards[1], ("dp", "seq"), axis=0, tiled=True),
-        lax.all_gather(attn_shards[2], ("dp", "seq"), axis=0, tiled=True),
-        lax.all_gather(attn_shards[3], ("dp", "seq"), axis=0, tiled=True),
-        lax.all_gather(attn_shards[4], ("dp", "seq"), axis=0, tiled=True),
-        lax.all_gather(attn_shards[5], ("dp", "seq"), axis=0, tiled=True),
-        lax.all_gather(attn_shards[6], ("dp", "seq"), axis=0, tiled=True),
-        lax.all_gather(attn_shards[7], ("dp", "seq"), axis=0, tiled=True),
-        lax.all_gather(attn_shards[8], ("dp", "seq"), axis=0, tiled=True),
-        lax.all_gather(attn_shards[9], ("dp", "seq"), axis=0, tiled=True),
-        lax.all_gather(attn_shards[10], ("dp", "seq"), axis=0, tiled=True),
-        lax.all_gather(attn_shards[11], ("dp", "seq"), axis=0, tiled=True),
-    )
-    (
-        table_full,
-        gain_attn,
-        query_full,
-        key_full,
-        value_full,
-        out_full,
-        state_key_complete,
-        svalue_full,
-        update_full,
-        squery_full,
-        sinit_full,
-        gbias_full,
-    ) = attn_full
+    take, add = (gather, scatter) if fast else (gather_any, scatter_any)
+    rows = attn_gain.shape[0]
+    vectors = jnp.concatenate(
+        [v.reshape(rows, -1) for v in (attn_gain, mlp_gain, gate_bias, down_bias, up_bias)], 1
+    )
+    vectors = jnp.pad(vectors, ((0, 0), (0, VEC - vectors.shape[1])))
+    ff = up_weight.shape[1]
+    folds = ff // D
+    (table_vec, qkv_full, squery_full), ahead = take(
+        jnp.concatenate(
+            [char_table, vectors, query_weight, key_weight, value_weight, state_query], 1
+        ),
+        ((0, VOCAB + VEC, 1), (VOCAB + VEC, 3 * D, 1), (VOCAB + VEC + 3 * D, NSTATE, 1)),
+    )
+    (sinit_full, update_full, skv_full, out_full), ahead = take(
+        jnp.concatenate(
+            [state_init, update_weight, state_key_weight, state_value_weight, out_weight], 1
+        ),
+        (
+            (0, NSTATE, 1),
+            (NSTATE, D, 1),
+            (NSTATE + D, 2 * D, 1),
+            (NSTATE + 3 * D, D, 1),
+        ),
+        ahead,
+    )
+    down_folded = down_weight.reshape(folds, rows, D).transpose(1, 0, 2).reshape(rows, ff)
+    (up_full, down_full), _ = take(
+        jnp.concatenate([up_weight, down_folded], 1), ((0, ff, 1), (ff, D, folds)), ahead
+    )
+    table_full = table_vec[:, :VOCAB]
+    columns = jnp.transpose(table_vec[:, VOCAB : VOCAB + 4])
+    gain_attn, gain_mlp, gbias_full, downbias_full = (columns[i] for i in range(4))
+    upbias_full = table_vec[:, VOCAB + 4 : VOCAB + 4 + folds].reshape(-1)
+    query_full, key_full, value_full = (qkv_full[:, i * D : (i + 1) * D] for i in range(3))
+    state_key_complete, svalue_full = skv_full[:, :D], skv_full[:, D:]
     count_of_rows = char_ids.shape[0]
     score_scale = HD ** (-0.5)
     is_first = lax.axis_index("seq") == 0
@@ -206,10 +370,14 @@
     update = matrix_product(state_mix, update_full)
     unit_gain = jnp.ones_like(keep_gate)
     zero_state = jnp.zeros_like(update)
-    prefix_gain, prefix_sum = entering(
-        (keep_gate, (1.0 - keep_gate) * update), "seq", combine, (unit_gain, zero_state), False
-    )
-    state_prev = prefix_gain * jnp.transpose(sinit_full.astype(jnp.float32)) + prefix_sum
+    start = jnp.transpose(f32(sinit_full))
+    if fast:
+        state_prev = earlier_sum(keep_gate, low((1.0 - keep_gate) * update), start)
+    else:
+        prefix_gain, prefix_sum = entering(
+            (keep_gate, (1.0 - keep_gate) * update), "seq", combine, (unit_gain, zero_state), False
+        )
+        state_prev = prefix_gain * start + prefix_sum
     state_reduced_precision = state_prev.astype(jnp.bfloat16)
     recurrent_state_key = matrix_product(state_reduced_precision, state_key_complete).astype(
         jnp.bfloat16
@@ -236,29 +404,13 @@
     )
     attn_mixed = attn_mixed.reshape(count_of_rows, D).astype(jnp.bfloat16)
     hidden = embedded + matrix_product(attn_mixed, out_full)
-    mlp_full = (
-        lax.all_gather(mlp_shards[0], ("dp", "seq"), axis=0, tiled=True),
-        lax.all_gather(mlp_shards[1], ("dp", "seq"), axis=0, tiled=True),
-        lax.all_gather(mlp_shards[2], ("dp", "seq"), axis=0, tiled=True),
-        lax.all_gather(mlp_shards[3], ("dp", "seq"), axis=0, tiled=True),
-        lax.all_gather(mlp_shards[4], ("dp", "seq"), axis=0, tiled=True),
-    )
-    gain_mlp, up_full, upbias_full, down_full, downbias_full = mlp_full
     normed_mlp, norm_mlp_back = jax.vjp(rms_norm, hidden, gain_mlp.astype(jnp.float32))
     normed_mlp_low = normed_mlp.astype(jnp.bfloat16)
     up_pre = matrix_product(normed_mlp_low, up_full) + upbias_full.astype(jnp.float32)
     activation, gelu_back = jax.vjp(jax.nn.gelu, up_pre)
     activation_low = activation.astype(jnp.bfloat16)
     output = hidden + matrix_product(activation_low, down_full) + downbias_full.astype(jnp.float32)
-    mlp_back = (
-        lax.all_gather(mlp_shards[0], ("dp", "seq"), axis=0, tiled=True),
-        lax.all_gather(mlp_shards[1], ("dp", "seq"), axis=0, tiled=True),
-        lax.all_gather(mlp_shards[2], ("dp", "seq"), axis=0, tiled=True),
-        lax.all_gather(mlp_shards[3], ("dp", "seq"), axis=0, tiled=True),
-        lax.all_gather(mlp_shards[4], ("dp", "seq"), axis=0, tiled=True),
-    )
-    up_back = mlp_back[1]
-    down_back = mlp_back[3]
+    up_back, down_back = up_full, down_full
     grad_out = out_grad.astype(jnp.float32)
     grad_down = grad_out.astype(jnp.bfloat16)
     down_bias_grad = jnp.sum(grad_out, 0)
@@ -271,41 +423,10 @@
         matrix_product_transposed_right(grad_up, up_back)
     )
     grad_hidden = grad_out + grad_hidden_norm
-    mlp_grads = (
-        lax.psum_scatter(mlp_gain_grad, ("dp", "seq"), scatter_dimension=0, tiled=True),
-        lax.psum_scatter(up_weight_grad, ("dp", "seq"), scatter_dimension=0, tiled=True),
-        lax.psum_scatter(up_bias_grad, ("dp", "seq"), scatter_dimension=0, tiled=True),
-        lax.psum_scatter(down_weight_grad, ("dp", "seq"), scatter_dimension=0, tiled=True),
-        lax.psum_scatter(down_bias_grad, ("dp", "seq"), scatter_dimension=0, tiled=True),
-    )
-    attn_back = (
-        lax.all_gather(attn_shards[0], ("dp", "seq"), axis=0, tiled=True),
-        lax.all_gather(attn_shards[1], ("dp", "seq"), axis=0, tiled=True),
-        lax.all_gather(attn_shards[2], ("dp", "seq"), axis=0, tiled=True),
-        lax.all_gather(attn_shards[3], ("dp", "seq"), axis=0, tiled=True),
-        lax.all_gather(attn_shards[4], ("dp", "seq"), axis=0, tiled=True),
-        lax.all_gather(attn_shards[5], ("dp", "seq"), axis=0, tiled=True),
-        lax.all_gather(attn_shards[6], ("dp", "seq"), axis=0, tiled=True),
-        lax.all_gather(attn_shards[7], ("dp", "seq"), axis=0, tiled=True),
-        lax.all_gather(attn_shards[8], ("dp", "seq"), axis=0, tiled=True),
-        lax.all_gather(attn_shards[9], ("dp", "seq"), axis=0, tiled=True),
-        lax.all_gather(attn_shards[10], ("dp", "seq"), axis=0, tiled=True),
-        lax.all_gather(attn_shards[11], ("dp", "seq"), axis=0, tiled=True),
-    )
-    (
-        table_back,
-        gain_back,
-        query_back,
-        key_back,
-        value_back,
-        out_back,
-        state_key_backward,
-        state_value_backward,
-        update_back,
-        squery_back,
-        sinit_back,
-        gbias_back,
-    ) = attn_back
+    up_grad, down_grad = add(up_weight_grad), add(down_weight_grad)
+    query_back, key_back, value_back = query_full, key_full, value_full
+    out_back, update_back, squery_back = out_full, update_full, squery_full
+    state_key_backward, state_value_backward = state_key_complete, svalue_full
     grad_branch = grad_hidden.astype(jnp.bfloat16)
     out_weight_grad = matrix_product_transposed_left(attn_mixed, grad_branch)
     grad_mixed = (
@@ -353,9 +474,12 @@
     readout_gradient = matrix_product_transposed_right(
         state_key_gradient, state_key_backward
     ) + matrix_product_transposed_right(state_value_gradient, state_value_backward)
-    later_gain, after_grad = entering(
-        (keep_gate, readout_gradient), "seq", combine, (unit_gain, zero_state), True
-    )
+    if fast:
+        after_grad = later_sum(keep_gate, low(readout_gradient))
+    else:
+        later_gain, after_grad = entering(
+            (keep_gate, readout_gradient), "seq", combine, (unit_gain, zero_state), True
+        )
     gate_term = jnp.sum(after_grad * (state_prev - update), 0)
     gate_bias_grad = gate_term * keep_gate * (1.0 - keep_gate)
     state_init_grad = jnp.transpose(
@@ -408,32 +532,63 @@
         precision=lax.Precision.HIGHEST,
         preferred_element_type=jnp.float32,
     )
-    attn_grads = (
-        lax.psum_scatter(char_table_grad, ("dp", "seq"), scatter_dimension=0, tiled=True),
-        lax.psum_scatter(attn_gain_grad, ("dp", "seq"), scatter_dimension=0, tiled=True),
-        lax.psum_scatter(query_weight_grad, ("dp", "seq"), scatter_dimension=0, tiled=True),
-        lax.psum_scatter(key_weight_grad, ("dp", "seq"), scatter_dimension=0, tiled=True),
-        lax.psum_scatter(value_weight_grad, ("dp", "seq"), scatter_dimension=0, tiled=True),
-        lax.psum_scatter(out_weight_grad, ("dp", "seq"), scatter_dimension=0, tiled=True),
-        lax.psum_scatter(state_key_matrix_gradient, ("dp", "seq"), scatter_dimension=0, tiled=True),
-        lax.psum_scatter(state_value_weight_grad, ("dp", "seq"), scatter_dimension=0, tiled=True),
-        lax.psum_scatter(update_weight_grad, ("dp", "seq"), scatter_dimension=0, tiled=True),
-        lax.psum_scatter(state_query_grad, ("dp", "seq"), scatter_dimension=0, tiled=True),
-        lax.psum_scatter(state_init_grad, ("dp", "seq"), scatter_dimension=0, tiled=True),
-        lax.psum_scatter(gate_bias_grad, ("dp", "seq"), scatter_dimension=0, tiled=True),
-    )
-    position_table_grad = lax.psum(table_grad_local, ("dp", "seq"))
+    rows_of_table = jnp.pad(table_grad_local, ((0, HEADS), (0, 0)))
+    position_table_grad = jnp.sum(lax.all_gather(rows_of_table, AX), 0)[:HEADS]
+    vector_grads = jnp.concatenate(
+        [
+            v.reshape(D, -1)
+            for v in (attn_gain_grad, mlp_gain_grad, gate_bias_grad, down_bias_grad, up_bias_grad)
+        ],
+        1,
+    )
+    vector_grads = jnp.pad(vector_grads, ((0, 0), (0, VEC - vector_grads.shape[1])))
+    out_weight_sum = add(out_weight_grad)
+    state_sum = add(jnp.concatenate([state_key_matrix_gradient, state_value_weight_grad], 1))
+    update_sum = add(
+        jnp.concatenate([update_weight_grad, state_query_grad, state_init_grad], 1)
+    )
+    last = add(
+        jnp.concatenate(
+            [
+                char_table_grad,
+                vector_grads,
+                query_weight_grad,
+                key_weight_grad,
+                value_weight_grad,
+            ],
+            1,
+        )
+    )
+    table_sum, vector_sum = last[:, :VOCAB], last[:, VOCAB : VOCAB + VEC]
+    main = VOCAB + VEC
     return (
-        (output.astype(jnp.bfloat16), embedded_grad)
-        + tuple(attn_grads)
-        + (position_table_grad,)
-        + tuple(mlp_grads)
+        low(output),
+        embedded_grad,
+        table_sum,
+        vector_sum[:, 0],
+        last[:, main : main + D],
+        last[:, main + D : main + 2 * D],
+        last[:, main + 2 * D :],
+        out_weight_sum,
+        state_sum[:, :D],
+        state_sum[:, D:],
+        update_sum[:, :D],
+        update_sum[:, D : D + NSTATE],
+        update_sum[:, D + NSTATE :],
+        vector_sum[:, 2],
+        position_table_grad,
+        vector_sum[:, 1],
+        up_grad,
+        vector_sum[:, 4 : 4 + folds].reshape(-1),
+        down_grad,
+        vector_sum[:, 3],
     )
 
 
 def solution(mesh):
+    fast = dict(mesh.shape) == {"dp": 8, "seq": 4}
     return jax.shard_map(
-        shards,
+        functools.partial(shards, fast),
         mesh=mesh,
         in_specs=(
             P(("dp", "seq")),

time: 2620 us -> 996 us (0.38)
  waiting for transfers between devices: 1840 us -> 237 us
  blocking collectives: 216 us -> 0 us
  starting transfers between devices: 6.48 us -> 104 us
  local copies, waits for them, and re-layouts: 196 us -> 244 us
  other arithmetic: 79.9 us -> 123 us
  Pallas kernels: 0 us -> 31.4 us
    reduce_scatter x11 -> x0, waiting for transfers between devices: 1350 us -> none  [the longest x1 188 us: shards(): lax.psum_scatter(up_weight_grad, ('dp', 'seq'), scatter_dimension=0, tile...]
    all_gather x13 -> x1, waiting for transfers between devices: 345 us -> 1.75 us  [shards(): position_table_grad = jnp.sum(lax.all_gather(rows_of_table, AX), 0)[:HEADS]]
    ppermute x0 -> x78, waiting for transfers between devices: none -> 235 us  [send(): return lax.ppermute(v, AX, pairs)]
    unnamed x26 -> x1, waiting for transfers between devices: 142 us -> 0.02 us
    unnamed x2 -> x0, blocking collectives: 109 us -> none
    all_gather x3 -> x0, blocking collectives: 108 us -> none  [the longest x1 59.9 us: shards(): lax.all_gather(mlp_shards[2], ('dp', 'seq'), axis=0, tiled=True)]
    ppermute x0 -> x78, starting transfers between devices: none -> 99.4 us  [send(): return lax.ppermute(v, AX, pairs)]
    pallas_call x0 -> x6, Pallas kernels: none -> 31.4 us  [the longest x3 23.6 us: assemble(): pl.pallas_call(body, out_shape=[jax.ShapeDtypeStruct((4, 2, 2, 2, rows *...]
  transfers between devices with their start and end apart: 27 -> 81, of which waited for: 19 -> 27; matrix products, arithmetic and copies ran while one was open for 16% -> 42% of each run, Pallas kernels for 0% -> 2%
where the time goes in v1:
time: 996 us; the launch traced here: 991 us
  local copies, waits for them, and re-layouts  244 us (24%)
  waiting for transfers between devices  237 us (24%)
  matrix products  236 us (24%)
  other arithmetic  123 us (12%)
  starting transfers between devices  104 us (10%)
  Pallas kernels  31.4 us (3%)
  between operations  16 us (2%)
    ppermute x78, waiting for transfers between devices, send(): return lax.ppermute(v, AX, pairs)  235 us
    unnamed x254, local copies, waits for them, and re-layouts  112 us
    ppermute x78, starting transfers between devices, send(): return lax.ppermute(v, AX, pairs)  99.4 us
    dot_general x9, matrix products, matrix_product(): return jnp.dot(left_side, right_side, preferred_element_type=jnp.float32)  45.3 us
    dot_general x10, matrix products, matrix_product_transposed_right(): lax.dot_general(left_side, right_side, (((1,), (1,)), ((), ())), preferre...  43.7 us
    dot_general x9, matrix products, matrix_product_transposed_left(): lax.dot_general(left_side, right_side, (((0,), (0,)), ((), ())), preferre...  30.8 us
    convert_element_type x14, other arithmetic, low(): return v.astype(jnp.bfloat16)  25.6 us
    pallas_call x3, Pallas kernels, assemble(): pl.pallas_call(body, out_shape=[jax.ShapeDtypeStruct((4, 2, 2, 2, rows *...  23.6 us
  transfers between devices with their start and end apart: 81, of which 27 were waited for; matrix products, arithmetic and copies ran while one was open for 42% of the time, Pallas kernels for 2%

profile of v1, /device:TPU:0, one launch (start us, length us, event | category | flops | bytes accessed | tf_op | source)
XLA Modules:
  0.0 991.0 jit_solution(12064896037355247917)
XLA Ops:
  26.8 15.0 %collective-permute-done.1.refs_2_ = bf16[32,3968]{1,0:T(8,128)(2,1)S(1)} collective-permute-done((bf16[32,3968]{1,0:T(8,128)(2,1)S(1)}, bf16[32,3968]{1,0:T(8,128)(2,1)S(1)}, u32[]{:S(2)}, u32[]{:S(2)}) %collective-permute-start.1) | collective-permute-done | bytes 253984 | tf_op jit(solution)/shard_map/ppermute | solution.py:52
  54.1 19.0 %collective-permute-done.12.refs_2_ = bf16[32,4608]{1,0:T(8,128)(2,1)S(1)} collective-permute-done((bf16[32,4608]{1,0:T(8,128)(2,1)S(1)}, bf16[32,4608]{1,0:T(8,128)(2,1)S(1)}, u32[]{:S(2)}, u32[]{:S(2)}) %collective-permute-start.12) | collective-permute-done | bytes 294944 | tf_op jit(solution)/shard_map/ppermute | solution.py:52
  90.9 19.8 %collective-permute-done.25.refs_2_ = bf16[32,8192]{1,0:T(8,128)(2,1)S(1)} collective-permute-done((bf16[32,8192]{1,0:T(8,128)(2,1)S(1)}, bf16[32,8192]{1,0:T(8,128)(2,1)S(1)}, u32[]{:S(2)}, u32[]{:S(2)}) %collective-permute-start.25) | collective-permute-done | bytes 524320 | tf_op jit(solution)/shard_map/ppermute | solution.py:52
  111.0 15.1 %collective-permute-done.24.refs_1_ = bf16[32,8192]{1,0:T(8,128)(2,1)S(1)} collective-permute-done((bf16[32,8192]{1,0:T(8,128)(2,1)S(1)}, bf16[32,8192]{1,0:T(8,128)(2,1)S(1)}, u32[]{:S(2)}, u32[]{:S(2)}) %collective-permute-start.24) | collective-permute-done | bytes 524320 | tf_op jit(solution)/shard_map/ppermute | solution.py:52
  144.4 20.0 %collective-permute-done.16.refs_3_ = bf16[4,32,4608]{2,1,0:T(8,128)(2,1)} collective-permute-done((bf16[4,32,4608]{2,1,0:T(8,128)(2,1)}, bf16[4,32,4608]{2,1,0:T(8,128)(2,1)}, u32[]{:S(2)}, u32[]{:S(2)}) %collective-permute-start.16) | collective-permute-done | bytes 1179680 | tf_op jit(solution)/shard_map/ppermute | solution.py:52
  193.1 11.8 %fusion.237 = (f32[8,512]{1,0:T(8,128)S(1)}, f32[8,512,512]{1,2,0:T(8,128)}) fusion(f32[8,512,512]{1,2,0:T(8,128)} %fusion.127), kind=kOutput, calls=%fused_computation.383 | output fusion | flops 8389119 | bytes 16793600 | tf_op jit(solution)/shard_map/sub | solution.py:235
  239.5 25.2 %reshape.872 = f32[4198400]{0:T(1024)} reshape(f32[8,512,1025]{2,1,0:T(8,128)} %broadcast_in_dim.27) | data formatting | bytes 33587200
  264.8 16.6 %reshape.799 = f32[8,524800]{1,0:T(8,128)} reshape(f32[4198400]{0:T(1024)} %reshape.872) | data formatting | bytes 33587200 | tf_op jit(solution)/shard_map/reshape | solution.py:251
  287.1 19.0 %copy.388 = f32[1,8,512,1024]{3,2,1,0:T(8,128)} copy(f32[1,8,512,1024]{3,1,2,0:T(8,128)S(1)} %bitcast.525) | data formatting | bytes 33554432
  355.1 15.8 %fusion.238 = (f32[8,512]{1,0:T(8,128)S(1)}, f32[8,512,1536]{2,1,0:T(8,128)}) fusion(f32[8,512,1024]{2,1,0:T(8,128)} %bitcast.526, bf16[512,8,128]{0,2,1:T(8,128)(2,1)S(1)} %bitcast.546, bf16[1536,8,128]{2,0,1:T(8,128)(2,1)} %bitcast_dynamic-update-slice_fusion, pred[512,1536]{1,0:T(8,128)(4,1)} %concatenate.83), kind=kOutput, calls=%fused_computation.384 | convolution fusion | flops 1635774464 | bytes 46940160 | tf_op jit(solution)/shard_map/ihd,jhd->hij/dot_general | solution.py:281
  370.9 11.7 %exponential_reduce_fusion = f32[8,512]{1,0:T(8,128)S(1)} fusion(f32[8,512,1536]{2,1,0:T(8,128)} %get-tuple-element.117, f32[8,512]{1,0:T(8,128)S(1)} %get-tuple-element.116), kind=kLoop, calls=%fused_computation.4 | loop fusion | flops 12578816 | bytes 25198592 | tf_op jit(solution)/shard_map/reduce_sum | solution.py:397
  382.6 12.2 %fusion.85 = bf16[8,128,512]{2,1,0:T(8,128)(2,1)} fusion(f32[8,512,1536]{2,1,0:T(8,128)} %get-tuple-element.117, f32[8,512]{1,0:T(8,128)S(1)} %log_add_fusion, bf16[512,8,128]{0,2,1:T(8,128)(2,1)} %bitcast.541, bf16[512,8,128]{0,2,1:T(8,128)(2,1)S(1)} %bitcast.536, bf16[512,8,128]{0,2,1:T(8,128)(2,1)} %bitcast.539), kind=kOutput, calls=%fused_computation.169 | convolution fusion | flops 1633157120 | bytes 29376512 | tf_op jit(solution)/shard_map/hij,jhd->ihd/dot_general | solution.py:399
  420.7 13.3 %convolution_convert_fusion = bf16[4096,1024]{1,0:T(8,128)(2,1)} fusion(bf16[512,1024]{1,0:T(8,128)(2,1)S(1)} %copy-done.49, f32[512,4096]{1,0:T(8,128)} %fusion.218, f32[4096]{0:T(1024)S(1)} %reshape.832), kind=kOutput, calls=%fused_computation.28 | convolution fusion | flops 4320133120 | bytes 17842176 | tf_op jit(solution)/shard_map/dot_general | solution.py:219
  434.0 14.1 %fusion.227 = (bf16[4096]{0:T(1024)(128)(2,1)}, bf16[512,4096]{1,0:T(8,128)(2,1)}) fusion(f32[512,4096]{1,0:T(8,128)} %fusion.218, f32[4096]{0:T(1024)S(1)} %reshape.832, bf16[4096,1024]{1,0:T(8,128)(2,1)S(1)} %bitcast.633, bf16[512,1024]{1,0:T(8,128)(2,1)S(1)} %copy-done.49), kind=kOutput, calls=%fused_computation.375 | convolution fusion | flops 4341100544 | bytes 22044672 | tf_op jit(solution)/shard_map/dot_general | solution.py:225
  470.5 12.9 %convolution_bitcast_fusion = f32[1536,8,128]{0,2,1:T(8,128)} fusion(bf16[512,8,128]{0,2,1:T(8,128)(2,1)S(1)} %bitcast.533, f32[8,512,1536]{2,1,0:T(8,128)} %get-tuple-element.117, f32[8,512]{1,0:T(8,128)S(1)} %log_add_fusion), kind=kOutput, calls=%fused_computation.43 | convolution fusion | flops 1623195648 | bytes 32522240 | tf_op jit(solution)/shard_map/hij,ihd->jhd/dot_general | solution.py:439
  483.4 16.0 %multiply_reduce_fusion = (f32[8,512]{1,0:T(8,128)S(1)}, f32[8,512,1536]{2,1,0:T(8,128)}) fusion(f32[8,512,1536]{2,1,0:T(8,128)} %get-tuple-element.117, f32[8,512]{1,0:T(8,128)S(1)} %log_add_fusion, bf16[512,8,128]{0,2,1:T(8,128)(2,1)S(1)} %bitcast.534, bf16[512,8,128]{0,2,1:T(8,128)(2,1)} %bitcast.542, bf16[512,8,128]{0,2,1:T(8,128)(2,1)S(1)} %bitcast.537, ...), kind=kOutput, calls=%fused_computation.2 | convolution fusion | flops 1638920192 | bytes 54558720 | tf_op jit(solution)/shard_map/ihd,jhd->hij/dot_general | solution.py:445
  499.4 22.2 %multiply_convert_fusion = bf16[8,512,1536]{2,1,0:T(8,128)(2,1)} fusion(f32[8,512,1536]{2,1,0:T(8,128)} %get-tuple-element.122, f32[8,512,1536]{2,1,0:T(8,128)} %get-tuple-element.117, f32[8,512]{1,0:T(8,128)S(1)} %get-tuple-element.121, f32[8,512]{1,0:T(8,128)S(1)} %log_add_fusion), kind=kLoop, calls=%fused_computation.1 | loop fusion | flops 25165824 | bytes 62947328 | tf_op jit(solution)/shard_map/convert_element_type | solution.py:449
  549.3 12.4 %add_convert_fusion.2 = bf16[512,1024]{1,0:T(8,128)(2,1)} fusion(f32[512,1024]{1,0:T(8,128)S(1)} %copy-done.61, bf16[4096,1024]{1,0:T(8,128)(2,1)} %bitcast.630, f32[1024]{0:T(1024)S(1)} %bitcast.625, f32[512,4096]{1,0:T(8,128)} %fusion.218, f32[4096]{0:T(1024)S(1)} %reshape.832), kind=kOutput, calls=%fused_computation.114 | convolution fusion | flops 4317511680 | bytes 19943424 | tf_op jit(solution)/shard_map/dot_general | solution.py:215
  589.1 19.5 %reshape.874 = bf16[4198400]{0:T(1024)(128)(2,1)} reshape(bf16[8,524800]{1,0:T(8,128)(2,1)} %concatenate.99) | data formatting | bytes 16793600
  608.7 18.5 %reshape.822 = bf16[8,512,1025]{2,1,0:T(8,128)(2,1)} reshape(bf16[4198400]{0:T(1024)(128)(2,1)} %reshape.874) | data formatting | bytes 16793600 | tf_op jit(solution)/shard_map/reshape | solution.py:264
  827.3 27.7 %collective-permute-done.62 = bf16[4,32,2048]{2,1,0:T(8,128)(2,1)S(1)} collective-permute-done((bf16[4,32,2048]{2,1,0:T(8,128)(2,1)S(1)}, bf16[4,32,2048]{2,1,0:T(8,128)(2,1)S(1)}, u32[]{:S(2)}, u32[]{:S(2)}) %collective-permute-start.62) | collective-permute-done | bytes 524320 | tf_op jit(solution)/shard_map/ppermute | solution.py:52
  875.1 17.8 %collective-permute-done.75 = bf16[4,128,1024]{2,1,0:T(8,128)(2,1)S(1)} collective-permute-done((bf16[4,128,1024]{2,1,0:T(8,128)(2,1)S(1)}, bf16[4,128,1024]{2,1,0:T(8,128)(2,1)S(1)}, u32[]{:S(2)}, u32[]{:S(2)}) %collective-permute-start.75) | collective-permute-done | bytes 1048608 | tf_op jit(solution)/shard_map/ppermute | solution.py:52
  897.5 17.9 %collective-permute-done.68 = bf16[4,32,4096]{2,1,0:T(8,128)(2,1)S(1)} collective-permute-done((bf16[4,32,4096]{2,1,0:T(8,128)(2,1)S(1)}, bf16[4,32,4096]{2,1,0:T(8,128)(2,1)S(1)}, u32[]{:S(2)}, u32[]{:S(2)}) %collective-permute-start.68) | collective-permute-done | bytes 1048608 | tf_op jit(solution)/shard_map/ppermute | solution.py:52
  931.8 15.2 %collective-permute-start.78 = (bf16[128,1024]{1,0:T(8,128)(2,1)S(1)}, bf16[128,1024]{1,0:T(8,128)(2,1)S(1)}, u32[]{:S(2)}, u32[]{:S(2)}) collective-permute-start(bf16[128,1024]{1,0:T(8,128)(2,1)S(1)} %get-tuple-element.76), channel_id=1, source_target_pairs={{0,16},{1,17},{2,18},{3,19},{4,20},{5,21},{6,22},{7,23},{8,24},{9,... | collective-permute-start | bytes 786440 | tf_op jit(solution)/shard_map/ppermute | solution.py:52
  (577 shorter events, 566.2 us)
Async XLA Ops:
  7.2 681.4 %all-gather.3.cloned.1.call-start = ((), (), s32[]{:S(2)}) async-start(), calls=%async_computation | async-start | bytes 1081344 | tf_op jit(solution)/shard_map/all_gather | solution.py:536
  142.6 72.6 %collective-permute-start.17 = (bf16[4,32,4608]{2,1,0:T(8,128)(2,1)S(1)}, bf16[4,32,4608]{2,1,0:T(8,128)(2,1)}, u32[]{:S(2)}, u32[]{:S(2)}) collective-permute-start(bf16[4,32,4608]{2,1,0:T(8,128)(2,1)S(1)} %copy-done.1), channel_id=1, source_target_pairs={{0,1},{1,0},{2,3},{3,2},{4,5},{5,4},{6,7},{7,6},{8,9},{9,8},{10,11... | collective-permute-start | bytes 3538952 | tf_op jit(solution)/shard_map/ppermute | solution.py:52
  142.6 74.1 %collective-permute-start.27 = (bf16[4,32,8192]{2,1,0:T(8,128)(2,1)}, bf16[4,32,8192]{2,1,0:T(8,128)(2,1)}, u32[]{:S(2)}, u32[]{:S(2)}) collective-permute-start(bf16[4,32,8192]{2,1,0:T(8,128)(2,1)} %stack_z.5.refs_0_), channel_id=1, source_target_pairs={{0,2},{1,5},{2,0},{3,7},{4,6},{5,1},{6,4},{7,3},{8,10},{9,13},{10,... | collective-permute-start | bytes 6291464 | tf_op jit(solution)/shard_map/ppermute | solution.py:52
  144.2 76.4 %collective-permute-start.18 = (bf16[4,32,4608]{2,1,0:T(8,128)(2,1)}, bf16[4,32,4608]{2,1,0:T(8,128)(2,1)}, u32[]{:S(2)}, u32[]{:S(2)}) collective-permute-start(bf16[4,32,4608]{2,1,0:T(8,128)(2,1)} %collective-permute-done.14.refs_1_), channel_id=1, source_target_pairs={{0,1},{1,0},{2,3},{3,2},{4,5},{5,4},{6,7},{7,6},{8,9},{9,8},{10,11... | collective-permute-start | bytes 3538952 | tf_op jit(solution)/shard_map/ppermute | solution.py:52
  164.4 56.1 %collective-permute-start.20 = (bf16[4,32,4608]{2,1,0:T(8,128)(2,1)}, bf16[4,32,4608]{2,1,0:T(8,128)(2,1)}, u32[]{:S(2)}, u32[]{:S(2)}) collective-permute-start(bf16[4,32,4608]{2,1,0:T(8,128)(2,1)} %collective-permute-done.16.refs_3_), channel_id=1, source_target_pairs={{0,1},{1,0},{2,3},{3,2},{4,5},{5,4},{6,7},{7,6},{8,9},{9,8},{10,11... | collective-permute-start | bytes 3538952 | tf_op jit(solution)/shard_map/ppermute | solution.py:52
  215.2 112.2 %collective-permute-start.28 = (bf16[4,32,8192]{2,1,0:T(8,128)(2,1)S(1)}, bf16[4,32,8192]{2,1,0:T(8,128)(2,1)}, u32[]{:S(2)}, u32[]{:S(2)}) collective-permute-start(bf16[4,32,8192]{2,1,0:T(8,128)(2,1)S(1)} %copy-done), channel_id=1, source_target_pairs={{0,4},{1,3},{2,6},{3,1},{4,0},{5,7},{6,2},{7,5},{8,12},{9,11},{10,... | collective-permute-start | bytes 6291464 | tf_op jit(solution)/shard_map/ppermute | solution.py:52
  216.8 110.7 %collective-permute-start.29 = (bf16[4,32,8192]{2,1,0:T(8,128)(2,1)}, bf16[4,32,8192]{2,1,0:T(8,128)(2,1)}, u32[]{:S(2)}, u32[]{:S(2)}) collective-permute-start(bf16[4,32,8192]{2,1,0:T(8,128)(2,1)} %collective-permute-done.27.refs_1_), channel_id=1, source_target_pairs={{0,4},{1,3},{2,6},{3,1},{4,0},{5,7},{6,2},{7,5},{8,12},{9,11},{10,... | collective-permute-start | bytes 6291464 | tf_op jit(solution)/shard_map/ppermute | solution.py:52
  217.3 110.6 %collective-permute-start.10 = (bf16[2,512,1024]{2,1,0:T(8,128)(2,1)}, bf16[2,512,1024]{2,1,0:T(8,128)(2,1)}, u32[]{:S(2)}, u32[]{:S(2)}) collective-permute-start(bf16[2,512,1024]{2,1,0:T(8,128)(2,1)} %pad_maximum_fusion.2), channel_id=1, source_target_pairs={{0,1},{1,2},{2,3},{4,5},{5,6},{6,7},{8,9},{9,10},{10,11},{12,13},{... | collective-permute-start | bytes 6291464 | tf_op jit(solution)/shard_map/ppermute | solution.py:187
  229.9 88.9 %collective-permute-start.21 = (bf16[512,1024]{1,0:T(8,128)(2,1)}, bf16[512,1024]{1,0:T(8,128)(2,1)}, u32[]{:S(2)}, u32[]{:S(2)}) collective-permute-start(bf16[512,1024]{1,0:T(8,128)(2,1)} %get-tuple-element.114), channel_id=1, source_target_pairs={{0,1},{1,0},{2,3},{3,2},{4,5},{5,4},{6,7},{7,6},{8,9},{9,8},{10,11... | collective-permute-start | bytes 3145736 | tf_op jit(solution)/shard_map/ppermute | solution.py:52
  307.3 91.4 %collective-permute-start.30 = (bf16[4,32,8192]{2,1,0:T(8,128)(2,1)S(1)}, bf16[4,32,8192]{2,1,0:T(8,128)(2,1)}, u32[]{:S(2)}, u32[]{:S(2)}) collective-permute-start(bf16[4,32,8192]{2,1,0:T(8,128)(2,1)S(1)} %copy-done), channel_id=1, source_target_pairs={{0,1},{1,0},{2,3},{3,2},{4,5},{5,4},{6,7},{7,6},{8,9},{9,8},{10,11... | collective-permute-start | bytes 6291464 | tf_op jit(solution)/shard_map/ppermute | solution.py:52
  327.3 71.4 %collective-permute-start.31 = (bf16[4,32,8192]{2,1,0:T(8,128)(2,1)}, bf16[4,32,8192]{2,1,0:T(8,128)(2,1)}, u32[]{:S(2)}, u32[]{:S(2)}) collective-permute-start(bf16[4,32,8192]{2,1,0:T(8,128)(2,1)} %collective-permute-done.27.refs_1_), channel_id=1, source_target_pairs={{0,1},{1,0},{2,3},{3,2},{4,5},{5,4},{6,7},{7,6},{8,9},{9,8},{10,11... | collective-permute-start | bytes 6291464 | tf_op jit(solution)/shard_map/ppermute | solution.py:52
  327.5 71.3 %collective-permute-start.32 = (bf16[4,32,8192]{2,1,0:T(8,128)(2,1)}, bf16[4,32,8192]{2,1,0:T(8,128)(2,1)}, u32[]{:S(2)}, u32[]{:S(2)}) collective-permute-start(bf16[4,32,8192]{2,1,0:T(8,128)(2,1)} %collective-permute-done.28.refs_2_), channel_id=1, source_target_pairs={{0,1},{1,0},{2,3},{3,2},{4,5},{5,4},{6,7},{7,6},{8,9},{9,8},{10,11... | collective-permute-start | bytes 6291464 | tf_op jit(solution)/shard_map/ppermute | solution.py:52
  327.9 70.9 %collective-permute-start.33 = (bf16[4,32,8192]{2,1,0:T(8,128)(2,1)}, bf16[4,32,8192]{2,1,0:T(8,128)(2,1)}, u32[]{:S(2)}, u32[]{:S(2)}) collective-permute-start(bf16[4,32,8192]{2,1,0:T(8,128)(2,1)} %collective-permute-done.29.refs_3_), channel_id=1, source_target_pairs={{0,1},{1,0},{2,3},{3,2},{4,5},{5,4},{6,7},{7,6},{8,9},{9,8},{10,11... | collective-permute-start | bytes 6291464 | tf_op jit(solution)/shard_map/ppermute | solution.py:52
  562.9 84.4 %collective-permute-start.45 = (bf16[4,2,2,32,1024]{4,3,0,2,1:T(8,128)(2,1)}, bf16[4,2,2,32,1024]{4,3,0,2,1:T(8,128)(2,1)}, u32[]{:S(2)}, u32[]{:S(2)}) collective-permute-start(bf16[4,2,2,32,1024]{4,3,0,2,1:T(8,128)(2,1)} %copy_bitcast_fusion.6), channel_id=1, source_target_pairs={{0,1},{1,0},{2,3},{3,2},{4,5},{5,4},{6,7},{7,6},{8,9},{9,8},{10,11... | collective-permute-start | bytes 3145736 | tf_op jit(solution)/shard_map/ppermute | solution.py:52
  661.0 59.0 %collective-permute-start.52 = (bf16[4,2,2,32,2048]{4,3,0,2,1:T(8,128)(2,1)}, bf16[4,2,2,32,2048]{4,3,0,2,1:T(8,128)(2,1)}, u32[]{:S(2)}, u32[]{:S(2)}) collective-permute-start(bf16[4,2,2,32,2048]{4,3,0,2,1:T(8,128)(2,1)} %copy_bitcast_fusion.5), channel_id=1, source_target_pairs={{0,1},{1,0},{2,3},{3,2},{4,5},{5,4},{6,7},{7,6},{8,9},{9,8},{10,11... | collective-permute-start | bytes 6291464 | tf_op jit(solution)/shard_map/ppermute | solution.py:52
  680.9 126.5 %collective-permute-start.73 = (bf16[4,2,2,128,1024]{4,3,0,2,1:T(8,128)(2,1)}, bf16[4,2,2,128,1024]{4,3,0,2,1:T(8,128)(2,1)}, u32[]{:S(2)}, u32[]{:S(2)}) collective-permute-start(bf16[4,2,2,128,1024]{4,3,0,2,1:T(8,128)(2,1)} %copy_bitcast_fusion.1), channel_id=1, source_target_pairs={{0,1},{1,0},{2,3},{3,2},{4,5},{5,4},{6,7},{7,6},{8,9},{9,8},{10,11... | collective-permute-start | bytes 12582920 | tf_op jit(solution)/shard_map/ppermute | solution.py:52
  680.9 111.0 %collective-permute-start.66 = (bf16[4,2,2,32,4096]{4,3,0,2,1:T(8,128)(2,1)}, bf16[4,2,2,32,4096]{4,3,0,2,1:T(8,128)(2,1)}, u32[]{:S(2)}, u32[]{:S(2)}) collective-permute-start(bf16[4,2,2,32,4096]{4,3,0,2,1:T(8,128)(2,1)} %copy_bitcast_fusion.2), channel_id=1, source_target_pairs={{0,1},{1,0},{2,3},{3,2},{4,5},{5,4},{6,7},{7,6},{8,9},{9,8},{10,11... | collective-permute-start | bytes 12582920 | tf_op jit(solution)/shard_map/ppermute | solution.py:52
  683.9 59.3 %collective-permute-start.37 = (bf16[2,512,1024]{2,1,0:T(8,128)(2,1)}, bf16[2,512,1024]{2,1,0:T(8,128)(2,1)}, u32[]{:S(2)}, u32[]{:S(2)}) collective-permute-start(bf16[2,512,1024]{2,1,0:T(8,128)(2,1)} %pad_maximum_fusion.3), channel_id=1, source_target_pairs={{1,0},{2,1},{3,2},{5,4},{6,5},{7,6},{9,8},{10,9},{11,10},{13,12},{... | collective-permute-start | bytes 6291464 | tf_op jit(solution)/shard_map/ppermute | solution.py:187
  722.8 53.8 %collective-permute-start.53 = (bf16[4,32,2048]{2,1,0:T(8,128)(2,1)}, bf16[4,32,2048]{2,1,0:T(8,128)(2,1)}, u32[]{:S(2)}, u32[]{:S(2)}) collective-permute-start(bf16[4,32,2048]{2,1,0:T(8,128)(2,1)} %get-tuple-element.64), channel_id=1, source_target_pairs={{0,4},{1,3},{2,6},{3,1},{4,0},{5,7},{6,2},{7,5},{8,12},{9,11},{10,... | collective-permute-start | bytes 1572872 | tf_op jit(solution)/shard_map/ppermute | solution.py:52
  724.4 57.0 %collective-permute-start.55 = (bf16[4,32,2048]{2,1,0:T(8,128)(2,1)}, bf16[4,32,2048]{2,1,0:T(8,128)(2,1)}, u32[]{:S(2)}, u32[]{:S(2)}) collective-permute-start(bf16[4,32,2048]{2,1,0:T(8,128)(2,1)} %get-tuple-element.65), channel_id=1, source_target_pairs={{0,4},{1,3},{2,6},{3,1},{4,0},{5,7},{6,2},{7,5},{8,12},{9,11},{10,... | collective-permute-start | bytes 1572872 | tf_op jit(solution)/shard_map/ppermute | solution.py:52
  781.5 91.1 %collective-permute-start.38 = (bf16[4,2,2,32,3456]{4,3,0,2,1:T(8,128)(2,1)S(1)}, bf16[4,2,2,32,3456]{4,3,0,2,1:T(8,128)(2,1)S(1)}, u32[]{:S(2)}, u32[]{:S(2)}) collective-permute-start(bf16[4,2,2,32,3456]{4,3,0,2,1:T(8,128)(2,1)S(1)} %copy_bitcast_fusion.3), channel_id=1, source_target_pairs={{0,1},{1,0},{2,3},{3,2},{4,5},{5,4},{6,7},{7,6},{8,9},{9,8},{10,11... | collective-permute-start | bytes 10616840 | tf_op jit(solution)/shard_map/ppermute | solution.py:52
  812.5 61.8 %collective-permute-start.76 = (bf16[4,128,1024]{2,1,0:T(8,128)(2,1)S(1)}, bf16[4,128,1024]{2,1,0:T(8,128)(2,1)S(1)}, u32[]{:S(2)}, u32[]{:S(2)}) collective-permute-start(bf16[4,128,1024]{2,1,0:T(8,128)(2,1)S(1)} %get-tuple-element.57), channel_id=1, source_target_pairs={{0,4},{1,3},{2,6},{3,1},{4,0},{5,7},{6,2},{7,5},{8,12},{9,11},{10,... | collective-permute-start | bytes 3145736 | tf_op jit(solution)/shard_map/ppermute | solution.py:52
  874.3 74.8 %collective-permute-start.41 = (bf16[4,32,3456]{2,1,0:T(8,128)(2,1)S(1)}, bf16[4,32,3456]{2,1,0:T(8,128)(2,1)S(1)}, u32[]{:S(2)}, u32[]{:S(2)}) collective-permute-start(bf16[4,32,3456]{2,1,0:T(8,128)(2,1)S(1)} %get-tuple-element.61), channel_id=1, source_target_pairs={{0,4},{1,3},{2,6},{3,1},{4,0},{5,7},{6,2},{7,5},{8,12},{9,11},{10,... | collective-permute-start | bytes 2654216 | tf_op jit(solution)/shard_map/ppermute | solution.py:52
  895.1 75.0 %collective-permute-start.77 = (bf16[128,1024]{1,0:T(8,128)(2,1)S(1)}, bf16[128,1024]{1,0:T(8,128)(2,1)S(1)}, u32[]{:S(2)}, u32[]{:S(2)}) collective-permute-start(bf16[128,1024]{1,0:T(8,128)(2,1)S(1)} %get-tuple-element.74), channel_id=1, source_target_pairs={{0,8},{1,9},{2,10},{3,11},{4,12},{5,13},{6,14},{7,15},{8,16},{9,17... | collective-permute-start | bytes 786440 | tf_op jit(solution)/shard_map/ppermute | solution.py:52
  (174 other events, 2710.1 us)
Sparse Core Ops, SparseCore 0:
  632.9 55.6 all-gather.2

commit v2 on v1

v2 whole, which is shorter than its diff:
```python
import functools

import jax
import jax.numpy as jnp
from jax import lax
from jax.experimental import pallas as pl
from jax.experimental.pallas import tpu as pltpu
from jax.sharding import PartitionSpec as P

D = 1024
HEADS = 8
HD = 128
NSTATE = 512
VOCAB = 256
BLK = 512
AX = ("dp", "seq")
VEC = 128


def f32(v):
    return v.astype(jnp.float32)


def low(v):
    return v.astype(jnp.bfloat16)


def route(move):
    pairs = []
    for z in range(4):
        for y in range(2):
            for x in range(2):
                for c in range(2):
                    tz, ty, tx, tc = move(z, y, x, c)
                    pairs.append((z * 8 + y * 4 + x * 2 + c, tz * 8 + ty * 4 + tx * 2 + tc))
    return pairs


A_ROUTE = route(lambda z, y, x, c: (z, y, 1 - x, c) if c == 0 else (z, 1 - y, x, c))
B_ROUTE = route(lambda z, y, x, c: (z, 1 - y, x, c) if c == 0 else (z, y, 1 - x, c))
CORE_ROUTE = route(lambda z, y, x, c: (z, y, x, 1 - c))
X_ROUTE = route(lambda z, y, x, c: (z, y, 1 - x, c))
Z_ROUTE = {k: route(lambda z, y, x, c, k=k: ((z + k) % 4, y, x, c)) for k in (1, 2, 3)}


def place():
    d, s = lax.axis_index("dp"), lax.axis_index("seq")
    return d // 2, d % 2, s // 2, s % 2


def send(v, pairs):
    return lax.ppermute(v, AX, pairs)


def stack_z(shard, *others):
    def body(*refs):
        z = lax.axis_index("dp") // 2
        for i, src in enumerate(refs[:4]):
            refs[4][lax.rem(z + 4 - i, 4)] = src[...]

    return pl.pallas_call(
        body, out_shape=jax.ShapeDtypeStruct((4,) + shard.shape, shard.dtype), name="stack_z"
    )(shard, *others)


def assemble(pieces, layout):
    rows, width = pieces[0].shape[1:]

    def body(*refs):
        ins, outs = refs[:8], refs[8:]
        y = lax.rem(lax.axis_index("dp"), 2)
        s = lax.axis_index("seq")
        x, c = s // 2, lax.rem(s, 2)
        for i, src in enumerate(ins):
            core = c if i < 4 else 1 - c
            flip_x = (0, 1 - core, core, 1)[i % 4]
            flip_y = (0, core, 1 - core, 1)[i % 4]
            tx, ty = lax.rem(x + flip_x, 2), lax.rem(y + flip_y, 2)
            for (first, w, folds), out in zip(layout, outs):
                for q in range(folds):
                    out[0, ty, tx, core, q * rows : (q + 1) * rows, :] = src[
                        0, :, first + q * w : first + (q + 1) * w
                    ]

    full = pl.pallas_call(
        body,
        out_shape=[
            jax.ShapeDtypeStruct((4, 2, 2, 2, rows * n, w), pieces[0].dtype) for _, w, n in layout
        ],
        grid=(4,),
        in_specs=[pl.BlockSpec((1, rows, width), lambda z: (z, 0, 0))] * 8,
        out_specs=[
            pl.BlockSpec((1, 2, 2, 2, rows * n, w), lambda z: (z, 0, 0, 0, 0, 0))
            for _, w, n in layout
        ],
        compiler_params=pltpu.CompilerParams(vmem_limit_bytes=40 * 2**20),
        name="assemble",
    )(*pieces)
    return [o.reshape(32 * rows * n, w) for o, (_, w, n) in zip(full, layout)]


def tie(value, *others):
    return lax.optimization_barrier((value, others))[0]


def join(*values):
    return lax.optimization_barrier(values)


def along_z(shard):
    return [send(shard, Z_ROUTE[k]) for k in (1, 2, 3)]


def to_sides(p):
    return send(p, A_ROUTE), send(p, B_ROUTE)


def to_corner(p, sides):
    return send(sides[0], B_ROUTE), [send(v, CORE_ROUTE) for v in (p,) + tuple(sides)]


def full(p, sides, corner, layout):
    last = send(corner[0], CORE_ROUTE)
    return assemble((p,) + tuple(sides) + (corner[0],) + tuple(corner[1]) + (last,), layout)


def to_core(away):
    return send(away, CORE_ROUTE)


def chip_part(keep, got, ty, tx):
    rows, width = keep.shape[0] // 16, keep.shape[1]
    at = [
        lax.dynamic_slice(
            a.reshape(2, 2, 4, rows, width), (ty, tx, 0, 0, 0), (1, 1, 4, rows, width)
        )
        for a in (keep, got)
    ]
    return (f32(at[0]) + f32(at[1])).reshape(4, rows, width)


def from_corner(keep, got):
    z, y, x, c = place()
    bx, by = jnp.where(c == 0, x, 1 - x), jnp.where(c == 0, 1 - y, y)
    corner, side = chip_part(keep, got, 1 - y, 1 - x), chip_part(keep, got, by, bx)
    return send(low(corner), B_ROUTE), send(low(side), B_ROUTE)


def from_side(keep, got, across):
    z, y, x, c = place()
    ax, ay = jnp.where(c == 0, 1 - x, x), jnp.where(c == 0, y, 1 - y)
    return send(low(chip_part(keep, got, ay, ax) + f32(across)), A_ROUTE)


def from_ends(keep, got, side_a, side_b):
    z, y, x, c = place()
    own = chip_part(keep, got, y, x) + f32(side_a) + f32(side_b)
    rest = [low(lax.dynamic_index_in_dim(own, (z + k) % 4, 0, False)) for k in (1, 2, 3)]
    mine = lax.dynamic_index_in_dim(own, z, 0, False)
    return [mine] + [send(v, Z_ROUTE[k]) for v, k in zip(rest, (1, 2, 3))]


def finish(parts):
    return parts[0] + f32(parts[1]) + f32(parts[2]) + f32(parts[3])


def gather_any(shard, layout):
    rows = shard.shape[0]
    full = lax.all_gather(shard, AX, axis=0, tiled=True)
    outs = []
    for first, w, folds in layout:
        part = full[:, first : first + w * folds]
        if folds > 1:
            part = part.reshape(-1, rows, folds, w).transpose(0, 2, 1, 3).reshape(-1, w)
        outs.append(part)
    return outs


def scatter_any(grad):
    return lax.psum_scatter(f32(grad), AX, scatter_dimension=0, tiled=True)


def earlier_sum(keep_gate, mine, start):
    z, y, x, c = place()
    sibling = send(mine, CORE_ROUTE)
    first = jnp.where(c == 0, f32(mine), f32(sibling))
    second = jnp.where(c == 0, f32(sibling), f32(mine))
    chip = low(keep_gate * first + second)
    half = NSTATE // 2
    near = send(lax.dynamic_slice(chip, (c * half, 0), (half, D)), X_ROUTE)
    far = send(near, CORE_ROUTE)
    other = jnp.concatenate([jnp.where(c == 0, near, far), jnp.where(c == 0, far, near)], 0)
    before = jnp.where(x == 0, start, keep_gate * keep_gate * start + f32(other))
    return jnp.where(c == 0, before, keep_gate * before + f32(sibling))


def later_sum(keep_gate, mine):
    z, y, x, c = place()
    sibling = send(mine, CORE_ROUTE)
    first = jnp.where(c == 0, f32(mine), f32(sibling))
    second = jnp.where(c == 0, f32(sibling), f32(mine))
    chip = low(first + keep_gate * second)
    half = NSTATE // 2
    near = send(lax.dynamic_slice(chip, (c * half, 0), (half, D)), X_ROUTE)
    far = send(near, CORE_ROUTE)
    other = jnp.concatenate([jnp.where(c == 0, near, far), jnp.where(c == 0, far, near)], 0)
    after = jnp.where(x == 0, f32(other), 0.0)
    return jnp.where(c == 0, f32(sibling) + keep_gate * after, after)


def from_behind(block, axis, distance):
    devices = range(lax.axis_size(axis))
    pairs = [(i - distance, i) for i in devices if i - distance in devices]
    return lax.ppermute(block, axis, pairs)


def entering(keep_gate, mine, reverse):
    devices, at_home = lax.axis_size("seq"), lax.axis_index("seq")
    everything = lax.all_gather(mine, "seq")

    def turn(k, before):
        at = devices - 1 - k if reverse else k
        reached = at > at_home if reverse else at < at_home
        gain, total = before
        return (
            jnp.where(reached, gain * keep_gate, gain),
            jnp.where(reached, keep_gate * total + f32(everything[at]), total),
        )

    start = (jnp.ones_like(keep_gate), jnp.zeros(mine.shape, jnp.float32))
    return lax.fori_loop(0, devices, turn, start)


def norm_scale(values):
    return lax.rsqrt(jnp.mean(values * values, -1, keepdims=True) + 1e-06)


def halves_of_columns(a):
    parts = a.reshape(a.shape[0], CHUNKS, 2, -1)
    return [parts[:, :, i].reshape(a.shape[0], -1) for i in range(2)]


def halves_of_rows(a, chunks):
    parts = a.reshape(chunks, 2, -1, a.shape[1])
    return [parts[:, i].reshape(-1, a.shape[1]) for i in range(2)]


def fold(a, rows):
    return a.reshape(-1, rows, D).transpose(1, 0, 2).reshape(rows, -1)


def unfold(a):
    rows = a.shape[0]
    return a.reshape(rows, -1, D).transpose(1, 0, 2).reshape(-1, D)


SCALE = HD ** (-0.5)


def dot(a, b, dims):
    return lax.dot_general(a, b, (dims, ((), ())), preferred_element_type=jnp.float32)


NN, NT, TN = ((1,), (0,)), ((1,), (1,)), ((0,), (0,))


def head_block(first):
    return pl.BlockSpec((BLK, HD), lambda h: (0, first + h))


def pair_block():
    return pl.BlockSpec((2, BLK, HD), lambda h: (0, 0, h))


def row_block():
    return pl.BlockSpec((1, 1, BLK), lambda h: (h, 0, 0))


def token_scores(q, k, kp, bias_row, is_first):
    row = lax.broadcasted_iota(jnp.int32, (BLK, BLK), 0)
    col = lax.broadcasted_iota(jnp.int32, (BLK, BLK), 1)
    own = row <= col
    bias = jnp.concatenate([bias_row] + [pltpu.roll(bias_row, i, 1) for i in range(1, 8)], 0)
    while bias.shape[0] < BLK:
        bias = jnp.concatenate([bias, pltpu.roll(bias, bias.shape[0], 1)], 0)
    raw = jnp.where(own, dot(k, q, NT), dot(kp, q, NT))
    scores = raw * SCALE + bias
    return jnp.where(own | jnp.logical_not(is_first), scores, -1e30), own


def attention_body(q, k, v, kp, vp, sk, sv, bias, mixed, lse):
    is_first = lax.axis_index("seq") == 0
    q = q[...]
    tokens, own = token_scores(q, k[...], kp[...], bias[0], is_first)
    states = dot(sk[...], q, NT) * SCALE
    top = jnp.maximum(jnp.max(tokens, 0, keepdims=True), jnp.max(states, 0, keepdims=True))
    tokens, states = jnp.exp(tokens - top), jnp.exp(states - top)
    total = jnp.sum(tokens, 0, keepdims=True) + jnp.sum(states, 0, keepdims=True)
    lse[0] = top + jnp.log(total)
    mix = dot(jnp.transpose(v[...]), low(jnp.where(own, tokens, 0.0)), NN)
    mix += dot(jnp.transpose(vp[...]), low(jnp.where(own, 0.0, tokens)), NN)
    mix += dot(jnp.transpose(sv[...]), low(states), NN)
    mixed[...] = low(jnp.transpose(mix * (1.0 / total)))


def attention(qkv, prev, skv, bias):
    return pl.pallas_call(
        attention_body,
        grid=(HEADS,),
        in_specs=[head_block(0), head_block(HEADS), head_block(2 * HEADS)]
        + [head_block(0), head_block(HEADS)] * 2
        + [row_block()],
        out_specs=[head_block(0), row_block()],
        out_shape=[
            jax.ShapeDtypeStruct((BLK, D), jnp.bfloat16),
            jax.ShapeDtypeStruct((HEADS, 1, BLK), jnp.float32),
        ],
        compiler_params=pltpu.CompilerParams(vmem_limit_bytes=40 * 2**20),
        cost_estimate=pl.CostEstimate(
            flops=12 * HEADS * BLK * BLK * HD,
            bytes_accessed=9 * 2**20,
            transcendentals=2 * HEADS * BLK * BLK,
        ),
        name="attention",
    )(qkv, qkv, qkv, prev, prev, skv, skv, bias)


def attention_back_body(
    q, k, v, kp, vp, sk, sv, bias, lse, go, gq, gkv, gprev, gstate, gbias
):
    is_first = lax.axis_index("seq") == 0
    q, k, kp, sk, go = q[...], k[...], kp[...], sk[...], go[...]
    tokens, own = token_scores(q, k, kp, bias[0], is_first)
    log_total = lse[0]
    tokens = jnp.exp(tokens - log_total)
    states = jnp.exp(dot(sk, q, NT) * SCALE - log_total)
    gtokens = jnp.where(own, dot(v[...], go, NT), dot(vp[...], go, NT))
    gstates = dot(sv[...], go, NT)
    mean = jnp.sum(tokens * gtokens, 0, keepdims=True) + jnp.sum(states * gstates, 0, keepdims=True)
    gkv[1] = dot(low(jnp.where(own, tokens, 0.0)), go, NN)
    gprev[1] = low(dot(low(jnp.where(own, 0.0, tokens)), go, NN))
    gstate[1] = low(dot(low(states), go, NN))
    gtokens = low(tokens * (gtokens - mean))
    gstates = low(states * (gstates - mean))
    wide = f32(gtokens)
    gown, gbefore = low(jnp.where(own, wide, 0.0)), low(jnp.where(own, 0.0, wide))
    gkv[0] = dot(gown, q, NN) * SCALE
    gprev[0] = low(dot(gbefore, q, NN) * SCALE)
    gstate[0] = low(dot(gstates, q, NN) * SCALE)
    g = dot(jnp.transpose(k), gown, NN)
    g += dot(jnp.transpose(kp), gbefore, NN)
    g += dot(jnp.transpose(sk), gstates, NN)
    gq[...] = low(jnp.transpose(g * SCALE))
    rows = BLK
    while rows > 1:
        rows //= 2
        wide = wide[:rows] + pltpu.roll(wide[rows:], BLK - rows, 1)
    gbias[0] = wide


def attention_back(qkv, prev, skv, bias, lse, go):
    return pl.pallas_call(
        attention_back_body,
        grid=(HEADS,),
        in_specs=[head_block(0), head_block(HEADS), head_block(2 * HEADS)]
        + [head_block(0), head_block(HEADS)] * 2
        + [row_block(), row_block(), head_block(0)],
        out_specs=[head_block(0), pair_block(), pair_block(), pair_block(), row_block()],
        out_shape=[
            jax.ShapeDtypeStruct((BLK, D), jnp.bfloat16),
            jax.ShapeDtypeStruct((2, BLK, D), jnp.float32),
            jax.ShapeDtypeStruct((2, BLK, D), jnp.bfloat16),
            jax.ShapeDtypeStruct((2, BLK, D), jnp.bfloat16),
            jax.ShapeDtypeStruct((HEADS, 1, BLK), jnp.float32),
        ],
        compiler_params=pltpu.CompilerParams(vmem_limit_bytes=48 * 2**20),
        cost_estimate=pl.CostEstimate(
            flops=30 * HEADS * BLK * BLK * HD,
            bytes_accessed=18 * 2**20,
            transcendentals=2 * HEADS * BLK * BLK,
        ),
        name="attention_back",
    )(qkv, qkv, qkv, prev, prev, skv, skv, bias, lse, go)


def query_block():
    return pl.BlockSpec((HD, NSTATE), lambda h: (h, 0))


def state_body(k, v, query, mixed, lse):
    scores = dot(k[...], query[...], NN) * SCALE
    top = jnp.max(scores, 0, keepdims=True)
    scores = jnp.exp(scores - top)
    total = jnp.sum(scores, 0, keepdims=True)
    lse[0] = top + jnp.log(total)
    mix = dot(jnp.transpose(v[...]), low(scores), NN)
    mixed[...] = low(jnp.transpose(mix * (1.0 / total)))


def state_attention(qkv, query):
    return pl.pallas_call(
        state_body,
        grid=(HEADS,),
        in_specs=[head_block(HEADS), head_block(2 * HEADS), query_block()],
        out_specs=[head_block(0), row_block()],
        out_shape=[
            jax.ShapeDtypeStruct((NSTATE, D), jnp.bfloat16),
            jax.ShapeDtypeStruct((HEADS, 1, NSTATE), jnp.float32),
        ],
        compiler_params=pltpu.CompilerParams(vmem_limit_bytes=32 * 2**20),
        cost_estimate=pl.CostEstimate(
            flops=4 * HEADS * BLK * BLK * HD,
            bytes_accessed=4 * 2**20,
            transcendentals=HEADS * BLK * BLK,
        ),
        name="state_attention",
    )(qkv, qkv, query)


def state_back_body(k, v, query, lse, go, gkv, gsum, gquery):
    k, query, go = k[...], query[...], go[...]
    probs = jnp.exp(dot(k, query, NN) * SCALE - lse[0])
    gprobs = dot(v[...], go, NT)
    mean = jnp.sum(probs * gprobs, 0, keepdims=True)
    gsum[1] = dot(low(probs), go, NN) + gkv[1]
    gscores = low(probs * (gprobs - mean))
    gsum[0] = dot(gscores, query, NT) * SCALE + gkv[0]
    gquery[...] = low(dot(jnp.transpose(k), gscores, NN) * SCALE)


def state_attention_back(qkv, query, lse, go, gkv):
    return pl.pallas_call(
        state_back_body,
        grid=(HEADS,),
        in_specs=[
            head_block(HEADS),
            head_block(2 * HEADS),
            query_block(),
            row_block(),
            head_block(0),
            pair_block(),
        ],
        out_specs=[pair_block(), query_block()],
        out_shape=[
            jax.ShapeDtypeStruct((2, BLK, D), jnp.float32),
            jax.ShapeDtypeStruct((D, NSTATE), jnp.bfloat16),
        ],
        compiler_params=pltpu.CompilerParams(vmem_limit_bytes=32 * 2**20),
        cost_estimate=pl.CostEstimate(
            flops=10 * HEADS * BLK * BLK * HD,
            bytes_accessed=14 * 2**20,
            transcendentals=HEADS * BLK * BLK,
        ),
        name="state_attention_back",
    )(qkv, qkv, query, lse, go, gkv)


STEP = 512
HALF = 2048
CHUNKS = 32


def owner_row(chip):
    return chip % 4 * 4 + chip // 4


def gelu_parts(x):
    a, b = 0.7978845608028654, 0.044715
    square = x * x
    t = jnp.tanh(a * x * (1.0 + b * square))
    half = 0.5 * (1.0 + t)
    slope = half + (0.5 * a) * x * (1.0 - t * t) * (1.0 + 3.0 * b * square)
    return x * half, slope


def mlp_body(last, core_of, *refs):
    hidden, og, rows, up_bias, up, down = refs[:6]
    if last:
        out_in, u_in, keep, away, up_bias_grad, output, grad, branch, sums = refs[6:15]
        xn, xs, out_acc, u_acc = refs[15:]
    else:
        keep, away, up_bias_grad, out_acc, u_acc = refs[6:11]
        xn, xs = refs[11:]
    j = pl.program_id(0)
    core = core_of()
    rk = D // CHUNKS
    hk = HALF // CHUNKS

    @pl.when(j == 0)
    def _():
        h = hidden[...]
        r = lax.rsqrt(jnp.mean(h * h, -1, keepdims=True) + 1e-06)
        n = low(h * r * rows[0:1, :])
        xn[...] = n
        nt = jnp.transpose(n)
        for i in range(CHUNKS):
            to = owner_row(i // 2) * rk + lax.rem(i % 2 + core, 2) * (D // 2)
            xs[pl.ds(pl.multiple_of(to, rk), rk), :] = nt[i * rk : (i + 1) * rk]
        if last:
            out_acc[...] = out_in[...]
            u_acc[...] = u_in[...]
        else:
            out_acc[...] = jnp.zeros_like(out_acc)
            u_acc[...] = jnp.zeros_like(u_acc)

    up_w, down_w, g_out = up[...], down[...], og[...]
    act, slope = gelu_parts(dot(xn[...], up_w, NN) + up_bias[...])
    act = low(act)
    out_acc[...] += dot(act, down_w, NN)
    g_up = low(slope * dot(g_out, down_w, NT))
    up_bias_grad[...] = jnp.sum(f32(g_up), 0, keepdims=True)
    u_acc[...] += dot(g_up, up_w, NT)
    d_up = low(dot(xs[...], g_up, NN))
    at = pl.ds(pl.multiple_of(j * STEP, STEP), STEP)
    keep[:, at] = d_up[: D // 2]
    away[:, at] = d_up[D // 2 :]
    d_down = low(dot(jnp.transpose(act), g_out, NN))
    for i in range(STEP // hk // 2):
        even = d_down[2 * i * hk : (2 * i + 1) * hk]
        odd = d_down[(2 * i + 1) * hk : (2 * i + 2) * hk]
        mine, other = jnp.where(core == 0, even, odd), jnp.where(core == 0, odd, even)
        to = pl.ds(pl.multiple_of((i * (STEP // hk // 2) + j) * rk, rk), rk)
        for q in range(hk // rk):
            cols = slice(HALF + q * D, HALF + (q + 1) * D)
            keep[to, cols] = mine[q * rk : (q + 1) * rk]
            away[to, cols] = other[q * rk : (q + 1) * rk]

    if last:

        @pl.when(j == pl.num_programs(0) - 1)
        def _():
            h = hidden[...]
            output[...] = low(h + out_acc[...] + rows[1:2, :])
            r = lax.rsqrt(jnp.mean(h * h, -1, keepdims=True) + 1e-06)
            n = h * r
            u = u_acc[...]
            ug = u * rows[0:1, :]
            g = f32(og[...]) + r * (ug - n * jnp.mean(ug * n, -1, keepdims=True))
            grad[...] = g
            branch[...] = low(g)
            sums[0:1, :] = jnp.sum(u * n, 0, keepdims=True)
            sums[1:2, :] = jnp.sum(f32(og[...]), 0, keepdims=True)


def mlp_half(core_of, hidden, og, rows, up_bias, up, down, before):
    last = before is not None
    whole = lambda a, b: pl.BlockSpec((a, b), lambda j: (0, 0))
    tall = lambda a, b: pl.BlockSpec((a, b), lambda j: (0, 0), pipeline_mode=pl.Buffered(1))
    acc = jax.ShapeDtypeStruct((BLK, D), jnp.float32)
    lows = jax.ShapeDtypeStruct((BLK, D), jnp.bfloat16)
    grads = jax.ShapeDtypeStruct((D // 2, 2 * HALF), jnp.bfloat16)
    return pl.pallas_call(
        functools.partial(mlp_body, last, core_of),
        grid=(HALF // STEP,),
        in_specs=[
            tall(BLK, D),
            tall(BLK, D),
            whole(8, D),
            pl.BlockSpec((1, STEP), lambda j: (0, j)),
            pl.BlockSpec((D, STEP), lambda j: (0, j)),
            pl.BlockSpec((STEP, D), lambda j: (j, 0)),
        ]
        + [tall(BLK, D)] * (2 if last else 0),
        out_specs=[tall(D // 2, 2 * HALF)] * 2
        + [pl.BlockSpec((1, STEP), lambda j: (0, j))]
        + ([tall(BLK, D)] * 3 + [whole(8, D)] if last else [tall(BLK, D)] * 2),
        out_shape=[grads, grads, jax.ShapeDtypeStruct((1, HALF), jnp.float32)]
        + (
            [lows, acc, lows, jax.ShapeDtypeStruct((8, D), jnp.float32)]
            if last
            else [acc, acc]
        ),
        scratch_shapes=[pltpu.VMEM((BLK, D), jnp.bfloat16), pltpu.VMEM((D, BLK), jnp.bfloat16)]
        + ([pltpu.VMEM((BLK, D), jnp.float32)] * 2 if last else []),
        compiler_params=pltpu.CompilerParams(vmem_limit_bytes=58 * 2**20),
        cost_estimate=pl.CostEstimate(
            flops=12 * BLK * D * HALF, bytes_accessed=30 * 2**20, transcendentals=BLK * HALF
        ),
        name="mlp_half",
    )(hidden, og, rows, up_bias, up, down, *(before or ()))


def weight_grads_body(core_of, plan, columns, *refs):
    keep, away, split = refs[-3:]
    core = core_of()
    rk = D // CHUNKS

    def put(pairs, first):
        for chip, (even, odd) in enumerate(pairs):
            to = owner_row(chip) * rk
            at = slice(to, to + rk), slice(first, first + even.shape[1])
            keep[at] = jnp.where(core == 0, even, odd)
            away[at] = jnp.where(core == 0, odd, even)

    for (kind, ins), first in zip(plan, columns):
        if kind == "dot":
            nt = jnp.transpose(refs[ins[0]][...])
            for i in range(CHUNKS):
                to = owner_row(i // 2) * rk + lax.rem(i % 2 + core, 2) * (D // 2)
                split[pl.ds(pl.multiple_of(to, rk), rk), :] = nt[i * rk : (i + 1) * rk]
            for i in ins[1:]:
                width = refs[i].shape[-1]
                for s in range(0, width, 512):
                    n = min(512, width - s)
                    g = low(dot(split[...], refs[i][:, s : s + n], NN))
                    keep[:, first + s : first + s + n] = g[: D // 2]
                    away[:, first + s : first + s + n] = g[D // 2 :]
                first += width
        else:
            a = refs[ins[0]][...]
            if kind == "transposed":
                a = low(jnp.transpose(a))
            put(
                [
                    (a[i * rk : (i + 1) * rk], a[(i + 1) * rk : (i + 2) * rk])
                    for i in range(0, CHUNKS, 2)
                ],
                first,
            )


def weight_grads(core_of, plan):
    args, steps, columns, width, flops = [], [], [], 0, 0
    for kind, *arrays in plan:
        steps.append((kind, tuple(range(len(args), len(args) + len(arrays)))))
        args += arrays
        columns.append(width)
        if kind == "dot":
            n = sum(a.shape[1] for a in arrays[1:])
            flops += 2 * BLK * D * n
        else:
            n = arrays[0].shape[1 if kind == "rows" else 0]
        width += n
    return pl.pallas_call(
        functools.partial(weight_grads_body, core_of, steps, columns),
        out_shape=[jax.ShapeDtypeStruct((D // 2, width), jnp.bfloat16)] * 2,
        scratch_shapes=[pltpu.VMEM((D, BLK), jnp.bfloat16)],
        compiler_params=pltpu.CompilerParams(vmem_limit_bytes=48 * 2**20),
        cost_estimate=pl.CostEstimate(
            flops=flops, bytes_accessed=4 * D * width, transcendentals=0
        ),
        name="weight_grads",
    )(*args)


def natural(keep, away):
    parts = [a.reshape(4, 4, -1, a.shape[1]).transpose(1, 0, 2, 3) for a in (keep, away)]
    return jnp.stack(parts, 2).reshape(-1, keep.shape[1])


def layer(
    fast,
    char_ids,
    char_table,
    attn_gain,
    query_weight,
    key_weight,
    value_weight,
    out_weight,
    state_key_weight,
    state_value_weight,
    update_weight,
    state_query,
    state_init,
    gate_bias,
    position_table,
    mlp_gain,
    up_weight,
    up_bias,
    down_weight,
    down_bias,
    out_grad,
):
    rows = attn_gain.shape[0]
    ff = up_weight.shape[1]
    folds = ff // D
    core_of = (lambda: lax.rem(lax.axis_index("seq"), 2)) if fast else (lambda: jnp.int32(0))
    vectors = jnp.concatenate(
        [v.reshape(rows, -1) for v in (attn_gain, mlp_gain, gate_bias, down_bias, up_bias)], 1
    )
    vectors = jnp.pad(vectors, ((0, 0), (0, VEC - vectors.shape[1])))
    main = VOCAB + VEC
    layouts = (
        ((0, main, 1), (main, 3 * D, 1), (main + 3 * D, NSTATE, 1)),
        ((0, NSTATE, 1), (NSTATE, D, 1), (NSTATE + D, 2 * D, 1), (NSTATE + 3 * D, D, 1)),
        ((0, HALF, 1), (HALF, D, folds // 2)),
    )
    packed = [
        jnp.concatenate(
            [char_table, vectors, query_weight, key_weight, value_weight, state_query], 1
        ),
        jnp.concatenate(
            [state_init, update_weight, state_key_weight, state_value_weight, out_weight], 1
        ),
    ]
    if fast:
        packed += [
            jnp.concatenate([up, fold(down, rows)], 1)
            for up, down in zip(halves_of_columns(up_weight), halves_of_rows(down_weight, 1))
        ]
        p1 = stack_z(packed[0], *along_z(packed[0]))
        shard = tie(packed[1], p1)
        sides1, z2 = join(to_sides(p1), along_z(shard))
        corner1, p2 = join(to_corner(p1, sides1), stack_z(shard, *z2))
        shard = tie(packed[2], p2)
        sides2, z3 = to_sides(p2), along_z(shard)
        table_vec, qkv_full, squery_full = full(p1, sides1, corner1, layouts[0])
    else:
        table_vec, qkv_full, squery_full = gather_any(packed[0], layouts[0])

    columns = jnp.transpose(f32(table_vec[:, VOCAB : VOCAB + 4]))
    gain_attn, gain_mlp, gbias_full, downbias_full = (columns[i] for i in range(4))
    mlp_rows = jnp.pad(jnp.stack([gain_mlp, downbias_full]), ((0, 6), (0, 0)))
    upbias_full = f32(table_vec[:, VOCAB + 4 : VOCAB + 4 + folds]).reshape(1, ff)
    keep_gate = jax.nn.sigmoid(gbias_full)
    is_first = lax.axis_index("seq") == 0
    bias_rows = f32(position_table)[:, None, :]

    one_hot = (char_ids[:, None] == jnp.arange(VOCAB)[None, :]).astype(jnp.bfloat16)
    embedded = dot(one_hot, table_vec[:, :VOCAB], NT)
    attn_scale = norm_scale(embedded)
    normed_low = low(embedded * attn_scale * gain_attn)
    qkv = low(dot(normed_low, qkv_full, NN))
    prev = from_behind(qkv[:, D:], "seq", 1)
    state_mix, state_lse = state_attention(qkv, squery_full)
    if fast:
        sides2, z3, state_mix = join(sides2, z3, state_mix)
        corner2, p3 = join(to_corner(p2, sides2), stack_z(shard, *z3))
        shard = tie(packed[3], p3)
        sides3, z4 = to_sides(p3), along_z(shard)
        sinit_full, update_full, skv_full, out_full = full(p2, sides2, corner2, layouts[1])
    else:
        sinit_full, update_full, skv_full, out_full = gather_any(packed[1], layouts[1])
    update = dot(state_mix, update_full, NN)
    start = f32(join(jnp.transpose(sinit_full))[0])
    mine = low((1.0 - keep_gate) * update)
    if fast:
        state_prev = earlier_sum(keep_gate, mine, start)
    else:
        gain, total = entering(keep_gate, mine, False)
        state_prev = gain * start + total
    state_low = low(state_prev)
    skv = low(dot(state_low, skv_full, NN))
    if fast:
        sides3, z4, skv, prev = join(sides3, z4, skv, prev)
        corner3, p4 = to_corner(p3, sides3), stack_z(shard, *z4)
    mixed, lse = attention(qkv, prev, skv, bias_rows)
    if fast:
        corner3, p4, mixed = join(corner3, p4, mixed)
    hidden = embedded + dot(mixed, out_full, NN)

    biases = halves_of_columns(upbias_full)
    if fast:
        sides4 = to_sides(p4)
        keep_a, away_a, bias_a, *before = mlp_half(
            core_of,
            hidden,
            out_grad,
            mlp_rows,
            biases[0],
            *full(p3, sides3, corner3, layouts[2]),
            None,
        )
        sides4, away_a, before = join(sides4, away_a, before)
        corner4, got_a = join(to_corner(p4, sides4), to_core(away_a))
        corner_a = from_corner(keep_a, got_a)
        keep_b, away_b, bias_b, *before = mlp_half(
            core_of,
            hidden,
            out_grad,
            mlp_rows,
            biases[1],
            *full(p4, sides4, corner4, layouts[2]),
            before,
        )
        corner_a, away_b, before = join(corner_a, away_b, before)
    else:
        shard = jnp.concatenate([up_weight, fold(down_weight, rows)], 1)
        up_full, down_full = gather_any(shard, ((0, ff, 1), (ff, D, folds)))
        mlp_weights = list(zip(halves_of_columns(up_full), halves_of_rows(down_full, CHUNKS)))
        keep_a, away_a, bias_a, *before = mlp_half(
            core_of, hidden, out_grad, mlp_rows, biases[0], *mlp_weights[0], None
        )
        keep_b, away_b, bias_b, *before = mlp_half(
            core_of, hidden, out_grad, mlp_rows, biases[1], *mlp_weights[1], before
        )
    output, grad_hidden, grad_branch, mlp_sums = before
    up_bias_grad = jnp.concatenate([b.reshape(CHUNKS, -1) for b in (bias_a, bias_b)], 1)

    grad_mixed = low(dot(grad_branch, out_full, NT))
    if fast:
        side_a, got_b, grad_mixed = join(
            from_side(keep_a, got_a, corner_a[0]), to_core(away_b), grad_mixed
        )
        ends_a = from_ends(keep_a, got_a, side_a, corner_a[1])
        corner_b = from_corner(keep_b, got_b)
    gq, gkv, gprev, gstate, gbias = attention_back(qkv, prev, skv, bias_rows, lse, grad_mixed)
    if fast:
        ends_a, corner_b, gprev, gstate = join(ends_a, corner_b, gprev, gstate)
    gnext = from_behind(gprev, "seq", -1)
    read = dot(gstate[0], skv_full[:, :D], NT) + dot(gstate[1], skv_full[:, D:], NT)
    first = weight_grads(
        core_of, [("dot", mixed, grad_branch), ("dot", state_low, gstate[0], gstate[1])]
    )
    if fast:
        side_b, got_c = from_side(keep_b, got_b, corner_b[0]), to_core(first[1])
        after = later_sum(keep_gate, low(read))
    else:
        after = entering(keep_gate, low(read), True)[1]
    gate_term = jnp.sum(after * (state_prev - update), 0)
    gate_bias_grad = gate_term * keep_gate * (1.0 - keep_gate)
    state_init_grad = jnp.where(is_first, read + keep_gate * after, 0.0)
    grad_update = low((1.0 - keep_gate) * after)
    grad_smix = low(dot(grad_update, update_full, NT))
    if fast:
        side_b, got_c, grad_smix = join(side_b, got_c, grad_smix)
        ends_b = from_ends(keep_b, got_b, side_b, corner_b[1])
        corner_c = from_corner(first[0], got_c)
    gsum, gquery = state_attention_back(qkv, squery_full, state_lse, grad_smix, gkv)
    second = weight_grads(
        core_of,
        [
            ("dot", state_mix, grad_update),
            ("rows", gquery),
            ("transposed", state_init_grad),
            ("dot", normed_low, gq),
        ],
    )
    if fast:
        ends_b, corner_c, second, gsum = join(ends_b, corner_c, second, gsum)
        side_c, got_d = from_side(first[0], got_c, corner_c[0]), to_core(second[1])
    gk, gv = (low(gsum[i] + f32(gnext[i])) for i in range(2))
    grad_normed = sum(
        dot(g, qkv_full[:, i * D : (i + 1) * D], NT) for i, g in enumerate((gq, gk, gv))
    )
    normed = embedded * attn_scale
    gained = grad_normed * gain_attn
    embedded_grad = grad_hidden + attn_scale * (
        gained - normed * jnp.mean(gained * normed, -1, keepdims=True)
    )
    attn_gain_grad = jnp.sum(grad_normed * normed, 0)
    position_rows = jnp.pad(gbias.reshape(HEADS, BLK), ((0, HEADS), (0, 0)))
    position_table_grad = jnp.sum(lax.all_gather(position_rows, AX), 0)[:HEADS]
    vector_grads = jnp.concatenate(
        [v[None] for v in (attn_gain_grad, mlp_sums[0], gate_bias_grad, mlp_sums[1])]
        + [jnp.transpose(up_bias_grad.reshape(D, folds))],
        0,
    )
    vector_grads = jnp.pad(vector_grads, ((0, VEC - vector_grads.shape[0]), (0, 0)))
    embedded_low = low(embedded_grad)
    if fast:
        side_c, got_d, embedded_low = join(side_c, got_d, embedded_low)
        ends_c = from_ends(first[0], got_c, side_c, corner_c[1])
        corner_d = from_corner(second[0], got_d)
    last = weight_grads(
        core_of,
        [
            ("dot", normed_low, gk, gv),
            ("dot", embedded_low, one_hot),
            ("transposed", vector_grads),
        ],
    )
    if fast:
        ends_c, corner_d, last = join(ends_c, corner_d, last)
        side_d, got_e = join(from_side(second[0], got_d, corner_d[0]), to_core(last[1]))
        ends_d = from_ends(second[0], got_d, side_d, corner_d[1])
        corner_e = from_corner(last[0], got_e)
        ends_d, corner_e = join(ends_d, corner_e)
        side_e = from_side(last[0], got_e, corner_e[0])
        ends_e = from_ends(last[0], got_e, side_e, corner_e[1])
        sums = [finish(s) for s in (ends_a, ends_b, ends_c, ends_d, ends_e)]
        up_sum = jnp.concatenate([s[:, :HALF].reshape(rows, CHUNKS, -1) for s in sums[:2]], 2)
        up_sum = up_sum.reshape(rows, ff)
        down_sum = jnp.concatenate([unfold(s[:, HALF:]) for s in sums[:2]], 0)
        first, second, last = sums[2:]
    else:
        pairs = [natural(keep_a, away_a), natural(keep_b, away_b)]
        up_sum = jnp.concatenate([s[:, :HALF].reshape(D, CHUNKS, -1) for s in pairs], 2)
        up_sum = scatter_any(up_sum.reshape(D, ff))
        down_sum = jnp.concatenate(
            [
                s[:, HALF:].reshape(CHUNKS, D // CHUNKS, -1, D).transpose(0, 2, 1, 3)
                for s in pairs
            ],
            1,
        )
        down_sum = scatter_any(down_sum.reshape(ff, D))
        first, second, last = (scatter_any(natural(*s)) for s in (first, second, last))
    table_at = 2 * D
    vector_sum = last[:, table_at + VOCAB :]
    return (
        output,
        embedded_grad,
        last[:, table_at : table_at + VOCAB],
        vector_sum[:, 0],
        second[:, 2 * D :],
        last[:, :D],
        last[:, D : 2 * D],
        first[:, :D],
        first[:, D : 2 * D],
        first[:, 2 * D :],
        second[:, :D],
        second[:, D : D + NSTATE],
        second[:, D + NSTATE : 2 * D],
        vector_sum[:, 2],
        position_table_grad,
        vector_sum[:, 1],
        up_sum,
        vector_sum[:, 4 : 4 + folds].reshape(-1),
        down_sum,
        vector_sum[:, 3],
    )


def solution(mesh):
    fast = dict(mesh.shape) == {"dp": 8, "seq": 4}
    return jax.shard_map(
        functools.partial(layer, fast),
        mesh=mesh,
        in_specs=(
            P(("dp", "seq")),
            P(("dp", "seq"), None),
            P(("dp", "seq")),
            P(("dp", "seq"), None),
            P(("dp", "seq"), None),
            P(("dp", "seq"), None),
            P(("dp", "seq"), None),
            P(("dp", "seq"), None),
            P(("dp", "seq"), None),
            P(("dp", "seq"), None),
            P(("dp", "seq"), None),
            P(("dp", "seq"), None),
            P(("dp", "seq")),
            P(),
            P(("dp", "seq")),
            P(("dp", "seq"), None),
            P(("dp", "seq")),
            P(("dp", "seq"), None),
            P(("dp", "seq")),
            P(("dp", "seq"), None),
        ),
        out_specs=(
            P(("dp", "seq"), None),
            P(("dp", "seq"), None),
            P(("dp", "seq"), None),
            P(("dp", "seq")),
            P(("dp", "seq"), None),
            P(("dp", "seq"), None),
            P(("dp", "seq"), None),
            P(("dp", "seq"), None),
            P(("dp", "seq"), None),
            P(("dp", "seq"), None),
            P(("dp", "seq"), None),
            P(("dp", "seq"), None),
            P(("dp", "seq"), None),
            P(("dp", "seq")),
            P(),
            P(("dp", "seq")),
            P(("dp", "seq"), None),
            P(("dp", "seq")),
            P(("dp", "seq"), None),
            P(("dp", "seq")),
        ),
        check_vma=False,
    )
```

time: 996 us -> 634 us (0.64)
  matrix products: 236 us -> 37.7 us
  local copies, waits for them, and re-layouts: 244 us -> 70 us
  Pallas kernels: 31.4 us -> 154 us
  waiting for transfers between devices: 237 us -> 169 us
  other arithmetic: 123 us -> 64.3 us
  starting transfers between devices: 104 us -> 115 us
    dot_general x41 -> x12, matrix products: 236 us -> 37.7 us  [dot(): lax.dot_general(a, b, (dims, ((), ())), preferred_element_type=jnp.float32)]
    pallas_call x0 -> x9, Pallas kernels: none -> 122 us  [the longest x2 50 us: mlp_half(): pl.pallas_call(functools.partial(mlp_body, last, core_of), grid=(HALF //...]
    unnamed x254 -> x228, local copies, waits for them, and re-layouts: 112 us -> 27.7 us
    ppermute x78 -> x81, waiting for transfers between devices: 235 us -> 169 us  [send(): return lax.ppermute(v, AX, pairs)]
    convert_element_type x6 -> x1, other arithmetic: 31.2 us -> 0.13 us  [layer(): (char_ids[:, None] == jnp.arange(VOCAB)[None, :]).astype(jnp.bfloat16)]
    reshape x17 -> x18, local copies, waits for them, and re-layouts: 46.9 us -> 16.1 us  [the longest x5 3.76 us: layer(): v.reshape(rows, -1)]
    concatenate x11 -> x4, local copies, waits for them, and re-layouts: 19.7 us -> 0.91 us  [the longest x1 0.76 us: layer(): jnp.concatenate([char_table, vectors, query_weight, key_weight, value_wei...]
    reduce_sum x4 -> x2, other arithmetic: 17.8 us -> 5.37 us  [the longest x1 4.08 us: layer(): gate_term = jnp.sum(after * (state_prev - update), 0)]
  transfers between devices with their start and end apart: 81 -> 84, of which waited for: 27 -> 28; matrix products, arithmetic and copies ran while one was open for 42% -> 19% of each run, Pallas kernels for 2% -> 23%
where the time goes in v2:
time: 634 us; the launch traced here: 626 us
  waiting for transfers between devices  169 us (27%)
  Pallas kernels  154 us (24%)
  starting transfers between devices  115 us (18%)
  local copies, waits for them, and re-layouts  70 us (11%)
  other arithmetic  64.3 us (10%)
  matrix products  37.7 us (6%)
  between operations  16 us (3%)
    ppermute x81, waiting for transfers between devices, send(): return lax.ppermute(v, AX, pairs)  169 us
    ppermute x81, starting transfers between devices, send(): return lax.ppermute(v, AX, pairs)  111 us
    pallas_call x2, Pallas kernels, mlp_half(): pl.pallas_call(functools.partial(mlp_body, last, core_of), grid=(HALF //...  50 us
    dot_general x12, matrix products, dot(): lax.dot_general(a, b, (dims, ((), ())), preferred_element_type=jnp.float32)  37.7 us
    convert_element_type x16, other arithmetic, low(): return v.astype(jnp.bfloat16)  34.9 us
    unnamed x228, local copies, waits for them, and re-layouts  27.7 us
    pallas_call x1, Pallas kernels, attention_back(): pl.pallas_call(attention_back_body, grid=(HEADS,), in_specs=[head_block(0...  22.9 us
    pallas_call x4, Pallas kernels, assemble(): pl.pallas_call(body, out_shape=[jax.ShapeDtypeStruct((4, 2, 2, 2, rows *...  22.1 us
  transfers between devices with their start and end apart: 84, of which 28 were waited for; matrix products, arithmetic and copies ran while one was open for 19% of the time, Pallas kernels for 23%

profile of v2, /device:TPU:0, one launch (start us, length us, event | category | flops | bytes accessed | tf_op | source)
XLA Modules:
  0.0 625.9 jit_solution(13488376840631348420)
XLA Ops:
  27.4 10.0 %collective-permute-done.1.refs_2_ = bf16[32,3968]{1,0:T(8,128)(2,1)S(1)} collective-permute-done((bf16[32,3968]{1,0:T(8,128)(2,1)S(1)}, bf16[32,3968]{1,0:T(8,128)(2,1)S(1)}, u32[]{:S(2)}, u32[]{:S(2)}) %collective-permute-start.1) | collective-permute-done | bytes 253984 | tf_op jit(solution)/shard_map/ppermute | solution.py:52
  52.1 7.3 %collective-permute-done.5.refs_1_ = bf16[32,4608]{1,0:T(8,128)(2,1)S(1)} collective-permute-done((bf16[32,4608]{1,0:T(8,128)(2,1)S(1)}, bf16[32,4608]{1,0:T(8,128)(2,1)S(1)}, u32[]{:S(2)}, u32[]{:S(2)}) %collective-permute-start.5) | collective-permute-done | bytes 294944 | tf_op jit(solution)/shard_map/ppermute | solution.py:52
  59.4 10.3 %collective-permute-done.6.refs_2_ = bf16[32,4608]{1,0:T(8,128)(2,1)S(1)} collective-permute-done((bf16[32,4608]{1,0:T(8,128)(2,1)S(1)}, bf16[32,4608]{1,0:T(8,128)(2,1)S(1)}, u32[]{:S(2)}, u32[]{:S(2)}) %collective-permute-start.6) | collective-permute-done | bytes 294944 | tf_op jit(solution)/shard_map/ppermute | solution.py:52
  72.9 11.5 %collective-permute-done.8.refs_3_ = bf16[4,32,3968]{2,1,0:T(8,128)(2,1)} collective-permute-done((bf16[4,32,3968]{2,1,0:T(8,128)(2,1)S(1)}, bf16[4,32,3968]{2,1,0:T(8,128)(2,1)}, u32[]{:S(2)}, u32[]{:S(2)}) %collective-permute-start.8) | collective-permute-done | bytes 1015840 | tf_op jit(solution)/shard_map/ppermute | solution.py:52
  95.9 6.8 %collective-permute-start.15 = (bf16[32,4096]{1,0:T(8,128)(2,1)}, bf16[32,4096]{1,0:T(8,128)(2,1)}, u32[]{:S(2)}, u32[]{:S(2)}) collective-permute-start(bf16[32,4096]{1,0:T(8,128)(2,1)} %pad_maximum_fusion.2.refs_0_), channel_id=1, source_target_pairs={{0,8},{1,9},{2,10},{3,11},{4,12},{5,13},{6,14},{7,15},{8,16},{9,17... | collective-permute-start | bytes 786440 | tf_op jit(solution)/shard_map/ppermute | solution.py:52
  115.1 6.5 %convolution_convert_fusion.k.v.q = bf16[512,3072]{1,0:T(8,128)(2,1)S(1)} fusion(bf16[512,1024]{1,0:T(8,128)(2,1)S(1)} %multiply_convert_fusion.2.refs_4_.refs_0_, bf16[1024,3072]{1,0:T(8,128)(2,1)} %bitcast.236), kind=kOutput, calls=%fused_computation | convolution fusion | flops 3222798336 | bytes 10485760 | tf_op jit(solution)/shard_map/dot_general | solution.py:261
  121.6 7.0 %state_attention.1 = (bf16[512,1024]{1,0:T(8,128)(2,1)S(1)}, f32[8,1,512]{2,1,0:T(1,128)S(1)}) custom-call(bf16[512,3072]{1,0:T(8,128)(2,1)S(1)} %convolution_convert_fusion.k.v.q, bf16[512,3072]{1,0:T(8,128)(2,1)S(1)} %convolution_convert_fusion.k.v.q, bf16[1024,512]{1,0:T(8,128)(2,1)S(1)} %bitcast.198), custom_call_target="tpu_custom_call" | custom-call | flops 1073741824 | bytes 4194304 | tf_op jit(solution)/shard_map/state_attention/pallas_call | solution.py:401
  137.5 12.6 %collective-permute-done.18.refs_3_ = bf16[4,32,4608]{2,1,0:T(8,128)(2,1)} collective-permute-done((bf16[4,32,4608]{2,1,0:T(8,128)(2,1)}, bf16[4,32,4608]{2,1,0:T(8,128)(2,1)}, u32[]{:S(2)}, u32[]{:S(2)}) %collective-permute-start.18) | collective-permute-done | bytes 1179680 | tf_op jit(solution)/shard_map/ppermute | solution.py:52
  153.2 6.4 %assemble.5 = (bf16[4,2,2,2,32,512]{5,4,3,2,1,0:T(8,128)(2,1)S(1)}, bf16[4,2,2,2,32,1024]{5,4,3,2,1,0:T(8,128)(2,1)S(1)}, bf16[4,2,2,2,32,2048]{5,4,3,2,1,0:T(8,128)(2,1)}, bf16[4,2,2,2,32,1024]{5,4,3,2,1,0:T(8,128)(2,1)}) custom-call(bf16[4,32,4608]{2,1,0:T(8,128)(2,1)} %stack_z.5.refs_0_, bf16[4,32,4608]{2,1,0:T(8,128)(2,1)} %collective-permute-done.13.refs_1_, ...), custom_call_target="tpu_custom_call" | custom-call | tf_op jit(solution)/shard_map/assemble/pallas_call | solution.py:85
  173.5 8.9 %collective-permute-done.29 = bf16[256,1024]{1,0:T(8,128)(2,1)} collective-permute-done((bf16[256,1024]{1,0:T(8,128)(2,1)S(1)}, bf16[256,1024]{1,0:T(8,128)(2,1)}, u32[]{:S(2)}, u32[]{:S(2)}) %collective-permute-start.29) | collective-permute-done | bytes 524320 | tf_op jit(solution)/shard_map/ppermute | solution.py:52
  214.4 13.3 %collective-permute-start.34 = (bf16[4,32,4096]{2,1,0:T(8,128)(2,1)}, bf16[4,32,4096]{2,1,0:T(8,128)(2,1)}, u32[]{:S(2)}, u32[]{:S(2)}) collective-permute-start(bf16[4,32,4096]{2,1,0:T(8,128)(2,1)} %collective-permute-done.22.refs_1_), channel_id=1, source_target_pairs={{0,1},{1,0},{2,3},{3,2},{4,5},{5,4},{6,7},{7,6},{8,9},{9,8},{10,11... | collective-permute-start | bytes 3145736 | tf_op jit(solution)/shard_map/ppermute | solution.py:52
  231.6 13.8 %attention.1 = (bf16[512,1024]{1,0:T(8,128)(2,1)S(1)}, f32[8,1,512]{2,1,0:T(1,128)S(1)}) custom-call(bf16[512,3072]{1,0:T(8,128)(2,1)S(1)} %convolution_convert_fusion.k.v.q, bf16[512,3072]{1,0:T(8,128)(2,1)S(1)} %convolution_convert_fusion.k.v.q, bf16[512,3072]{1,0:T(8,128)(2,1)S(1)} %convolution_convert_fusion.k.v.q, ...), custom_call_target="tpu_custom_call" | custom-call | flops 3221225472 | bytes 9437184 | tf_op jit(solution)/shard_map/attention/pallas_call | solution.py:307
  263.8 23.3 %mlp_half.2 = (bf16[512,4096]{1,0:T(8,128)(2,1)}, bf16[512,4096]{1,0:T(8,128)(2,1)}, f32[1,2048]{1,0:T(1,128)}, f32[512,1024]{1,0:T(8,128)}, f32[512,1024]{1,0:T(8,128)}) custom-call(f32[512,1024]{1,0:T(8,128)} %convolution_add_fusion.refs_0_, bf16[512,1024]{1,0:T(8,128)(2,1)} %refs_1_.3, f32[8,1024]{1,0:T(8,128)} %select_maximum_fusion.refs_2_, ...), custom_call_target="tpu_custom_call" | custom-call | flops 12884901888 | bytes 31457280 | tf_op jit(solution)/shard_map/mlp_half/pallas_call | solution.py:552
  316.9 26.8 %mlp_half.3 = (bf16[512,4096]{1,0:T(8,128)(2,1)}, bf16[512,4096]{1,0:T(8,128)(2,1)}, f32[1,2048]{1,0:T(1,128)}, bf16[512,1024]{1,0:T(8,128)(2,1)}, f32[512,1024]...) custom-call(f32[512,1024]{1,0:T(8,128)} %convolution_add_fusion.refs_0_, bf16[512,1024]{1,0:T(8,128)(2,1)} %refs_1_.3, ...), custom_call_target="tpu_custom_call" | custom-call | flops 12884901888 | bytes 31457280 | tf_op jit(solution)/shard_map/mlp_half/pallas_call | solution.py:552
  354.1 7.1 %collective-permute-done.47 = bf16[4,32,4096]{2,1,0:T(8,128)(2,1)} collective-permute-done((bf16[4,32,4096]{2,1,0:T(8,128)(2,1)S(1)}, bf16[4,32,4096]{2,1,0:T(8,128)(2,1)}, u32[]{:S(2)}, u32[]{:S(2)}) %collective-permute-start.47) | collective-permute-done | bytes 1048608 | tf_op jit(solution)/shard_map/ppermute | solution.py:52
  373.1 22.9 %attention_back.1 = (bf16[512,1024]{1,0:T(8,128)(2,1)S(1)}, f32[2,512,1024]{2,1,0:T(8,128)}, bf16[2,512,1024]{2,1,0:T(8,128)(2,1)S(1)}, bf16[2,512,1024]{2,1,0:T(8,128)(2,1)}, f32[8,1,512]{2,1,0:T(1,128)S(1)}) custom-call(bf16[512,3072]{1,0:T(8,128)(2,1)} %copy-done, bf16[512,3072]{1,0:T(8,128)(2,1)} %copy-done, bf16[512,3072]{1,0:T(8,128)(2,1)} %copy-done, ...), custom_call_target="tpu_custom_call" | custom-call | flops 8053063680 | bytes 18874368 | tf_op jit(solution)/shard_map/attention_back/pallas_call | solution.py:362
  428.0 9.1 %collective-permute-done.57 = bf16[256,1024]{1,0:T(8,128)(2,1)S(1)} collective-permute-done((bf16[256,1024]{1,0:T(8,128)(2,1)S(1)}, bf16[256,1024]{1,0:T(8,128)(2,1)S(1)}, u32[]{:S(2)}, u32[]{:S(2)}) %collective-permute-start.57) | collective-permute-done | bytes 524320 | tf_op jit(solution)/shard_map/ppermute | solution.py:52
  458.8 7.7 %collective-permute-done.59 = bf16[32,4096]{1,0:T(8,128)(2,1)S(1)} collective-permute-done((bf16[32,4096]{1,0:T(8,128)(2,1)S(1)}, bf16[32,4096]{1,0:T(8,128)(2,1)S(1)}, u32[]{:S(2)}, u32[]{:S(2)}) %collective-permute-start.59) | collective-permute-done | bytes 262176 | tf_op jit(solution)/shard_map/ppermute | solution.py:52
  466.6 10.3 %state_attention_back.1 = (f32[2,512,1024]{2,1,0:T(8,128)S(1)}, bf16[1024,512]{1,0:T(8,128)(2,1)S(1)}) custom-call(bf16[512,3072]{1,0:T(8,128)(2,1)S(1)} %copy-done.1, bf16[512,3072]{1,0:T(8,128)(2,1)S(1)} %copy-done.1, bf16[1024,512]{1,0:T(8,128)(2,1)S(1)} %bitcast.199, f32[8,1,512]{2,1,0:T(1,128)S(1)} %get-tuple-element.246.lse, ...), custom_call_target="tpu_custom_call" | custom-call | flops 2684354560 | bytes 14680064 | tf_op jit(solution)/shard_map/state_attention_back/pallas_call | solution.py:432
  482.5 7.0 %weight_grads.4 = (bf16[512,3072]{1,0:T(8,128)(2,1)}, bf16[512,3072]{1,0:T(8,128)(2,1)}) custom-call(bf16[512,1024]{1,0:T(8,128)(2,1)S(1)} %copy-done.27, bf16[512,1024]{1,0:T(8,128)(2,1)S(1)} %get-tuple-element.319.refs_1_, bf16[1024,512]{1,0:T(8,128)(2,1)S(1)} %copy-done.31, f32[512,1024]{1,0:T(8,128)} %get-tuple-element.320.refs_3_, ...), custom_call_target="tpu_custom_call" | custom-call | flops 2147483648 | bytes 12582912 | tf_op jit(solution)/shard_map/weight_grads/pallas_call | solution.py:634
  520.0 8.4 %collective-permute-start.67 = (bf16[32,3072]{1,0:T(8,128)(2,1)S(1)}, bf16[32,3072]{1,0:T(8,128)(2,1)S(1)}, u32[]{:S(2)}, u32[]{:S(2)}) collective-permute-start(bf16[32,3072]{1,0:T(8,128)(2,1)S(1)} %get-tuple-element.334), channel_id=1, source_target_pairs={{0,8},{1,9},{2,10},{3,11},{4,12},{5,13},{6,14},{7,15},{8,16},{9,17... | collective-permute-start | bytes 589832 | tf_op jit(solution)/shard_map/ppermute | solution.py:52
  554.8 9.6 %collective-permute-done.72 = bf16[4,32,3072]{2,1,0:T(8,128)(2,1)S(1)} collective-permute-done((bf16[4,32,3072]{2,1,0:T(8,128)(2,1)S(1)}, bf16[4,32,3072]{2,1,0:T(8,128)(2,1)S(1)}, u32[]{:S(2)}, u32[]{:S(2)}) %collective-permute-start.72) | collective-permute-done | bytes 786464 | tf_op jit(solution)/shard_map/ppermute | solution.py:52
  581.0 6.3 %collective-permute-done.75 = bf16[32,3072]{1,0:T(8,128)(2,1)S(1)} collective-permute-done((bf16[32,3072]{1,0:T(8,128)(2,1)S(1)}, bf16[32,3072]{1,0:T(8,128)(2,1)S(1)}, u32[]{:S(2)}, u32[]{:S(2)}) %collective-permute-start.75) | collective-permute-done | bytes 196640 | tf_op jit(solution)/shard_map/ppermute | solution.py:52
  591.1 7.9 %collective-permute-done.79 = bf16[4,32,2432]{2,1,0:T(8,128)(2,1)S(1)} collective-permute-done((bf16[4,32,2432]{2,1,0:T(8,128)(2,1)S(1)}, bf16[4,32,2432]{2,1,0:T(8,128)(2,1)S(1)}, u32[]{:S(2)}, u32[]{:S(2)}) %collective-permute-start.79) | collective-permute-done | bytes 622624 | tf_op jit(solution)/shard_map/ppermute | solution.py:52
  (505 shorter events, 349.0 us)
Async XLA Ops:
  7.2 485.7 %all-gather.3.cloned.1.call-start = ((), (), s32[]{:S(2)}) async-start(), calls=%async_computation | async-start | bytes 1081344 | tf_op jit(solution)/shard_map/all_gather | solution.py:843
  41.2 28.5 %collective-permute-start.3 = (bf16[4,32,3968]{2,1,0:T(8,128)(2,1)}, bf16[4,32,3968]{2,1,0:T(8,128)(2,1)S(1)}, u32[]{:S(2)}, u32[]{:S(2)}) collective-permute-start(bf16[4,32,3968]{2,1,0:T(8,128)(2,1)} %stack_z.4.refs_0_), channel_id=1, source_target_pairs={{0,2},{1,5},{2,0},{3,7},{4,6},{5,1},{6,4},{7,3},{8,10},{9,13},{10,... | collective-permute-start | bytes 3047432 | tf_op jit(solution)/shard_map/ppermute | solution.py:52
  42.7 27.0 %collective-permute-start.4 = (bf16[4,32,3968]{2,1,0:T(8,128)(2,1)}, bf16[4,32,3968]{2,1,0:T(8,128)(2,1)S(1)}, u32[]{:S(2)}, u32[]{:S(2)}) collective-permute-start(bf16[4,32,3968]{2,1,0:T(8,128)(2,1)} %stack_z.4.refs_0_), channel_id=1, source_target_pairs={{0,4},{1,3},{2,6},{3,1},{4,0},{5,7},{6,2},{7,5},{8,12},{9,11},{10,... | collective-permute-start | bytes 3047432 | tf_op jit(solution)/shard_map/ppermute | solution.py:52
  95.9 33.6 %collective-permute-start.15 = (bf16[32,4096]{1,0:T(8,128)(2,1)}, bf16[32,4096]{1,0:T(8,128)(2,1)}, u32[]{:S(2)}, u32[]{:S(2)}) collective-permute-start(bf16[32,4096]{1,0:T(8,128)(2,1)} %pad_maximum_fusion.2.refs_0_), channel_id=1, source_target_pairs={{0,8},{1,9},{2,10},{3,11},{4,12},{5,13},{6,14},{7,15},{8,16},{9,17... | collective-permute-start | bytes 786440 | tf_op jit(solution)/shard_map/ppermute | solution.py:52
  105.2 28.4 %collective-permute-start.13 = (bf16[4,32,4608]{2,1,0:T(8,128)(2,1)}, bf16[4,32,4608]{2,1,0:T(8,128)(2,1)}, u32[]{:S(2)}, u32[]{:S(2)}) collective-permute-start(bf16[4,32,4608]{2,1,0:T(8,128)(2,1)} %stack_z.5.refs_0_), channel_id=1, source_target_pairs={{0,2},{1,5},{2,0},{3,7},{4,6},{5,1},{6,4},{7,3},{8,10},{9,13},{10,... | collective-permute-start | bytes 3538952 | tf_op jit(solution)/shard_map/ppermute | solution.py:52
  105.8 27.8 %collective-permute-start.14 = (bf16[4,32,4608]{2,1,0:T(8,128)(2,1)}, bf16[4,32,4608]{2,1,0:T(8,128)(2,1)}, u32[]{:S(2)}, u32[]{:S(2)}) collective-permute-start(bf16[4,32,4608]{2,1,0:T(8,128)(2,1)} %stack_z.5.refs_0_), channel_id=1, source_target_pairs={{0,4},{1,3},{2,6},{3,1},{4,0},{5,7},{6,2},{7,5},{8,12},{9,11},{10,... | collective-permute-start | bytes 3538952 | tf_op jit(solution)/shard_map/ppermute | solution.py:52
  170.4 39.4 %collective-permute-start.31 = (bf16[512,2048]{1,0:T(8,128)(2,1)}, bf16[512,2048]{1,0:T(8,128)(2,1)}, u32[]{:S(2)}, u32[]{:S(2)}) collective-permute-start(bf16[512,2048]{1,0:T(8,128)(2,1)} %slice.204), channel_id=1, source_target_pairs={{0,1},{1,2},{2,3},{4,5},{5,6},{6,7},{8,9},{9,10},{10,11},{12,13},{... | collective-permute-start | bytes 6291464 | tf_op jit(solution)/shard_map/ppermute | solution.py:214
  207.2 39.2 %collective-permute-start.33 = (bf16[4,32,4096]{2,1,0:T(8,128)(2,1)}, bf16[4,32,4096]{2,1,0:T(8,128)(2,1)}, u32[]{:S(2)}, u32[]{:S(2)}) collective-permute-start(bf16[4,32,4096]{2,1,0:T(8,128)(2,1)} %stack_z.6.refs_0_), channel_id=1, source_target_pairs={{0,1},{1,0},{2,3},{3,2},{4,5},{5,4},{6,7},{7,6},{8,9},{9,8},{10,11... | collective-permute-start | bytes 3145736 | tf_op jit(solution)/shard_map/ppermute | solution.py:52
  212.8 33.5 %collective-permute-start.32 = (bf16[4,32,4096]{2,1,0:T(8,128)(2,1)}, bf16[4,32,4096]{2,1,0:T(8,128)(2,1)}, u32[]{:S(2)}, u32[]{:S(2)}) collective-permute-start(bf16[4,32,4096]{2,1,0:T(8,128)(2,1)} %collective-permute-done.22.refs_1_), channel_id=1, source_target_pairs={{0,4},{1,3},{2,6},{3,1},{4,0},{5,7},{6,2},{7,5},{8,12},{9,11},{10,... | collective-permute-start | bytes 3145736 | tf_op jit(solution)/shard_map/ppermute | solution.py:52
  214.4 32.0 %collective-permute-start.34 = (bf16[4,32,4096]{2,1,0:T(8,128)(2,1)}, bf16[4,32,4096]{2,1,0:T(8,128)(2,1)}, u32[]{:S(2)}, u32[]{:S(2)}) collective-permute-start(bf16[4,32,4096]{2,1,0:T(8,128)(2,1)} %collective-permute-done.22.refs_1_), channel_id=1, source_target_pairs={{0,1},{1,0},{2,3},{3,2},{4,5},{5,4},{6,7},{7,6},{8,9},{9,8},{10,11... | collective-permute-start | bytes 3145736 | tf_op jit(solution)/shard_map/ppermute | solution.py:52
  249.7 37.3 %collective-permute-start.37 = (bf16[4,32,4096]{2,1,0:T(8,128)(2,1)}, bf16[4,32,4096]{2,1,0:T(8,128)(2,1)S(1)}, u32[]{:S(2)}, u32[]{:S(2)}) collective-permute-start(bf16[4,32,4096]{2,1,0:T(8,128)(2,1)} %stack_z.7.refs_0_), channel_id=1, source_target_pairs={{0,2},{1,5},{2,0},{3,7},{4,6},{5,1},{6,4},{7,3},{8,10},{9,13},{10,... | collective-permute-start | bytes 3145736 | tf_op jit(solution)/shard_map/ppermute | solution.py:52
  250.0 37.1 %collective-permute-start.38 = (bf16[4,32,4096]{2,1,0:T(8,128)(2,1)}, bf16[4,32,4096]{2,1,0:T(8,128)(2,1)S(1)}, u32[]{:S(2)}, u32[]{:S(2)}) collective-permute-start(bf16[4,32,4096]{2,1,0:T(8,128)(2,1)} %stack_z.7.refs_0_), channel_id=1, source_target_pairs={{0,4},{1,3},{2,6},{3,1},{4,0},{5,7},{6,2},{7,5},{8,12},{9,11},{10,... | collective-permute-start | bytes 3145736 | tf_op jit(solution)/shard_map/ppermute | solution.py:52
  308.3 35.4 %collective-permute-start.44 = (bf16[4,32,4096]{2,1,0:T(8,128)(2,1)S(1)}, bf16[4,32,4096]{2,1,0:T(8,128)(2,1)}, u32[]{:S(2)}, u32[]{:S(2)}) collective-permute-start(bf16[4,32,4096]{2,1,0:T(8,128)(2,1)S(1)} %get-tuple-element.309), channel_id=1, source_target_pairs={{0,4},{1,3},{2,6},{3,1},{4,0},{5,7},{6,2},{7,5},{8,12},{9,11},{10,... | collective-permute-start | bytes 3145736 | tf_op jit(solution)/shard_map/ppermute | solution.py:52
  309.3 34.4 %collective-permute-start.45 = (bf16[4,32,4096]{2,1,0:T(8,128)(2,1)S(1)}, bf16[4,32,4096]{2,1,0:T(8,128)(2,1)}, u32[]{:S(2)}, u32[]{:S(2)}) collective-permute-start(bf16[4,32,4096]{2,1,0:T(8,128)(2,1)S(1)} %get-tuple-element.308), channel_id=1, source_target_pairs={{0,4},{1,3},{2,6},{3,1},{4,0},{5,7},{6,2},{7,5},{8,12},{9,11},{10,... | collective-permute-start | bytes 3145736 | tf_op jit(solution)/shard_map/ppermute | solution.py:52
  363.6 33.4 %collective-permute-start.52 = (bf16[4,32,4096]{2,1,0:T(8,128)(2,1)S(1)}, bf16[4,32,4096]{2,1,0:T(8,128)(2,1)S(1)}, u32[]{:S(2)}, u32[]{:S(2)}) collective-permute-start(bf16[4,32,4096]{2,1,0:T(8,128)(2,1)S(1)} %get-tuple-element.307), channel_id=1, source_target_pairs={{0,4},{1,3},{2,6},{3,1},{4,0},{5,7},{6,2},{7,5},{8,12},{9,11},{10,... | collective-permute-start | bytes 3145736 | tf_op jit(solution)/shard_map/ppermute | solution.py:52
  364.6 32.5 %collective-permute-start.53 = (bf16[4,32,4096]{2,1,0:T(8,128)(2,1)S(1)}, bf16[4,32,4096]{2,1,0:T(8,128)(2,1)S(1)}, u32[]{:S(2)}, u32[]{:S(2)}) collective-permute-start(bf16[4,32,4096]{2,1,0:T(8,128)(2,1)S(1)} %get-tuple-element.306), channel_id=1, source_target_pairs={{0,4},{1,3},{2,6},{3,1},{4,0},{5,7},{6,2},{7,5},{8,12},{9,11},{10,... | collective-permute-start | bytes 3145736 | tf_op jit(solution)/shard_map/ppermute | solution.py:52
  369.3 27.7 %collective-permute-start.49 = (bf16[32,4096]{1,0:T(8,128)(2,1)}, bf16[32,4096]{1,0:T(8,128)(2,1)S(1)}, u32[]{:S(2)}, u32[]{:S(2)}) collective-permute-start(bf16[32,4096]{1,0:T(8,128)(2,1)} %get-tuple-element.328), channel_id=1, source_target_pairs={{0,8},{1,9},{2,10},{3,11},{4,12},{5,13},{6,14},{7,15},{8,16},{9,17... | collective-permute-start | bytes 786440 | tf_op jit(solution)/shard_map/ppermute | solution.py:52
  420.1 28.2 %collective-permute-start.55 = (bf16[512,3072]{1,0:T(8,128)(2,1)}, bf16[512,3072]{1,0:T(8,128)(2,1)S(1)}, u32[]{:S(2)}, u32[]{:S(2)}) collective-permute-start(bf16[512,3072]{1,0:T(8,128)(2,1)} %get-tuple-element.241), channel_id=1, source_target_pairs={{0,1},{1,0},{2,3},{3,2},{4,5},{5,4},{6,7},{7,6},{8,9},{9,8},{10,11... | collective-permute-start | bytes 9437192 | tf_op jit(solution)/shard_map/ppermute | solution.py:52
  426.6 73.1 %collective-permute-start.64 = (bf16[2,512,1024]{2,1,0:T(8,128)(2,1)S(1)}, bf16[2,512,1024]{2,1,0:T(8,128)(2,1)}, u32[]{:S(2)}, u32[]{:S(2)}) collective-permute-start(bf16[2,512,1024]{2,1,0:T(8,128)(2,1)S(1)} %get-tuple-element.254), channel_id=1, source_target_pairs={{1,0},{2,1},{3,2},{5,4},{6,5},{7,6},{9,8},{10,9},{11,10},{13,12},{... | collective-permute-start | bytes 6291464 | tf_op jit(solution)/shard_map/ppermute | solution.py:214
  450.5 39.0 %collective-permute-start.62 = (bf16[4,32,3072]{2,1,0:T(8,128)(2,1)}, bf16[4,32,3072]{2,1,0:T(8,128)(2,1)}, u32[]{:S(2)}, u32[]{:S(2)}) collective-permute-start(bf16[4,32,3072]{2,1,0:T(8,128)(2,1)} %get-tuple-element.315), channel_id=1, source_target_pairs={{0,4},{1,3},{2,6},{3,1},{4,0},{5,7},{6,2},{7,5},{8,12},{9,11},{10,... | collective-permute-start | bytes 2359304 | tf_op jit(solution)/shard_map/ppermute | solution.py:52
  451.4 38.0 %collective-permute-start.63 = (bf16[4,32,3072]{2,1,0:T(8,128)(2,1)}, bf16[4,32,3072]{2,1,0:T(8,128)(2,1)}, u32[]{:S(2)}, u32[]{:S(2)}) collective-permute-start(bf16[4,32,3072]{2,1,0:T(8,128)(2,1)} %get-tuple-element.314), channel_id=1, source_target_pairs={{0,4},{1,3},{2,6},{3,1},{4,0},{5,7},{6,2},{7,5},{8,12},{9,11},{10,... | collective-permute-start | bytes 2359304 | tf_op jit(solution)/shard_map/ppermute | solution.py:52
  456.3 33.1 %collective-permute-start.60 = (bf16[32,4096]{1,0:T(8,128)(2,1)}, bf16[32,4096]{1,0:T(8,128)(2,1)}, u32[]{:S(2)}, u32[]{:S(2)}) collective-permute-start(bf16[32,4096]{1,0:T(8,128)(2,1)} %get-tuple-element.322), channel_id=1, source_target_pairs={{0,16},{1,17},{2,18},{3,19},{4,20},{5,21},{6,22},{7,23},{8,24},{9,... | collective-permute-start | bytes 786440 | tf_op jit(solution)/shard_map/ppermute | solution.py:52
  515.5 29.0 %collective-permute-start.70 = (bf16[4,32,3072]{2,1,0:T(8,128)(2,1)S(1)}, bf16[4,32,3072]{2,1,0:T(8,128)(2,1)S(1)}, u32[]{:S(2)}, u32[]{:S(2)}) collective-permute-start(bf16[4,32,3072]{2,1,0:T(8,128)(2,1)S(1)} %get-tuple-element.311), channel_id=1, source_target_pairs={{0,4},{1,3},{2,6},{3,1},{4,0},{5,7},{6,2},{7,5},{8,12},{9,11},{10,... | collective-permute-start | bytes 2359304 | tf_op jit(solution)/shard_map/ppermute | solution.py:52
  516.5 28.1 %collective-permute-start.71 = (bf16[4,32,3072]{2,1,0:T(8,128)(2,1)S(1)}, bf16[4,32,3072]{2,1,0:T(8,128)(2,1)S(1)}, u32[]{:S(2)}, u32[]{:S(2)}) collective-permute-start(bf16[4,32,3072]{2,1,0:T(8,128)(2,1)S(1)} %get-tuple-element.310), channel_id=1, source_target_pairs={{0,4},{1,3},{2,6},{3,1},{4,0},{5,7},{6,2},{7,5},{8,12},{9,11},{10,... | collective-permute-start | bytes 2359304 | tf_op jit(solution)/shard_map/ppermute | solution.py:52
  (168 other events, 2007.8 us)
Sparse Core Ops, SparseCore 0:
  407.5 60.0 all-gather.2

commit v3 on v2

v3 whole, which is shorter than its diff:
```python
import functools

import jax
import jax.numpy as jnp
from jax import lax
from jax.experimental import pallas as pl
from jax.experimental.pallas import tpu as pltpu
from jax.sharding import PartitionSpec as P

D = 1024
HEADS = 8
HD = 128
NSTATE = 512
VOCAB = 256
BLK = 512
AX = ("dp", "seq")
VEC = 128


def f32(v):
    return v.astype(jnp.float32)


def low(v):
    return v.astype(jnp.bfloat16)


def route(move):
    pairs = []
    for z in range(4):
        for y in range(2):
            for x in range(2):
                for c in range(2):
                    tz, ty, tx, tc = move(z, y, x, c)
                    pairs.append((z * 8 + y * 4 + x * 2 + c, tz * 8 + ty * 4 + tx * 2 + tc))
    return pairs


A_ROUTE = route(lambda z, y, x, c: (z, y, 1 - x, c) if c == 0 else (z, 1 - y, x, c))
B_ROUTE = route(lambda z, y, x, c: (z, 1 - y, x, c) if c == 0 else (z, y, 1 - x, c))
CORE_ROUTE = route(lambda z, y, x, c: (z, y, x, 1 - c))
X_ROUTE = route(lambda z, y, x, c: (z, y, 1 - x, c))
Y_ROUTE = route(lambda z, y, x, c: (z, 1 - y, x, c))
Z_NEAR = route(lambda z, y, x, c: (z ^ 1, y, x, c))
Z_FAR = route(lambda z, y, x, c: (z ^ 2, y, x, c))
Z_ROUTE = {k: route(lambda z, y, x, c, k=k: ((z + k) % 4, y, x, c)) for k in (1, 2, 3)}


def place():
    d, s = lax.axis_index("dp"), lax.axis_index("seq")
    return d // 2, d % 2, s // 2, s % 2


def send(v, pairs):
    return lax.ppermute(v, AX, pairs)


def stack_z(shard, *others):
    others, cyclic = others[:3], others[3]

    def body(*refs):
        z = lax.axis_index("dp") // 2
        near = z + 1 - 2 * lax.rem(z, 2)
        spots = (
            [lax.rem(z + 4 - i, 4) for i in range(4)]
            if cyclic
            else [z, near, lax.rem(z + 2, 4), lax.rem(near + 2, 4)]
        )
        for at, src in zip(spots, refs[:4]):
            refs[4][at] = src[...]

    return pl.pallas_call(
        body, out_shape=jax.ShapeDtypeStruct((4,) + shard.shape, shard.dtype), name="stack_z"
    )(shard, *others)


def here():
    return lax.rem(lax.axis_index("dp"), 2), lax.axis_index("seq") // 2, core_index()


def core_index():
    return lax.rem(lax.axis_index("seq"), 2)


def origin(i, spot, alternate):
    y, x, c = spot
    core = c if i < 4 else 1 - c
    if alternate:
        flip_x = (0, 1 - core, core, 1)[i % 4]
        flip_y = (0, core, 1 - core, 1)[i % 4]
    else:
        flip_x, flip_y = i % 2, i % 4 // 2
    return lax.rem(y + flip_y, 2), lax.rem(x + flip_x, 2), core


def assemble(pieces, layout, alternate):
    rows, width = pieces[0].shape[1:]

    def body(*refs):
        ins, outs = refs[:8], refs[8:]
        spot = here()
        for i, src in enumerate(ins):
            ty, tx, core = origin(i, spot, alternate)
            for (first, w, folds), out in zip(layout, outs):
                for q in range(folds):
                    out[0, ty, tx, core, q * rows : (q + 1) * rows, :] = src[
                        0, :, first + q * w : first + (q + 1) * w
                    ]

    full = pl.pallas_call(
        body,
        out_shape=[
            jax.ShapeDtypeStruct((4, 2, 2, 2, rows * n, w), pieces[0].dtype) for _, w, n in layout
        ],
        grid=(4,),
        in_specs=[pl.BlockSpec((1, rows, width), lambda z: (z, 0, 0))] * 8,
        out_specs=[
            pl.BlockSpec((1, 2, 2, 2, rows * n, w), lambda z: (z, 0, 0, 0, 0, 0))
            for _, w, n in layout
        ],
        compiler_params=pltpu.CompilerParams(vmem_limit_bytes=40 * 2**20),
        name="assemble",
    )(*pieces)
    return [o.reshape(32 * rows * n, w) for o, (_, w, n) in zip(full, layout)]


def tie(value, *others):
    return lax.optimization_barrier((value, others))[0]


def join(*values):
    return lax.optimization_barrier(values)


def along_z(shard):
    return [send(shard, Z_ROUTE[k]) for k in (1, 2, 3)] + [True]


def far_z(shard, near):
    return [near, send(shard, Z_FAR), send(near, Z_FAR), False]


def to_sides(p, a=A_ROUTE, b=B_ROUTE):
    return send(p, a), send(p, b)


def to_corner(p, sides, b=B_ROUTE):
    return send(sides[0], b), [send(v, CORE_ROUTE) for v in (p,) + tuple(sides)]


def last_corner(corner):
    return send(corner[0], CORE_ROUTE)


def pieces(p, sides, corner, last):
    return (p,) + tuple(sides) + (corner[0],) + tuple(corner[1]) + (last,)


def to_core(away):
    return send(away, CORE_ROUTE)


def first_axis():
    z, y, x, c = place()
    return jnp.where(c == 0, y, x), jnp.where(c == 0, x, y)


def chip_part(keep, got, b, a=None):
    rows, width = keep.shape[0] // 16, keep.shape[1]
    start, size = ((b, 0), (1, 2)) if a is None else ((b, a), (1, 1))
    at = [
        lax.dynamic_slice(
            v.reshape(2, 2, 4, rows, width), start + (0, 0, 0), size + (4, rows, width)
        )
        for v in (keep, got)
    ]
    return (f32(at[0]) + f32(at[1])).reshape(size[1], 4, rows, width)


def over_first(keep, got):
    return send(low(chip_part(keep, got, 1 - first_axis()[0])), B_ROUTE)


def over_first_in_two(keep, got, corner):
    b, a = first_axis()
    return send(low(chip_part(keep, got, 1 - b, 1 - a if corner else a)), B_ROUTE)


def of_first(first, i):
    return lax.dynamic_index_in_dim(first, i, 0)


def over_second(keep, got, first):
    b, a = first_axis()
    far = first[0] if isinstance(first, tuple) else of_first(first, 1 - a)
    return send(low(chip_part(keep, got, b, 1 - a) + f32(far)), A_ROUTE)


def own_part(keep, got, first, second):
    b, a = first_axis()
    mine = first[1] if isinstance(first, tuple) else of_first(first, a)
    return (chip_part(keep, got, b, a) + f32(mine) + f32(second))[0]


def over_pairs(keep, got, first, second):
    z = place()[0]
    own = own_part(keep, got, first, second)
    pairs = own.reshape((2, 2) + own.shape[1:])
    away = lax.dynamic_index_in_dim(pairs, 1 - z // 2, 0, False)
    return lax.dynamic_index_in_dim(pairs, z // 2, 0, False), send(low(away), Z_FAR)


def within_pair(mine, got):
    z = place()[0]

    def pick(i):
        return lax.dynamic_index_in_dim(mine, i, 0, False) + f32(
            lax.dynamic_index_in_dim(got, i, 0, False)
        )

    return pick(z % 2), send(low(pick(1 - z % 2)), Z_NEAR)


def over_z(keep, got, first, second):
    z = place()[0]
    own = own_part(keep, got, first, second)
    rest = [low(lax.dynamic_index_in_dim(own, (z + k) % 4, 0, False)) for k in (1, 2, 3)]
    mine = lax.dynamic_index_in_dim(own, z, 0, False)
    return [mine] + [send(v, Z_ROUTE[k]) for v, k in zip(rest, (1, 2, 3))]


def finish(parts):
    return sum(f32(p) for p in parts)


def gather_any(shard, layout):
    rows = shard.shape[0]
    full = lax.all_gather(shard, AX, axis=0, tiled=True)
    outs = []
    for first, w, folds in layout:
        part = full[:, first : first + w * folds]
        if folds > 1:
            part = part.reshape(-1, rows, folds, w).transpose(0, 2, 1, 3).reshape(-1, w)
        outs.append(part)
    return outs


def scatter_any(grad):
    return lax.psum_scatter(f32(grad), AX, scatter_dimension=0, tiled=True)


def exchange(value, pairs):
    return value + send(value, pairs)


def half_across(chip):
    c = place()[3]
    half = NSTATE // 2
    return send(lax.dynamic_slice(chip, (c * half, 0), (half, D)), X_ROUTE)


def both_halves(near):
    c = place()[3]
    far = send(near, CORE_ROUTE)
    return jnp.concatenate([jnp.where(c == 0, near, far), jnp.where(c == 0, far, near)], 0)


def in_order(mine, sibling):
    c = place()[3]
    return jnp.where(c == 0, f32(mine), f32(sibling)), jnp.where(c == 0, f32(sibling), f32(mine))


def earlier_near(keep_gate, mine, sibling):
    first, second = in_order(mine, sibling)
    return half_across(low(keep_gate * first + second))


def earlier_sum(keep_gate, near, sibling, start):
    z, y, x, c = place()
    other = both_halves(near)
    before = jnp.where(x == 0, start, keep_gate * keep_gate * start + f32(other))
    return jnp.where(c == 0, before, keep_gate * before + f32(sibling))


def later_near(keep_gate, mine, sibling):
    first, second = in_order(mine, sibling)
    return half_across(low(first + keep_gate * second))


def later_sum(keep_gate, near, sibling):
    z, y, x, c = place()
    after = jnp.where(x == 0, f32(both_halves(near)), 0.0)
    return jnp.where(c == 0, f32(sibling) + keep_gate * after, after)


def from_behind(block, axis, distance):
    devices = range(lax.axis_size(axis))
    pairs = [(i - distance, i) for i in devices if i - distance in devices]
    return lax.ppermute(block, axis, pairs)


def entering(keep_gate, mine, reverse):
    devices, at_home = lax.axis_size("seq"), lax.axis_index("seq")
    everything = lax.all_gather(mine, "seq")

    def turn(k, before):
        at = devices - 1 - k if reverse else k
        reached = at > at_home if reverse else at < at_home
        gain, total = before
        return (
            jnp.where(reached, gain * keep_gate, gain),
            jnp.where(reached, keep_gate * total + f32(everything[at]), total),
        )

    start = (jnp.ones_like(keep_gate), jnp.zeros(mine.shape, jnp.float32))
    return lax.fori_loop(0, devices, turn, start)


def norm_scale(values):
    return lax.rsqrt(jnp.mean(values * values, -1, keepdims=True) + 1e-06)


def halves_of_columns(a):
    parts = a.reshape(a.shape[0], CHUNKS, 2, -1)
    return [parts[:, :, i].reshape(a.shape[0], -1) for i in range(2)]


def halves_of_rows(a, chunks):
    parts = a.reshape(chunks, 2, -1, a.shape[1])
    return [parts[:, i].reshape(-1, a.shape[1]) for i in range(2)]


def fold(a, rows):
    return a.reshape(-1, rows, D).transpose(1, 0, 2).reshape(rows, -1)


def unfold(a):
    rows = a.shape[0]
    return a.reshape(rows, -1, D).transpose(1, 0, 2).reshape(-1, D)


SCALE = HD ** (-0.5)


def dot(a, b, dims):
    return lax.dot_general(a, b, (dims, ((), ())), preferred_element_type=jnp.float32)


NN, NT, TN = ((1,), (0,)), ((1,), (1,)), ((0,), (0,))


def head_block(first):
    return pl.BlockSpec((BLK, HD), lambda h: (0, first + h))


def pair_block():
    return pl.BlockSpec((2, BLK, HD), lambda h: (0, 0, h))


def row_block():
    return pl.BlockSpec((1, 1, BLK), lambda h: (h, 0, 0))


def token_scores(q, k, kp, bias_row, is_first):
    row = lax.broadcasted_iota(jnp.int32, (BLK, BLK), 0)
    col = lax.broadcasted_iota(jnp.int32, (BLK, BLK), 1)
    own = row <= col
    bias = jnp.concatenate([bias_row] + [pltpu.roll(bias_row, i, 1) for i in range(1, 8)], 0)
    while bias.shape[0] < BLK:
        bias = jnp.concatenate([bias, pltpu.roll(bias, bias.shape[0], 1)], 0)
    raw = jnp.where(own, dot(k, q, NT), dot(kp, q, NT))
    scores = raw * SCALE + bias
    return jnp.where(own | jnp.logical_not(is_first), scores, -1e30), own


def attention_body(q, k, v, kp, vp, sk, sv, bias, mixed, lse):
    is_first = lax.axis_index("seq") == 0
    q = q[...]
    tokens, own = token_scores(q, k[...], kp[...], bias[0], is_first)
    states = dot(sk[...], q, NT) * SCALE
    top = jnp.maximum(jnp.max(tokens, 0, keepdims=True), jnp.max(states, 0, keepdims=True))
    tokens, states = jnp.exp(tokens - top), jnp.exp(states - top)
    total = jnp.sum(tokens, 0, keepdims=True) + jnp.sum(states, 0, keepdims=True)
    lse[0] = top + jnp.log(total)
    mix = dot(jnp.transpose(v[...]), low(jnp.where(own, tokens, 0.0)), NN)
    mix += dot(jnp.transpose(vp[...]), low(jnp.where(own, 0.0, tokens)), NN)
    mix += dot(jnp.transpose(sv[...]), low(states), NN)
    mixed[...] = low(jnp.transpose(mix * (1.0 / total)))


def attention(query, kv, prev, skv, bias):
    return pl.pallas_call(
        attention_body,
        grid=(HEADS,),
        in_specs=[head_block(0)]
        + [head_block(0), head_block(HEADS)] * 3
        + [row_block()],
        out_specs=[head_block(0), row_block()],
        out_shape=[
            jax.ShapeDtypeStruct((BLK, D), jnp.bfloat16),
            jax.ShapeDtypeStruct((HEADS, 1, BLK), jnp.float32),
        ],
        compiler_params=pltpu.CompilerParams(vmem_limit_bytes=40 * 2**20),
        cost_estimate=pl.CostEstimate(
            flops=12 * HEADS * BLK * BLK * HD,
            bytes_accessed=9 * 2**20,
            transcendentals=2 * HEADS * BLK * BLK,
        ),
        name="attention",
    )(query, kv, kv, prev, prev, skv, skv, bias)


def attention_back_body(
    q, k, v, kp, vp, sk, sv, bias, lse, go, gq, gkv, gprev, gstate, gbias
):
    is_first = lax.axis_index("seq") == 0
    q, k, kp, sk, go = q[...], k[...], kp[...], sk[...], go[...]
    tokens, own = token_scores(q, k, kp, bias[0], is_first)
    log_total = lse[0]
    tokens = jnp.exp(tokens - log_total)
    states = jnp.exp(dot(sk, q, NT) * SCALE - log_total)
    gtokens = jnp.where(own, dot(v[...], go, NT), dot(vp[...], go, NT))
    gstates = dot(sv[...], go, NT)
    mean = jnp.sum(tokens * gtokens, 0, keepdims=True) + jnp.sum(states * gstates, 0, keepdims=True)
    gkv[1] = dot(low(jnp.where(own, tokens, 0.0)), go, NN)
    gprev[1] = low(dot(low(jnp.where(own, 0.0, tokens)), go, NN))
    gstate[1] = low(dot(low(states), go, NN))
    gtokens = low(tokens * (gtokens - mean))
    gstates = low(states * (gstates - mean))
    wide = f32(gtokens)
    gown, gbefore = low(jnp.where(own, wide, 0.0)), low(jnp.where(own, 0.0, wide))
    gkv[0] = dot(gown, q, NN) * SCALE
    gprev[0] = low(dot(gbefore, q, NN) * SCALE)
    gstate[0] = low(dot(gstates, q, NN) * SCALE)
    g = dot(jnp.transpose(k), gown, NN)
    g += dot(jnp.transpose(kp), gbefore, NN)
    g += dot(jnp.transpose(sk), gstates, NN)
    gq[...] = low(jnp.transpose(g * SCALE))
    rows = BLK
    while rows > 1:
        rows //= 2
        wide = wide[:rows] + pltpu.roll(wide[rows:], BLK - rows, 1)
    gbias[0] = wide


def attention_back(query, kv, prev, skv, bias, lse, go):
    return pl.pallas_call(
        attention_back_body,
        grid=(HEADS,),
        in_specs=[head_block(0)]
        + [head_block(0), head_block(HEADS)] * 3
        + [row_block(), row_block(), head_block(0)],
        out_specs=[head_block(0), pair_block(), pair_block(), pair_block(), row_block()],
        out_shape=[
            jax.ShapeDtypeStruct((BLK, D), jnp.bfloat16),
            jax.ShapeDtypeStruct((2, BLK, D), jnp.float32),
            jax.ShapeDtypeStruct((2, BLK, D), jnp.bfloat16),
            jax.ShapeDtypeStruct((2, BLK, D), jnp.bfloat16),
            jax.ShapeDtypeStruct((HEADS, 1, BLK), jnp.float32),
        ],
        compiler_params=pltpu.CompilerParams(vmem_limit_bytes=48 * 2**20),
        cost_estimate=pl.CostEstimate(
            flops=30 * HEADS * BLK * BLK * HD,
            bytes_accessed=18 * 2**20,
            transcendentals=2 * HEADS * BLK * BLK,
        ),
        name="attention_back",
    )(query, kv, kv, prev, prev, skv, skv, bias, lse, go)


def query_block():
    return pl.BlockSpec((HD, NSTATE), lambda h: (h, 0))


def state_body(k, v, query, mixed, lse):
    scores = dot(k[...], query[...], NN) * SCALE
    top = jnp.max(scores, 0, keepdims=True)
    scores = jnp.exp(scores - top)
    total = jnp.sum(scores, 0, keepdims=True)
    lse[0] = top + jnp.log(total)
    mix = dot(jnp.transpose(v[...]), low(scores), NN)
    mixed[...] = low(jnp.transpose(mix * (1.0 / total)))


def state_attention(kv, query):
    return pl.pallas_call(
        state_body,
        grid=(HEADS,),
        in_specs=[head_block(0), head_block(HEADS), query_block()],
        out_specs=[head_block(0), row_block()],
        out_shape=[
            jax.ShapeDtypeStruct((NSTATE, D), jnp.bfloat16),
            jax.ShapeDtypeStruct((HEADS, 1, NSTATE), jnp.float32),
        ],
        compiler_params=pltpu.CompilerParams(vmem_limit_bytes=32 * 2**20),
        cost_estimate=pl.CostEstimate(
            flops=4 * HEADS * BLK * BLK * HD,
            bytes_accessed=4 * 2**20,
            transcendentals=HEADS * BLK * BLK,
        ),
        name="state_attention",
    )(kv, kv, query)


def state_back_body(k, v, query, lse, go, gkv, gsum, gquery):
    k, query, go = k[...], query[...], go[...]
    probs = jnp.exp(dot(k, query, NN) * SCALE - lse[0])
    gprobs = dot(v[...], go, NT)
    mean = jnp.sum(probs * gprobs, 0, keepdims=True)
    gsum[1] = dot(low(probs), go, NN) + gkv[1]
    gscores = low(probs * (gprobs - mean))
    gsum[0] = dot(gscores, query, NT) * SCALE + gkv[0]
    gquery[...] = low(dot(jnp.transpose(k), gscores, NN) * SCALE)


def state_attention_back(kv, query, lse, go, gkv):
    return pl.pallas_call(
        state_back_body,
        grid=(HEADS,),
        in_specs=[
            head_block(0),
            head_block(HEADS),
            query_block(),
            row_block(),
            head_block(0),
            pair_block(),
        ],
        out_specs=[pair_block(), query_block()],
        out_shape=[
            jax.ShapeDtypeStruct((2, BLK, D), jnp.float32),
            jax.ShapeDtypeStruct((D, NSTATE), jnp.bfloat16),
        ],
        compiler_params=pltpu.CompilerParams(vmem_limit_bytes=32 * 2**20),
        cost_estimate=pl.CostEstimate(
            flops=10 * HEADS * BLK * BLK * HD,
            bytes_accessed=14 * 2**20,
            transcendentals=HEADS * BLK * BLK,
        ),
        name="state_attention_back",
    )(kv, kv, query, lse, go, gkv)


STEP = 512
HALF = 2048
CHUNKS = 32


def owner_row(chip, swap):
    z, y, x = chip // 4, chip // 2 % 2, chip % 2
    return (x * 8 + y * 4 if swap else y * 8 + x * 4) + z


def gelu_parts(x):
    a, b = 0.7978845608028654, 0.044715
    square = x * x
    t = jnp.tanh(a * x * (1.0 + b * square))
    half = 0.5 * (1.0 + t)
    slope = half + (0.5 * a) * x * (1.0 - t * t) * (1.0 + 3.0 * b * square)
    return x * half, slope


def mlp_body(last, spot_of, alternate, *refs):
    hidden, og, rows, up_bias = refs[:4]
    ups, downs, refs = refs[4:12], refs[12:20], refs[20:]
    if last:
        out_in, u_in, keep, away, up_bias_grad, output, grad, branch, sums = refs[:9]
        up, down, xn, xs, out_acc, u_acc = refs[9:]
    else:
        keep, away, up_bias_grad, out_acc, u_acc = refs[:5]
        up, down, xn, xs = refs[5:]
    j = pl.program_id(0)
    spot = spot_of()
    core = spot[2]
    rk = D // CHUNKS
    hk = HALF // CHUNKS

    @pl.when(j == 0)
    def _():
        h = hidden[...]
        r = lax.rsqrt(jnp.mean(h * h, -1, keepdims=True) + 1e-06)
        n = low(h * r * rows[1:2, :])
        xn[...] = n
        nt = jnp.transpose(n)
        for i in range(CHUNKS):
            to = owner_row(i // 2, i % 2) * rk + lax.rem(i % 2 + core, 2) * (D // 2)
            xs[pl.ds(pl.multiple_of(to, rk), rk), :] = nt[i * rk : (i + 1) * rk]
        if last:
            out_acc[...] = out_in[...]
            u_acc[...] = u_in[...]
        else:
            out_acc[...] = jnp.zeros_like(out_acc)
            u_acc[...] = jnp.zeros_like(u_acc)

    for i in range(8):
        ty, tx, c = origin(i, spot, alternate)
        at = ty * 4 + tx * 2 + c
        for z in range(4):
            up[pl.ds(pl.multiple_of((z * 8 + at) * rk, rk), rk), :] = ups[i][z]
        for q in range(hk // rk):
            down[pl.ds(pl.multiple_of(at * hk + q * rk, rk), rk), :] = downs[i][
                0, :, q * D : (q + 1) * D
            ]
    up_w, down_w, g_out = up[...], down[...], og[...]
    act, slope = gelu_parts(dot(xn[...], up_w, NN) + up_bias[...])
    act = low(act)
    out_acc[...] += dot(act, down_w, NN)
    g_up = low(slope * dot(g_out, down_w, NT))
    up_bias_grad[...] = jnp.sum(f32(g_up), 0, keepdims=True)
    u_acc[...] += dot(g_up, up_w, NT)
    d_up = low(dot(xs[...], g_up, NN))
    at = pl.ds(pl.multiple_of(j * STEP, STEP), STEP)
    keep[:, at] = d_up[: D // 2]
    away[:, at] = d_up[D // 2 :]
    d_down = low(dot(jnp.transpose(act), g_out, NN))
    for i in range(STEP // hk // 2):
        even = d_down[2 * i * hk : (2 * i + 1) * hk]
        odd = d_down[(2 * i + 1) * hk : (2 * i + 2) * hk]
        mine, other = jnp.where(core == 0, even, odd), jnp.where(core == 0, odd, even)
        for q in range(hk // rk):
            cols = slice(HALF + q * D, HALF + (q + 1) * D)
            part = slice(q * rk, (q + 1) * rk)
            for out, value, owner in ((keep, mine, core), (away, other, 1 - core)):
                to = jnp.where(owner == 0, owner_row(i, 0), owner_row(i, 1)) + j
                out[pl.ds(pl.multiple_of(to * rk, rk), rk), cols] = value[part]

    if last:

        @pl.when(j == pl.num_programs(0) - 1)
        def _():
            h = hidden[...]
            output[...] = low(h + out_acc[...] + rows[3:4, :])
            r = lax.rsqrt(jnp.mean(h * h, -1, keepdims=True) + 1e-06)
            n = h * r
            u = u_acc[...]
            ug = u * rows[1:2, :]
            g = f32(og[...]) + r * (ug - n * jnp.mean(ug * n, -1, keepdims=True))
            grad[...] = g
            branch[...] = low(g)
            sums[0:1, :] = jnp.sum(u * n, 0, keepdims=True)
            sums[1:2, :] = jnp.sum(f32(og[...]), 0, keepdims=True)


def mlp_half(spot_of, alternate, hidden, og, rows, up_bias, parts, before):
    last = before is not None
    whole = lambda a, b: pl.BlockSpec((a, b), lambda j: (0, 0))
    tall = lambda a, b: pl.BlockSpec((a, b), lambda j: (0, 0), pipeline_mode=pl.Buffered(1))
    acc = jax.ShapeDtypeStruct((BLK, D), jnp.float32)
    lows = jax.ShapeDtypeStruct((BLK, D), jnp.bfloat16)
    width = 2 * HALF + (D if last else 0)
    grads = jax.ShapeDtypeStruct((D // 2, width), jnp.bfloat16)
    return pl.pallas_call(
        functools.partial(mlp_body, last, spot_of, alternate),
        grid=(HALF // STEP,),
        in_specs=[
            tall(BLK, D),
            tall(BLK, D),
            whole(8, D),
            pl.BlockSpec((1, STEP), lambda j: (0, j)),
        ]
        + [pl.BlockSpec((4, D // CHUNKS, STEP), lambda j: (0, 0, j))] * 8
        + [pl.BlockSpec((1, D // CHUNKS, HALF), lambda j: (j, 0, 1))] * 8
        + [tall(BLK, D)] * (2 if last else 0),
        out_specs=[tall(D // 2, 2 * HALF)] * 2
        + [pl.BlockSpec((1, STEP), lambda j: (0, j))]
        + ([tall(BLK, D)] * 3 + [whole(8, D)] if last else [tall(BLK, D)] * 2),
        out_shape=[grads, grads, jax.ShapeDtypeStruct((1, HALF), jnp.float32)]
        + (
            [lows, acc, lows, jax.ShapeDtypeStruct((8, D), jnp.float32)]
            if last
            else [acc, acc]
        ),
        scratch_shapes=[
            pltpu.VMEM((D, STEP), jnp.bfloat16),
            pltpu.VMEM((STEP, D), jnp.bfloat16),
            pltpu.VMEM((BLK, D), jnp.bfloat16),
            pltpu.VMEM((D, BLK), jnp.bfloat16),
        ]
        + ([pltpu.VMEM((BLK, D), jnp.float32)] * 2 if last else []),
        compiler_params=pltpu.CompilerParams(vmem_limit_bytes=58 * 2**20),
        cost_estimate=pl.CostEstimate(
            flops=12 * BLK * D * HALF, bytes_accessed=30 * 2**20, transcendentals=BLK * HALF
        ),
        name="mlp_half",
    )(hidden, og, rows, up_bias, *parts, *parts, *(before or ()))


def weight_grads_body(core_of, plan, columns, *refs):
    keep, away, split = refs[-3:]
    core = core_of()
    rk = D // CHUNKS

    def put(pairs, first):
        for chip, (even, odd) in enumerate(pairs):
            cols = slice(first, first + even.shape[1])
            mine, other = jnp.where(core == 0, even, odd), jnp.where(core == 0, odd, even)
            for out, value, owner in ((keep, mine, core), (away, other, 1 - core)):
                to = jnp.where(owner == 0, owner_row(chip, 0), owner_row(chip, 1))
                out[pl.ds(pl.multiple_of(to * rk, rk), rk), cols] = value

    for (kind, ins), first in zip(plan, columns):
        if kind == "dot":
            nt = jnp.transpose(refs[ins[0]][...])
            for i in range(CHUNKS):
                to = owner_row(i // 2, i % 2) * rk + lax.rem(i % 2 + core, 2) * (D // 2)
                split[pl.ds(pl.multiple_of(to, rk), rk), :] = nt[i * rk : (i + 1) * rk]
            for i in ins[1:]:
                width = refs[i].shape[-1]
                for s in range(0, width, 512):
                    n = min(512, width - s)
                    g = low(dot(split[...], refs[i][:, s : s + n], NN))
                    keep[:, first + s : first + s + n] = g[: D // 2]
                    away[:, first + s : first + s + n] = g[D // 2 :]
                first += width
        else:
            a = refs[ins[0]][...]
            if kind == "transposed":
                a = low(jnp.transpose(a))
            put(
                [
                    (a[i * rk : (i + 1) * rk], a[(i + 1) * rk : (i + 2) * rk])
                    for i in range(0, CHUNKS, 2)
                ],
                first,
            )


def weight_grads(core_of, plan):
    args, steps, columns, width, flops = [], [], [], 0, 0
    for kind, *arrays in plan:
        steps.append((kind, tuple(range(len(args), len(args) + len(arrays)))))
        args += arrays
        columns.append(width)
        if kind == "dot":
            n = sum(a.shape[1] for a in arrays[1:])
            flops += 2 * BLK * D * n
        else:
            n = arrays[0].shape[1 if kind == "rows" else 0]
        width += n
    return pl.pallas_call(
        functools.partial(weight_grads_body, core_of, steps, columns),
        out_shape=[jax.ShapeDtypeStruct((D // 2, width), jnp.bfloat16)] * 2,
        scratch_shapes=[pltpu.VMEM((D, BLK), jnp.bfloat16)],
        compiler_params=pltpu.CompilerParams(vmem_limit_bytes=48 * 2**20),
        cost_estimate=pl.CostEstimate(
            flops=flops, bytes_accessed=4 * D * width, transcendentals=0
        ),
        name="weight_grads",
    )(*args)


def natural(keep, away):
    parts = [a.reshape(2, 2, 4, -1, a.shape[1]).transpose(2, 0, 1, 3, 4) for a in (keep, away)]
    parts[1] = parts[1].transpose(0, 2, 1, 3, 4)
    return jnp.stack(parts, 3).reshape(-1, keep.shape[1])


def out_weight_grad(core_of, mixed, branch, keep, away):
    def body(x, g, keep_in, away_in, keep_out, away_out, split):
        weight_grads_body(
            core_of, [("dot", (0, 1))], [0], x, g, keep_out, away_out, split
        )

    whole = pl.BlockSpec((BLK, D), lambda i: (0, 0))
    here = pl.BlockSpec(memory_space=pl.ANY)
    last = pl.BlockSpec((D // 2, D), lambda i: (0, keep.shape[1] // D - 1))
    return pl.pallas_call(
        body,
        grid=(1,),
        in_specs=[whole, whole, here, here],
        out_specs=[last, last],
        out_shape=[jax.ShapeDtypeStruct(keep.shape, keep.dtype)] * 2,
        input_output_aliases={2: 0, 3: 1},
        scratch_shapes=[pltpu.VMEM((D, BLK), jnp.bfloat16)],
        compiler_params=pltpu.CompilerParams(vmem_limit_bytes=32 * 2**20),
        cost_estimate=pl.CostEstimate(
            flops=2 * BLK * D * D, bytes_accessed=4 * 2**20, transcendentals=0
        ),
        name="out_weight_grad",
    )(mixed, branch, keep, away)


def pack_first(attn_gain, mlp_gain, gate, down_bias, up_bias, *matrices):
    rows = matrices[0].shape[0]
    vectors = [v.reshape(1, -1) for v in (attn_gain, mlp_gain, gate, down_bias, up_bias)]

    def body(a, m, g, d, u, table, *rest):
        out = rest[-1]
        up = f32(u[...])
        column = [f32(v[...]) for v in (a, m, g, d)]
        column += [up[:, i : i + rows] for i in range(0, up.shape[1], rows)]
        column = jnp.transpose(jnp.concatenate(column, 0))
        column = jnp.concatenate(
            [column, jnp.zeros((rows, VEC - column.shape[1]), jnp.float32)], 1
        )
        first = 0
        for part in [table[...], low(column)] + [r[...] for r in rest[:-1]]:
            out[:, first : first + part.shape[1]] = part
            first += part.shape[1]

    return pl.pallas_call(
        body,
        out_shape=jax.ShapeDtypeStruct((rows, VEC + sum(m.shape[1] for m in matrices)), jnp.bfloat16),
        name="pack_first",
    )(*vectors, *matrices)


def pack_rest(query, sinit, skey, svalue, out_weight, up, down):
    rows = query.shape[0]
    half = down.shape[0] // 2

    def body(r, s, k, w, o, up, down, second, third, fourth):
        first = 0
        for part in (r, s, k, w, o):
            second[:, first : first + part.shape[1]] = part[...]
            first += part.shape[1]
        lane = lax.broadcasted_iota(jnp.int32, (rows, 128), 1) < 64
        for i in range(0, CHUNKS, 2):
            a = f32(up[:, i * 128 : (i + 1) * 128])
            b = f32(up[:, (i + 1) * 128 : (i + 2) * 128])
            at = slice(i * 64, i * 64 + 128)
            third[:, at] = low(jnp.where(lane, a, pltpu.roll(b, 64, 1)))
            fourth[:, at] = low(jnp.where(lane, pltpu.roll(a, 64, 1), b))
        for i, out in enumerate((third, fourth)):
            for q in range(half // rows):
                start = i * half + q * rows
                out[:, HALF + q * D : HALF + (q + 1) * D] = down[start : start + rows, :]

    return pl.pallas_call(
        body,
        out_shape=[
            jax.ShapeDtypeStruct((rows, NSTATE + 4 * D), jnp.bfloat16),
            jax.ShapeDtypeStruct((rows, 2 * HALF), jnp.bfloat16),
            jax.ShapeDtypeStruct((rows, 2 * HALF), jnp.bfloat16),
        ],
        name="pack_rest",
    )(query, sinit, skey, svalue, out_weight, up, down)


def readout(gstate, skv_full):
    def body(g, w, read, sent):
        r = dot(g[0], w[:, :D], NT) + dot(g[1], w[:, D:], NT)
        read[...] = r
        sent[...] = low(r)

    return pl.pallas_call(
        body,
        out_shape=[
            jax.ShapeDtypeStruct((NSTATE, D), jnp.float32),
            jax.ShapeDtypeStruct((NSTATE, D), jnp.bfloat16),
        ],
        compiler_params=pltpu.CompilerParams(vmem_limit_bytes=32 * 2**20),
        cost_estimate=pl.CostEstimate(
            flops=4 * NSTATE * D * D, bytes_accessed=9 * 2**20, transcendentals=0
        ),
        name="readout",
    )(gstate, skv_full)


def embedding_back(gq, gk, gv, query_full, kv_full, embedded, grad_hidden, rows):
    def body(q, k, v, wq, w, e, g_out, r, grad, lowered, gain_grad):
        g = dot(q[...], wq[...], NT) + dot(k[...], w[:, :D], NT) + dot(v[...], w[:, D:], NT)
        emb = e[...]
        scale = lax.rsqrt(jnp.mean(emb * emb, -1, keepdims=True) + 1e-06)
        normed = emb * scale
        gain_grad[...] = jnp.broadcast_to(jnp.sum(g * normed, 0, keepdims=True), gain_grad.shape)
        g = g * r[0:1, :]
        g = g_out[...] + scale * (g - normed * jnp.mean(g * normed, -1, keepdims=True))
        grad[...] = g
        lowered[...] = low(g)

    return pl.pallas_call(
        body,
        out_shape=[
            jax.ShapeDtypeStruct((BLK, D), jnp.float32),
            jax.ShapeDtypeStruct((BLK, D), jnp.bfloat16),
            jax.ShapeDtypeStruct((8, D), jnp.float32),
        ],
        compiler_params=pltpu.CompilerParams(vmem_limit_bytes=48 * 2**20),
        cost_estimate=pl.CostEstimate(
            flops=6 * BLK * D * D, bytes_accessed=18 * 2**20, transcendentals=0
        ),
        name="embedding_back",
    )(gq, gk, gv, query_full, kv_full, embedded, grad_hidden, rows)


def layer(
    fast,
    char_ids,
    char_table,
    attn_gain,
    query_weight,
    key_weight,
    value_weight,
    out_weight,
    state_key_weight,
    state_value_weight,
    update_weight,
    state_query,
    state_init,
    gate_bias,
    position_table,
    mlp_gain,
    up_weight,
    up_bias,
    down_weight,
    down_bias,
    out_grad,
):
    rows = attn_gain.shape[0]
    ff = up_weight.shape[1]
    folds = ff // D
    main = VOCAB + VEC
    spot_of = here if fast else (lambda: (jnp.int32(0),) * 3)
    core_of = core_index if fast else (lambda: jnp.int32(0))
    layouts = (
        ((0, main, 1), (main, 2 * D, 1), (main + 2 * D, NSTATE, 1), (main + 2 * D + NSTATE, D, 1)),
        ((0, D, 1), (D, NSTATE, 1), (D + NSTATE, 2 * D, 1), (D + NSTATE + 2 * D, D, 1)),
    )
    if fast:
        shard1 = pack_first(
            attn_gain,
            mlp_gain,
            gate_bias,
            down_bias,
            up_bias,
            char_table,
            key_weight,
            value_weight,
            state_query,
            update_weight,
        )
        z1 = along_z(shard1)
        shard2, shard3, shard4 = pack_rest(
            query_weight,
            state_init,
            state_key_weight,
            state_value_weight,
            out_weight,
            up_weight,
            down_weight,
        )
        z1[:3], shard2, shard3, shard4 = join(z1[:3], shard2, shard3, shard4)
        p1 = stack_z(shard1, *z1)
        shard2 = tie(shard2, p1)
        z2 = along_z(shard2)
        sides1, z2[:3] = join(to_sides(p1), z2[:3])
        shard3, p2 = join(shard3, stack_z(shard2, *z2))
        corner1, near3 = join(to_corner(p1, sides1), send(shard3, Z_NEAR))
        z3, sides2 = far_z(shard3, near3), to_sides(p2, X_ROUTE, Y_ROUTE)
        table_vec, kv_full, squery_full, update_full = assemble(
            pieces(p1, sides1, corner1, last_corner(corner1)), layouts[0], True
        )
    else:
        vectors = jnp.concatenate([attn_gain, mlp_gain, gate_bias, down_bias, up_bias])
        vectors = vectors.reshape(4 + folds, rows)
        columns = jnp.pad(jnp.transpose(vectors), ((0, 0), (0, VEC - vectors.shape[0])))
        table_vec, kv_full, squery_full, update_full = gather_any(
            jnp.concatenate(
                [char_table, columns, key_weight, value_weight, state_query, update_weight], 1
            ),
            layouts[0],
        )

    vector_rows = jnp.transpose(f32(table_vec[:, VOCAB : VOCAB + 4 + folds]))
    biases = halves_of_columns(
        vector_rows[4:].reshape(folds, -1, rows).transpose(1, 0, 2).reshape(1, ff)
    )
    keep_gate = jax.nn.sigmoid(vector_rows[2])
    is_first = lax.axis_index("seq") == 0
    bias_rows = f32(position_table)[:, None, :]

    one_hot = (char_ids[:, None] == jnp.arange(VOCAB)[None, :]).astype(jnp.bfloat16)
    embedded = dot(one_hot, table_vec[:, :VOCAB], NT)
    normed_low = low(embedded * norm_scale(embedded) * vector_rows[0])
    kv = low(dot(normed_low, kv_full, NN))
    state_mix, state_lse = state_attention(kv, squery_full)
    update = dot(state_mix, update_full, NN)
    mine = low((1.0 - keep_gate) * update)
    if fast:
        sides2, z3[:3], mine = join(sides2, z3[:3], mine)
        sibling = send(mine, CORE_ROUTE)
        near = earlier_near(keep_gate, mine, sibling)
        prev = from_behind(tie(kv, mine), "seq", 1)
        corner2 = to_corner(p2, sides2, Y_ROUTE)
        near, corner2, prev, near4, p3 = join(
            near, corner2, prev, send(tie(shard4, mine), Z_NEAR), stack_z(shard3, *z3)
        )
        sides3, z4 = to_sides(p3), far_z(shard4, near4)
        query_full, sinit_full, skv_full, out_full = assemble(
            pieces(p2, sides2, corner2, last_corner(corner2)), layouts[1], False
        )
    else:
        prev = from_behind(kv, "seq", 1)
        query_full, sinit_full, skv_full, out_full = gather_any(
            jnp.concatenate(
                [query_weight, state_init, state_key_weight, state_value_weight, out_weight], 1
            ),
            layouts[1],
        )
    query = low(dot(normed_low, query_full, NN))
    start = f32(join(jnp.transpose(sinit_full))[0])
    if fast:
        state_prev = earlier_sum(keep_gate, near, sibling, start)
    else:
        gain, total = entering(keep_gate, mine, False)
        state_prev = gain * start + total
    state_low = low(state_prev)
    skv = low(dot(state_low, skv_full, NN))
    if fast:
        skv, query, sides3, z4[:3] = join(skv, query, sides3, z4[:3])
        corner3, p4 = to_corner(p3, sides3), stack_z(shard4, *z4)
    mixed, lse = attention(query, kv, prev, skv, bias_rows)
    hidden = embedded + dot(mixed, out_full, NN)

    if fast:
        corner3, hidden, p4 = join(corner3, hidden, p4)
        sides4 = to_sides(p4)
        parts = pieces(p3, sides3, corner3, last_corner(corner3))
        keep_a, away_a, bias_a, *before = mlp_half(
            spot_of, True, hidden, out_grad, vector_rows, biases[0], parts, None
        )
        sides4, away_a, before = join(sides4, away_a, before)
        corner4, got_a = join(to_corner(p4, sides4), to_core(away_a))
        parts = pieces(p4, sides4, corner4, last_corner(corner4))
        first_a = over_first(keep_a, got_a)
        keep_b, away_b, bias_b, *before = mlp_half(
            spot_of, True, hidden, out_grad, vector_rows, biases[1], parts, before
        )
        first_a, away_b, before = join(first_a, away_b, before)
    else:
        shard = jnp.concatenate([up_weight, fold(down_weight, rows)], 1)
        up_full, down_full = gather_any(shard, ((0, ff, 1), (ff, D, folds)))
        halves = []
        for up, down in zip(halves_of_columns(up_full), halves_of_rows(down_full, CHUNKS)):
            down = down.reshape(CHUNKS, 2, -1, D).transpose(0, 2, 1, 3).reshape(D, HALF)
            both = jnp.concatenate([up, down], 1).reshape(4, 2, 2, 2, -1, 2 * HALF)
            halves.append([both[:, i // 2 % 2, i % 2, i // 4] for i in range(8)])
        keep_a, away_a, bias_a, *before = mlp_half(
            spot_of, False, hidden, out_grad, vector_rows, biases[0], halves[0], None
        )
        keep_b, away_b, bias_b, *before = mlp_half(
            spot_of, False, hidden, out_grad, vector_rows, biases[1], halves[1], before
        )
    output, grad_hidden, grad_branch, mlp_sums = before

    keep_b, away_b = out_weight_grad(core_of, mixed, grad_branch, keep_b, away_b)
    grad_mixed = low(dot(grad_branch, out_full, NT))
    if fast:
        got_b, grad_mixed = join(to_core(away_b), grad_mixed)
        second_a = over_second(keep_a, got_a, first_a)
        corner_b = over_first_in_two(keep_b, got_b, True)
    gq, gkv, gprev, gstate, gbias = attention_back(
        query, kv, prev, skv, bias_rows, lse, grad_mixed
    )
    gbias = gbias.reshape(HEADS, BLK)
    if fast:
        second_a, corner_b, gprev, gstate = join(second_a, corner_b, gprev, gstate)
        side_b = over_first_in_two(keep_b, got_b, False)
    read, sent = readout(gstate, skv_full)
    if fast:
        sibling, gbias = send(sent, CORE_ROUTE), exchange(gbias, CORE_ROUTE)
        near = later_near(keep_gate, sent, sibling)
    first = weight_grads(
        core_of, [("dot", state_low, gstate[0], gstate[1]), ("dot", normed_low, gq)]
    )
    if fast:
        near, side_b, first, gbias = join(near, side_b, first, gbias)
        first_b = (corner_b, side_b)
        gnext = from_behind(tie(gprev, near), "seq", -1)
        pair_a = over_pairs(keep_a, got_a, first_a, second_a)
        got_c = to_core(first[1])
        gbias = exchange(gbias, X_ROUTE)
        after = later_sum(keep_gate, near, sibling)
    else:
        gnext = from_behind(gprev, "seq", -1)
        after = entering(keep_gate, sent, True)[1]
    grad_update = low((1.0 - keep_gate) * after)
    grad_smix = low(dot(grad_update, update_full, NT))
    if fast:
        grad_smix, second_b = join(grad_smix, over_second(keep_b, got_b, first_b))
    gsum, gquery = state_attention_back(kv, squery_full, state_lse, grad_smix, gkv)
    if fast:
        gsum, after = join(gsum, after)
    state_init_grad = jnp.where(is_first, read + keep_gate * after, 0.0)
    second = weight_grads(
        core_of,
        [
            ("dot", state_mix, grad_update),
            ("rows", gquery),
            ("transposed", state_init_grad),
        ],
    )
    if fast:
        gnext, pair_a, got_c, second, gbias = join(gnext, pair_a, got_c, second, gbias)
        first_c = over_first(first[0], got_c)
        pair_b = over_pairs(keep_b, got_b, first_b, second_b)
        got_d = to_core(second[1])
        gbias = exchange(gbias, Y_ROUTE)
    gk, gv = (low(gsum[i] + f32(gnext[i])) for i in range(2))
    key_grads = weight_grads(core_of, [("dot", normed_low, gk, gv)])
    if fast:
        gk, got_e = tie((gk, key_grads[1]), key_grads[0])
        got_e = to_core(got_e)
    embedded_grad, embedded_low, gain_grad = embedding_back(
        gq, gk, gv, query_full, kv_full, embedded, grad_hidden, vector_rows
    )
    if fast:
        first_c, got_d, got_e, embedded_low, gbias = join(
            first_c, got_d, got_e, embedded_low, gbias
        )
        second_c = over_second(first[0], got_c, first_c)
        first_d, first_e = over_first(second[0], got_d), over_first(key_grads[0], got_e)
        position_table_grad = exchange(exchange(gbias, Z_NEAR), Z_FAR)
        after, mlp_sums, bias_a, bias_b = join(after, mlp_sums, bias_a, bias_b, gain_grad)[:4]
    else:
        position_table_grad = lax.psum(gbias, AX)
    gate_bias_grad = jnp.sum(after * (state_prev - update), 0) * keep_gate * (1.0 - keep_gate)
    up_bias_grad = jnp.concatenate([b.reshape(CHUNKS, -1) for b in (bias_a, bias_b)], 1)
    vector_grads = jnp.concatenate(
        [gain_grad[:1], mlp_sums[:1], gate_bias_grad[None], mlp_sums[1:2]]
        + [up_bias_grad.reshape(-1, folds, rows).transpose(1, 0, 2).reshape(folds, D)]
        + [jnp.zeros((VEC - 4 - folds, D), jnp.float32)],
        0,
    )
    last = weight_grads(
        core_of, [("dot", embedded_low, one_hot), ("transposed", vector_grads)]
    )
    if fast:
        second_c, first_d, first_e, pair_b, got_f, position_table_grad = join(
            second_c, first_d, first_e, pair_b, to_core(last[1]), position_table_grad
        )
        second_d = over_second(second[0], got_d, first_d)
        second_e = over_second(key_grads[0], got_e, first_e)
        first_f = over_first(last[0], got_f)
        pair_c = over_pairs(first[0], got_c, first_c, second_c)
        end_b = within_pair(*pair_b)
        second_d, second_e, first_f, pair_c, end_b = join(
            second_d, second_e, first_f, pair_c, end_b
        )
        end_e = over_z(key_grads[0], got_e, first_e, second_e)
        second_f = over_second(last[0], got_f, first_f)
        pair_d = over_pairs(second[0], got_d, first_d, second_d)
        end_e, second_f, pair_d = join(end_e, second_f, pair_d)
        end_f = over_z(last[0], got_f, first_f, second_f)
        end_c, end_d = within_pair(*pair_c), within_pair(*pair_d)
        end_a = within_pair(*pair_a)
        sums = [finish(s) for s in (end_a, end_b, end_c, end_d, end_e, end_f)]
        up_sum = jnp.concatenate([s[:, :HALF].reshape(rows, CHUNKS, -1) for s in sums[:2]], 2)
        up_sum = up_sum.reshape(rows, ff)
        down_sum = jnp.concatenate([unfold(s[:, HALF : 2 * HALF]) for s in sums[:2]], 0)
        out_sum = sums[1][:, 2 * HALF :]
        first, second, key_sum, last = sums[2:]
    else:
        pairs = [natural(keep_a, away_a), natural(keep_b, away_b)]
        out_sum = scatter_any(pairs[1][:, 2 * HALF :])
        up_sum = jnp.concatenate([s[:, :HALF].reshape(D, CHUNKS, -1) for s in pairs], 2)
        up_sum = scatter_any(up_sum.reshape(D, ff))
        down_sum = jnp.concatenate(
            [
                s[:, HALF : 2 * HALF].reshape(CHUNKS, D // CHUNKS, -1, D).transpose(0, 2, 1, 3)
                for s in pairs
            ],
            1,
        )
        down_sum = scatter_any(down_sum.reshape(ff, D))
        first, second, key_sum, last = (
            scatter_any(natural(*s)) for s in (first, second, key_grads, last)
        )
    vector_sum = last[:, VOCAB:]
    return (
        output,
        embedded_grad,
        last[:, :VOCAB],
        vector_sum[:, 0],
        first[:, 2 * D :],
        key_sum[:, :D],
        key_sum[:, D:],
        out_sum,
        first[:, :D],
        first[:, D : 2 * D],
        second[:, :D],
        second[:, D : D + NSTATE],
        second[:, D + NSTATE :],
        vector_sum[:, 2],
        position_table_grad,
        vector_sum[:, 1],
        up_sum,
        jnp.transpose(vector_sum[:, 4 : 4 + folds]).reshape(-1),
        down_sum,
        vector_sum[:, 3],
    )


def solution(mesh):
    fast = dict(mesh.shape) == {"dp": 8, "seq": 4}
    return jax.shard_map(
        functools.partial(layer, fast),
        mesh=mesh,
        in_specs=(
            P(("dp", "seq")),
            P(("dp", "seq"), None),
            P(("dp", "seq")),
            P(("dp", "seq"), None),
            P(("dp", "seq"), None),
            P(("dp", "seq"), None),
            P(("dp", "seq"), None),
            P(("dp", "seq"), None),
            P(("dp", "seq"), None),
            P(("dp", "seq"), None),
            P(("dp", "seq"), None),
            P(("dp", "seq"), None),
            P(("dp", "seq")),
            P(),
            P(("dp", "seq")),
            P(("dp", "seq"), None),
            P(("dp", "seq")),
            P(("dp", "seq"), None),
            P(("dp", "seq")),
            P(("dp", "seq"), None),
        ),
        out_specs=(
            P(("dp", "seq"), None),
            P(("dp", "seq"), None),
            P(("dp", "seq"), None),
            P(("dp", "seq")),
            P(("dp", "seq"), None),
            P(("dp", "seq"), None),
            P(("dp", "seq"), None),
            P(("dp", "seq"), None),
            P(("dp", "seq"), None),
            P(("dp", "seq"), None),
            P(("dp", "seq"), None),
            P(("dp", "seq"), None),
            P(("dp", "seq"), None),
            P(("dp", "seq")),
            P(),
            P(("dp", "seq")),
            P(("dp", "seq"), None),
            P(("dp", "seq")),
            P(("dp", "seq"), None),
            P(("dp", "seq")),
        ),
        check_vma=False,
    )
```

time: 634 us -> 558 us (0.88)
  waiting for transfers between devices: 169 us -> 149 us
  local copies, waits for them, and re-layouts: 70 us -> 51.3 us
  matrix products: 37.7 us -> 20.6 us
  starting transfers between devices: 115 us -> 101 us
  between operations: 16 us -> 2.38 us
    ppermute x81 -> x84, waiting for transfers between devices: 169 us -> 149 us  [send(): return lax.ppermute(v, AX, pairs)]
    pallas_call x5 -> x10, Pallas kernels: 81.1 us -> 100 us  [the longest x2 50.4 us: mlp_half(): pl.pallas_call(functools.partial(mlp_body, last, spot_of, alternate), gri...]
    dot_general x12 -> x8, matrix products: 37.7 us -> 20.6 us  [dot(): lax.dot_general(a, b, (dims, ((), ())), preferred_element_type=jnp.float32)]
    ppermute x81 -> x84, starting transfers between devices: 111 us -> 96.9 us  [send(): return lax.ppermute(v, AX, pairs)]
    pallas_call x4 -> x2, Pallas kernels: 22.1 us -> 11.6 us  [assemble(): pl.pallas_call(body, out_shape=[jax.ShapeDtypeStruct((4, 2, 2, 2, rows *...]
    reshape x13 -> x4, local copies, waits for them, and re-layouts: 9.34 us -> 0.83 us  [the longest x1 0.6 us: layer(): jnp.transpose(vector_sum[:, 4:4 + folds]).reshape(-1)]
    convert_element_type x16 -> x22, other arithmetic: 34.9 us -> 41.1 us  [low(): return v.astype(jnp.bfloat16)]
    pallas_call x3 -> x4, Pallas kernels: 18.3 us -> 16 us  [weight_grads(): pl.pallas_call(functools.partial(weight_grads_body, core_of, steps, colum...]
  transfers between devices with their start and end apart: 84 -> 86, of which waited for: 28 -> 24; matrix products, arithmetic and copies ran while one was open for 19% -> 18% of each run, Pallas kernels for 23% -> 28%
where the time goes in v3:
time: 558 us; the launch traced here: 550 us
  Pallas kernels  160 us (29%)
  waiting for transfers between devices  149 us (27%)
  starting transfers between devices  101 us (18%)
  other arithmetic  66.4 us (12%)
  local copies, waits for them, and re-layouts  51.3 us (9%)
  matrix products  20.6 us (4%)
    ppermute x84, waiting for transfers between devices, send(): return lax.ppermute(v, AX, pairs)  149 us
    ppermute x84, starting transfers between devices, send(): return lax.ppermute(v, AX, pairs)  96.9 us
    pallas_call x2, Pallas kernels, mlp_half(): pl.pallas_call(functools.partial(mlp_body, last, spot_of, alternate), gri...  50.4 us
    convert_element_type x22, other arithmetic, low(): return v.astype(jnp.bfloat16)  41.1 us
    unnamed x161, local copies, waits for them, and re-layouts  27.7 us
    pallas_call x1, Pallas kernels, attention_back(): pl.pallas_call(attention_back_body, grid=(HEADS,), in_specs=[head_block(0...  22.8 us
    dot_general x8, matrix products, dot(): lax.dot_general(a, b, (dims, ((), ())), preferred_element_type=jnp.float32)  20.6 us
    pallas_call x4, Pallas kernels, weight_grads(): pl.pallas_call(functools.partial(weight_grads_body, core_of, steps, colum...  16 us
  transfers between devices with their start and end apart: 86, of which 24 were waited for; matrix products, arithmetic and copies ran while one was open for 18% of the time, Pallas kernels for 28%

profile of v3, /device:TPU:0, one launch (start us, length us, event | category | flops | bytes accessed | tf_op | source)
XLA Modules:
  0.0 550.4 jit_solution(491855441837302806)
XLA Ops:
  14.9 10.0 %collective-permute-done.1.refs_2_ = bf16[32,3968]{1,0:T(8,128)(2,1)S(1)} collective-permute-done((bf16[32,3968]{1,0:T(8,128)(2,1)}, bf16[32,3968]{1,0:T(8,128)(2,1)S(1)}, u32[]{:S(2)}, u32[]{:S(2)}) %collective-permute-start.1) | collective-permute-done | bytes 253984 | tf_op jit(solution)/shard_map/ppermute | solution.py:55
  31.1 5.8 %collective-permute-start.5 = (bf16[32,4608]{1,0:T(8,128)(2,1)}, bf16[32,4608]{1,0:T(8,128)(2,1)S(1)}, u32[]{:S(2)}, u32[]{:S(2)}) collective-permute-start(bf16[32,4608]{1,0:T(8,128)(2,1)} %get-tuple-element.196.refs_0_), channel_id=1, source_target_pairs={{0,8},{1,9},{2,10},{3,11},{4,12},{5,13},{6,14},{7,15},{8,16},{9,17... | collective-permute-start | bytes 884744 | tf_op jit(solution)/shard_map/ppermute | solution.py:55
  39.3 7.0 %collective-permute-done.5.refs_1_ = bf16[32,4608]{1,0:T(8,128)(2,1)S(1)} collective-permute-done((bf16[32,4608]{1,0:T(8,128)(2,1)}, bf16[32,4608]{1,0:T(8,128)(2,1)S(1)}, u32[]{:S(2)}, u32[]{:S(2)}) %collective-permute-start.5) | collective-permute-done | bytes 294944 | tf_op jit(solution)/shard_map/ppermute | solution.py:55
  46.3 10.3 %collective-permute-done.6.refs_2_ = bf16[32,4608]{1,0:T(8,128)(2,1)S(1)} collective-permute-done((bf16[32,4608]{1,0:T(8,128)(2,1)}, bf16[32,4608]{1,0:T(8,128)(2,1)S(1)}, u32[]{:S(2)}, u32[]{:S(2)}) %collective-permute-start.6) | collective-permute-done | bytes 294944 | tf_op jit(solution)/shard_map/ppermute | solution.py:55
  60.2 6.7 %collective-permute-start.14 = (bf16[32,4096]{1,0:T(8,128)(2,1)}, bf16[32,4096]{1,0:T(8,128)(2,1)}, u32[]{:S(2)}, u32[]{:S(2)}) collective-permute-start(bf16[32,4096]{1,0:T(8,128)(2,1)} %get-tuple-element.203.refs_0_), channel_id=1, source_target_pairs={{0,8},{1,9},{2,10},{3,11},{4,12},{5,13},{6,14},{7,15},{8,0},{9,1},... | collective-permute-start | bytes 786440 | tf_op jit(solution)/shard_map/ppermute | solution.py:55
  66.9 6.9 %collective-permute-done.14.refs_1_ = bf16[32,4096]{1,0:T(8,128)(2,1)} collective-permute-done((bf16[32,4096]{1,0:T(8,128)(2,1)}, bf16[32,4096]{1,0:T(8,128)(2,1)}, u32[]{:S(2)}, u32[]{:S(2)}) %collective-permute-start.14) | collective-permute-done | bytes 262176 | tf_op jit(solution)/shard_map/ppermute | solution.py:55
  93.6 7.0 %state_attention.1 = (bf16[512,1024]{1,0:T(8,128)(2,1)S(1)}, f32[8,1,512]{2,1,0:T(1,128)S(1)}) custom-call(bf16[512,2048]{1,0:T(8,128)(2,1)S(1)} %convolution_convert_fusion.1.k.v, bf16[512,2048]{1,0:T(8,128)(2,1)S(1)} %convolution_convert_fusion.1.k.v, bf16[1024,512]{1,0:T(8,128)(2,1)S(1)} %bitcast.201), custom_call_target="tpu_custom_call" | custom-call | flops 1073741824 | bytes 4194304 | tf_op jit(solution)/shard_map/state_attention/pallas_call | solution.py:486
  124.6 10.4 %collective-permute-done.20.refs_3_ = bf16[4,32,4608]{2,1,0:T(8,128)(2,1)} collective-permute-done((bf16[4,32,4608]{2,1,0:T(8,128)(2,1)}, bf16[4,32,4608]{2,1,0:T(8,128)(2,1)}, u32[]{:S(2)}, u32[]{:S(2)}) %collective-permute-start.20) | collective-permute-done | bytes 1179680 | tf_op jit(solution)/shard_map/ppermute | solution.py:55
  150.1 6.5 %assemble.3 = (bf16[4,2,2,2,32,1024]{5,4,3,2,1,0:T(8,128)(2,1)S(1)}, bf16[4,2,2,2,32,512]{5,4,3,2,1,0:T(8,128)(2,1)S(1)}, bf16[4,2,2,2,32,2048]{5,4,3,2,1,0:T(8,128)(2,1)}, bf16[4,2,2,2,32,1024]{5,4,3,2,1,0:T(8,128)(2,1)}) custom-call(bf16[4,32,4608]{2,1,0:T(8,128)(2,1)S(1)} %copy-done.6, bf16[4,32,4608]{2,1,0:T(8,128)(2,1)} %collective-permute-done.8.refs_1_, ...), custom_call_target="tpu_custom_call" | custom-call | tf_op jit(solution)/shard_map/assemble/pallas_call | solution.py:110
  177.3 14.0 %attention.1 = (bf16[512,1024]{1,0:T(8,128)(2,1)S(1)}, f32[8,1,512]{2,1,0:T(1,128)S(1)}) custom-call(bf16[512,1024]{1,0:T(8,128)(2,1)S(1)} %copy-done.31, bf16[512,2048]{1,0:T(8,128)(2,1)S(1)} %convolution_convert_fusion.1.k.v, bf16[512,2048]{1,0:T(8,128)(2,1)S(1)} %convolution_convert_fusion.1.k.v, bf16[512,2048]{1,0:T(8,128)(2,1)} %collective-permute-done.24.kp.vp, ...), custom_call_target="tpu_custom_call" | custom-call | flops 3221225472 | bytes 9437184 | tf_op jit(solution)/shard_map/attention/pallas_call | solution.py:392
  198.1 24.1 %mlp_half.2 = (bf16[512,4096]{1,0:T(8,128)(2,1)}, bf16[512,4096]{1,0:T(8,128)(2,1)}, f32[1,2048]{1,0:T(1,128)}, f32[512,1024]{1,0:T(8,128)}, f32[512,1024]{1,0:T(8,128)}) custom-call(f32[512,1024]{1,0:T(8,128)} %convolution_add_fusion.refs_0_, bf16[512,1024]{1,0:T(8,128)(2,1)} %refs_1_.3, f32[8,1024]{1,0:T(8,128)} %copy-done.35, ...), custom_call_target="tpu_custom_call" | custom-call | flops 12884901888 | bytes 31457280 | tf_op jit(solution)/shard_map/mlp_half/pallas_call | solution.py:651
  223.8 7.4 %collective-permute-done.40.refs_8_.refs_16_ = bf16[4,32,4096]{2,1,0:T(8,128)(2,1)} collective-permute-done((bf16[4,32,4096]{2,1,0:T(8,128)(2,1)S(1)}, bf16[4,32,4096]{2,1,0:T(8,128)(2,1)}, u32[]{:S(2)}, u32[]{:S(2)}) %collective-permute-start.40) | collective-permute-done | bytes 1048608 | tf_op jit(solution)/shard_map/ppermute | solution.py:55
  231.2 6.5 %collective-permute-done.39.refs_7_.refs_15_ = bf16[4,32,4096]{2,1,0:T(8,128)(2,1)} collective-permute-done((bf16[4,32,4096]{2,1,0:T(8,128)(2,1)S(1)}, bf16[4,32,4096]{2,1,0:T(8,128)(2,1)}, u32[]{:S(2)}, u32[]{:S(2)}) %collective-permute-start.39) | collective-permute-done | bytes 1048608 | tf_op jit(solution)/shard_map/ppermute | solution.py:55
  242.0 26.3 %mlp_half.3 = (bf16[512,5120]{1,0:T(8,128)(2,1)}, bf16[512,5120]{1,0:T(8,128)(2,1)}, f32[1,2048]{1,0:T(1,128)}, bf16[512,1024]{1,0:T(8,128)(2,1)}, f32[512,1024]...) custom-call(f32[512,1024]{1,0:T(8,128)} %convolution_add_fusion.refs_0_, bf16[512,1024]{1,0:T(8,128)(2,1)} %refs_1_.3, ...), custom_call_target="tpu_custom_call" | custom-call | flops 12884901888 | bytes 31457280 | tf_op jit(solution)/shard_map/mlp_half/pallas_call | solution.py:651
  280.2 5.8 %collective-permute-done.46 = bf16[512,5120]{1,0:T(8,128)(2,1)} collective-permute-done((bf16[512,5120]{1,0:T(8,128)(2,1)}, bf16[512,5120]{1,0:T(8,128)(2,1)}, u32[]{:S(2)}, u32[]{:S(2)}) %collective-permute-start.46) | collective-permute-done | bytes 5242912 | tf_op jit(solution)/shard_map/ppermute | solution.py:55
  295.4 22.8 %attention_back.1 = (bf16[512,1024]{1,0:T(8,128)(2,1)S(1)}, f32[2,512,1024]{2,1,0:T(8,128)}, bf16[2,512,1024]{2,1,0:T(8,128)(2,1)S(1)}, bf16[2,512,1024]{2,1,0:T(8,128)(2,1)}, f32[8,1,512]{2,1,0:T(1,128)S(1)}) custom-call(bf16[512,1024]{1,0:T(8,128)(2,1)S(1)} %copy-done.32, bf16[512,2048]{1,0:T(8,128)(2,1)} %copy-done, bf16[512,2048]{1,0:T(8,128)(2,1)} %copy-done, ...), custom_call_target="tpu_custom_call" | custom-call | flops 8053063680 | bytes 18874368 | tf_op jit(solution)/shard_map/attention_back/pallas_call | solution.py:447
  337.3 6.2 %weight_grads.4 = (bf16[512,3072]{1,0:T(8,128)(2,1)}, bf16[512,3072]{1,0:T(8,128)(2,1)}) custom-call(bf16[512,1024]{1,0:T(8,128)(2,1)S(1)} %fusion.30.refs_0_, bf16[512,1024]{1,0:T(8,128)(2,1)S(1)} %get-tuple-element.371.refs_1_, bf16[512,1024]{1,0:T(8,128)(2,1)S(1)} %get-tuple-element.370.refs_2_, bf16[512,1024]{1,0:T(8,128)(2,1)S(1)} %copy-done.27, ...), custom_call_target="tpu_custom_call" | custom-call | flops 3221225472 | bytes 12582912 | tf_op jit(solution)/shard_map/weight_grads/pallas_call | solution.py:739
  343.6 19.0 %collective-permute-done.50 = bf16[256,1024]{1,0:T(8,128)(2,1)S(1)} collective-permute-done((bf16[256,1024]{1,0:T(8,128)(2,1)S(1)}, bf16[256,1024]{1,0:T(8,128)(2,1)S(1)}, u32[]{:S(2)}, u32[]{:S(2)}) %collective-permute-start.50) | collective-permute-done | bytes 524320 | tf_op jit(solution)/shard_map/ppermute | solution.py:55
  376.6 10.4 %state_attention_back.1 = (f32[2,512,1024]{2,1,0:T(8,128)S(1)}, bf16[1024,512]{1,0:T(8,128)(2,1)S(1)}) custom-call(bf16[512,2048]{1,0:T(8,128)(2,1)S(1)} %copy-done.1, bf16[512,2048]{1,0:T(8,128)(2,1)S(1)} %copy-done.1, bf16[1024,512]{1,0:T(8,128)(2,1)S(1)} %bitcast.202, f32[8,1,512]{2,1,0:T(1,128)S(1)} %get-tuple-element.276.lse, ...), custom_call_target="tpu_custom_call" | custom-call | flops 2684354560 | bytes 14680064 | tf_op jit(solution)/shard_map/state_attention_back/pallas_call | solution.py:517
  411.8 9.4 %embedding_back.1 = (f32[512,1024]{1,0:T(8,128)}, bf16[512,1024]{1,0:T(8,128)(2,1)S(1)}, f32[8,1024]{1,0:T(8,128)S(1)}) custom-call(bf16[512,1024]{1,0:T(8,128)(2,1)S(1)} %copy-done.30, bf16[512,1024]{1,0:T(8,128)(2,1)S(1)} %get-tuple-element.306.refs_1_.k, bf16[512,1024]{1,0:T(8,128)(2,1)S(1)} %get-tuple-element.368.refs_2_.v, ...), custom_call_target="tpu_custom_call" | custom-call | flops 3221225472 | bytes 18874368 | tf_op jit(solution)/shard_map/embedding_back/pallas_call | solution.py:871
  455.0 11.0 %collective-permute-done.63 = bf16[1,4,32,3072]{3,2,1,0:T(8,128)(2,1)} collective-permute-done((bf16[1,4,32,3072]{3,2,1,0:T(8,128)(2,1)}, bf16[1,4,32,3072]{3,2,1,0:T(8,128)(2,1)}, u32[]{:S(2)}, u32[]{:S(2)}) %collective-permute-start.63) | collective-permute-done | bytes 786464 | tf_op jit(solution)/shard_map/ppermute | solution.py:55
  465.9 6.4 %collective-permute-done.64 = bf16[2,4,32,2048]{3,2,1,0:T(8,128)(2,1)} collective-permute-done((bf16[2,4,32,2048]{3,2,1,0:T(8,128)(2,1)}, bf16[2,4,32,2048]{3,2,1,0:T(8,128)(2,1)}, u32[]{:S(2)}, u32[]{:S(2)}) %collective-permute-start.64) | collective-permute-done | bytes 1048608 | tf_op jit(solution)/shard_map/ppermute | solution.py:55
  493.5 8.8 %collective-permute-done.73 = bf16[2,32,3072]{2,1,0:T(8,128)(2,1)S(1)} collective-permute-done((bf16[2,32,3072]{2,1,0:T(8,128)(2,1)S(1)}, bf16[2,32,3072]{2,1,0:T(8,128)(2,1)S(1)}, u32[]{:S(2)}, u32[]{:S(2)}) %collective-permute-start.73) | collective-permute-done | bytes 393248 | tf_op jit(solution)/shard_map/ppermute | solution.py:55
  519.5 13.4 %collective-permute-done.83 = bf16[32,3072]{1,0:T(8,128)(2,1)S(1)} collective-permute-done((bf16[32,3072]{1,0:T(8,128)(2,1)S(1)}, bf16[32,3072]{1,0:T(8,128)(2,1)S(1)}, u32[]{:S(2)}, u32[]{:S(2)}) %collective-permute-start.83) | collective-permute-done | bytes 196640 | tf_op jit(solution)/shard_map/ppermute | solution.py:55
  (443 shorter events, 285.8 us)
Async XLA Ops:
  28.1 28.5 %collective-permute-start.3 = (bf16[4,32,3968]{2,1,0:T(8,128)(2,1)}, bf16[4,32,3968]{2,1,0:T(8,128)(2,1)S(1)}, u32[]{:S(2)}, u32[]{:S(2)}) collective-permute-start(bf16[4,32,3968]{2,1,0:T(8,128)(2,1)} %stack_z.4.refs_0_), channel_id=1, source_target_pairs={{0,2},{1,5},{2,0},{3,7},{4,6},{5,1},{6,4},{7,3},{8,10},{9,13},{10,... | collective-permute-start | bytes 3047432 | tf_op jit(solution)/shard_map/ppermute | solution.py:55
  73.8 29.4 %collective-permute-start.8 = (bf16[4,32,4608]{2,1,0:T(8,128)(2,1)}, bf16[4,32,4608]{2,1,0:T(8,128)(2,1)}, u32[]{:S(2)}, u32[]{:S(2)}) collective-permute-start(bf16[4,32,4608]{2,1,0:T(8,128)(2,1)} %stack_z.5.refs_0_), channel_id=1, source_target_pairs={{0,2},{1,3},{2,0},{3,1},{4,6},{5,7},{6,4},{7,5},{8,10},{9,11},{10,... | collective-permute-start | bytes 3538952 | tf_op jit(solution)/shard_map/ppermute | solution.py:55
  75.0 28.4 %collective-permute-start.9 = (bf16[4,32,4608]{2,1,0:T(8,128)(2,1)}, bf16[4,32,4608]{2,1,0:T(8,128)(2,1)}, u32[]{:S(2)}, u32[]{:S(2)}) collective-permute-start(bf16[4,32,4608]{2,1,0:T(8,128)(2,1)} %stack_z.5.refs_0_), channel_id=1, source_target_pairs={{0,4},{1,5},{2,6},{3,7},{4,0},{5,1},{6,2},{7,3},{8,12},{9,13},{10,... | collective-permute-start | bytes 3538952 | tf_op jit(solution)/shard_map/ppermute | solution.py:55
  75.9 27.3 %collective-permute-start.15 = (bf16[32,4096]{1,0:T(8,128)(2,1)}, bf16[32,4096]{1,0:T(8,128)(2,1)}, u32[]{:S(2)}, u32[]{:S(2)}) collective-permute-start(bf16[32,4096]{1,0:T(8,128)(2,1)} %get-tuple-element.203.refs_0_), channel_id=1, source_target_pairs={{0,16},{1,17},{2,18},{3,19},{4,20},{5,21},{6,22},{7,23},{8,24},{9,... | collective-permute-start | bytes 786440 | tf_op jit(solution)/shard_map/ppermute | solution.py:55
  78.2 29.6 %collective-permute-start.21 = (bf16[4,32,4608]{2,1,0:T(8,128)(2,1)}, bf16[4,32,4608]{2,1,0:T(8,128)(2,1)}, u32[]{:S(2)}, u32[]{:S(2)}) collective-permute-start(bf16[4,32,4608]{2,1,0:T(8,128)(2,1)} %stack_z.5.refs_0_), channel_id=1, source_target_pairs={{0,1},{1,0},{2,3},{3,2},{4,5},{5,4},{6,7},{7,6},{8,9},{9,8},{10,11... | collective-permute-start | bytes 3538952 | tf_op jit(solution)/shard_map/ppermute | solution.py:55
  103.4 32.8 %collective-permute-start.24 = (bf16[512,2048]{1,0:T(8,128)(2,1)S(1)}, bf16[512,2048]{1,0:T(8,128)(2,1)}, u32[]{:S(2)}, u32[]{:S(2)}) collective-permute-start(bf16[512,2048]{1,0:T(8,128)(2,1)S(1)} %convolution_convert_fusion.1.k.v), channel_id=1, source_target_pairs={{0,1},{1,2},{2,3},{4,5},{5,6},{6,7},{8,9},{9,10},{10,11},{12,13},{... | collective-permute-start | bytes 6291464 | tf_op jit(solution)/shard_map/ppermute | solution.py:299
  106.4 28.6 %collective-permute-start.20 = (bf16[4,32,4608]{2,1,0:T(8,128)(2,1)}, bf16[4,32,4608]{2,1,0:T(8,128)(2,1)}, u32[]{:S(2)}, u32[]{:S(2)}) collective-permute-start(bf16[4,32,4608]{2,1,0:T(8,128)(2,1)} %collective-permute-done.8.refs_1_), channel_id=1, source_target_pairs={{0,4},{1,5},{2,6},{3,7},{4,0},{5,1},{6,2},{7,3},{8,12},{9,13},{10,... | collective-permute-start | bytes 3538952 | tf_op jit(solution)/shard_map/ppermute | solution.py:55
  107.9 27.2 %collective-permute-start.22 = (bf16[4,32,4608]{2,1,0:T(8,128)(2,1)}, bf16[4,32,4608]{2,1,0:T(8,128)(2,1)}, u32[]{:S(2)}, u32[]{:S(2)}) collective-permute-start(bf16[4,32,4608]{2,1,0:T(8,128)(2,1)} %collective-permute-done.8.refs_1_), channel_id=1, source_target_pairs={{0,1},{1,0},{2,3},{3,2},{4,5},{5,4},{6,7},{7,6},{8,9},{9,8},{10,11... | collective-permute-start | bytes 3538952 | tf_op jit(solution)/shard_map/ppermute | solution.py:55
  107.9 27.2 %collective-permute-start.23 = (bf16[4,32,4608]{2,1,0:T(8,128)(2,1)}, bf16[4,32,4608]{2,1,0:T(8,128)(2,1)}, u32[]{:S(2)}, u32[]{:S(2)}) collective-permute-start(bf16[4,32,4608]{2,1,0:T(8,128)(2,1)} %collective-permute-done.9.refs_2_), channel_id=1, source_target_pairs={{0,1},{1,0},{2,3},{3,2},{4,5},{5,4},{6,7},{7,6},{8,9},{9,8},{10,11... | collective-permute-start | bytes 3538952 | tf_op jit(solution)/shard_map/ppermute | solution.py:55
  140.6 29.7 %collective-permute-start.30 = (bf16[32,4096]{1,0:T(8,128)(2,1)}, bf16[32,4096]{1,0:T(8,128)(2,1)}, u32[]{:S(2)}, u32[]{:S(2)}) collective-permute-start(bf16[32,4096]{1,0:T(8,128)(2,1)} %get-tuple-element.219.refs_0_), channel_id=1, source_target_pairs={{0,16},{1,17},{2,18},{3,19},{4,20},{5,21},{6,22},{7,23},{8,24},{9,... | collective-permute-start | bytes 786440 | tf_op jit(solution)/shard_map/ppermute | solution.py:55
  146.6 47.4 %collective-permute-start.33 = (bf16[4,32,4096]{2,1,0:T(8,128)(2,1)}, bf16[4,32,4096]{2,1,0:T(8,128)(2,1)}, u32[]{:S(2)}, u32[]{:S(2)}) collective-permute-start(bf16[4,32,4096]{2,1,0:T(8,128)(2,1)} %stack_z.6.refs_4_.refs_12_), channel_id=1, source_target_pairs={{0,1},{1,0},{2,3},{3,2},{4,5},{5,4},{6,7},{7,6},{8,9},{9,8},{10,11... | collective-permute-start | bytes 3145736 | tf_op jit(solution)/shard_map/ppermute | solution.py:55
  240.8 27.6 %collective-permute-start.44 = (bf16[2,4,32,4096]{3,2,1,0:T(8,128)(2,1)S(1)}, bf16[2,4,32,4096]{3,2,1,0:T(8,128)(2,1)}, u32[]{:S(2)}, u32[]{:S(2)}) collective-permute-start(bf16[2,4,32,4096]{3,2,1,0:T(8,128)(2,1)S(1)} %fusion.3), channel_id=1, source_target_pairs={{0,4},{1,3},{2,6},{3,1},{4,0},{5,7},{6,2},{7,5},{8,12},{9,11},{10,... | collective-permute-start | bytes 6291464 | tf_op jit(solution)/shard_map/ppermute | solution.py:55
  290.2 31.3 %collective-permute-start.48 = (bf16[1,4,32,5120]{3,2,1,0:T(8,128)(2,1)}, bf16[1,4,32,5120]{3,2,1,0:T(8,128)(2,1)}, u32[]{:S(2)}, u32[]{:S(2)}) collective-permute-start(bf16[1,4,32,5120]{3,2,1,0:T(8,128)(2,1)} %get-tuple-element.367), channel_id=1, source_target_pairs={{0,4},{1,3},{2,6},{3,1},{4,0},{5,7},{6,2},{7,5},{8,12},{9,11},{10,... | collective-permute-start | bytes 3932168 | tf_op jit(solution)/shard_map/ppermute | solution.py:55
  331.8 40.1 %collective-permute-start.54 = (bf16[1,4,32,5120]{3,2,1,0:T(8,128)(2,1)}, bf16[1,4,32,5120]{3,2,1,0:T(8,128)(2,1)}, u32[]{:S(2)}, u32[]{:S(2)}) collective-permute-start(bf16[1,4,32,5120]{3,2,1,0:T(8,128)(2,1)} %fusion.1), channel_id=1, source_target_pairs={{0,2},{1,5},{2,0},{3,7},{4,6},{5,1},{6,4},{7,3},{8,10},{9,13},{10,... | collective-permute-start | bytes 3932168 | tf_op jit(solution)/shard_map/ppermute | solution.py:55
  362.6 37.1 %collective-permute-start.56 = (bf16[2,32,4096]{2,1,0:T(8,128)(2,1)S(1)}, bf16[2,32,4096]{2,1,0:T(8,128)(2,1)}, u32[]{:S(2)}, u32[]{:S(2)}) collective-permute-start(bf16[2,32,4096]{2,1,0:T(8,128)(2,1)S(1)} %fusion.26), channel_id=1, source_target_pairs={{0,16},{1,17},{2,18},{3,19},{4,20},{5,21},{6,22},{7,23},{8,24},{9,... | collective-permute-start | bytes 1572872 | tf_op jit(solution)/shard_map/ppermute | solution.py:55
  366.3 33.5 %collective-permute-start.55 = (bf16[2,512,1024]{2,1,0:T(8,128)(2,1)S(1)}, bf16[2,512,1024]{2,1,0:T(8,128)(2,1)}, u32[]{:S(2)}, u32[]{:S(2)}) collective-permute-start(bf16[2,512,1024]{2,1,0:T(8,128)(2,1)S(1)} %copy-done.43), channel_id=1, source_target_pairs={{1,0},{2,1},{3,2},{5,4},{6,5},{7,6},{9,8},{10,9},{11,10},{13,12},{... | collective-permute-start | bytes 6291464 | tf_op jit(solution)/shard_map/ppermute | solution.py:299
  367.6 32.2 %collective-permute-start.57 = (bf16[512,3072]{1,0:T(8,128)(2,1)}, bf16[512,3072]{1,0:T(8,128)(2,1)}, u32[]{:S(2)}, u32[]{:S(2)}) collective-permute-start(bf16[512,3072]{1,0:T(8,128)(2,1)} %get-tuple-element.296), channel_id=1, source_target_pairs={{0,1},{1,0},{2,3},{3,2},{4,5},{5,4},{6,7},{7,6},{8,9},{9,8},{10,11... | collective-permute-start | bytes 9437192 | tf_op jit(solution)/shard_map/ppermute | solution.py:55
  388.0 66.8 %collective-permute-start.66 = (bf16[2,32,5120]{2,1,0:T(8,128)(2,1)}, bf16[2,32,5120]{2,1,0:T(8,128)(2,1)}, u32[]{:S(2)}, u32[]{:S(2)}) collective-permute-start(bf16[2,32,5120]{2,1,0:T(8,128)(2,1)} %fusion.25), channel_id=1, source_target_pairs={{0,16},{1,17},{2,18},{3,19},{4,20},{5,21},{6,22},{7,23},{8,24},{9,... | collective-permute-start | bytes 1966088 | tf_op jit(solution)/shard_map/ppermute | solution.py:55
  399.8 31.7 %collective-permute-start.62 = (f32[8,512]{1,0:T(8,128)S(1)}, f32[8,512]{1,0:T(8,128)S(1)}, u32[]{:S(2)}, u32[]{:S(2)}) collective-permute-start(f32[8,512]{1,0:T(8,128)S(1)} %add.519), channel_id=1, source_target_pairs={{0,4},{1,5},{2,6},{3,7},{4,0},{5,1},{6,2},{7,3},{8,12},{9,13},{10,... | collective-permute-start | bytes 49160 | tf_op jit(solution)/shard_map/ppermute | solution.py:55
  406.5 28.2 %collective-permute-start.61 = (bf16[512,2048]{1,0:T(8,128)(2,1)}, bf16[512,2048]{1,0:T(8,128)(2,1)}, u32[]{:S(2)}, u32[]{:S(2)}) collective-permute-start(bf16[512,2048]{1,0:T(8,128)(2,1)} %get-tuple-element.312), channel_id=1, source_target_pairs={{0,1},{1,0},{2,3},{3,2},{4,5},{5,4},{6,7},{7,6},{8,9},{9,8},{10,11... | collective-permute-start | bytes 6291464 | tf_op jit(solution)/shard_map/ppermute | solution.py:55
  406.5 28.3 %collective-permute-start.60 = (bf16[512,2048]{1,0:T(8,128)(2,1)}, bf16[512,2048]{1,0:T(8,128)(2,1)}, u32[]{:S(2)}, u32[]{:S(2)}) collective-permute-start(bf16[512,2048]{1,0:T(8,128)(2,1)} %get-tuple-element.311), channel_id=1, source_target_pairs={{0,1},{1,0},{2,3},{3,2},{4,5},{5,4},{6,7},{7,6},{8,9},{9,8},{10,11... | collective-permute-start | bytes 6291464 | tf_op jit(solution)/shard_map/ppermute | solution.py:55
  437.5 28.4 %collective-permute-start.65 = (bf16[2,4,32,2048]{3,2,1,0:T(8,128)(2,1)}, bf16[2,4,32,2048]{3,2,1,0:T(8,128)(2,1)}, u32[]{:S(2)}, u32[]{:S(2)}) collective-permute-start(bf16[2,4,32,2048]{3,2,1,0:T(8,128)(2,1)} %fusion.20), channel_id=1, source_target_pairs={{0,4},{1,3},{2,6},{3,1},{4,0},{5,7},{6,2},{7,5},{8,12},{9,11},{10,... | collective-permute-start | bytes 3145736 | tf_op jit(solution)/shard_map/ppermute | solution.py:55
  441.0 31.2 %collective-permute-start.64 = (bf16[2,4,32,2048]{3,2,1,0:T(8,128)(2,1)}, bf16[2,4,32,2048]{3,2,1,0:T(8,128)(2,1)}, u32[]{:S(2)}, u32[]{:S(2)}) collective-permute-start(bf16[2,4,32,2048]{3,2,1,0:T(8,128)(2,1)} %fusion.19), channel_id=1, source_target_pairs={{0,4},{1,3},{2,6},{3,1},{4,0},{5,7},{6,2},{7,5},{8,12},{9,11},{10,... | collective-permute-start | bytes 3145736 | tf_op jit(solution)/shard_map/ppermute | solution.py:55
  511.0 27.2 %collective-permute-start.79 = (bf16[2,32,2048]{2,1,0:T(8,128)(2,1)S(1)}, bf16[2,32,2048]{2,1,0:T(8,128)(2,1)S(1)}, u32[]{:S(2)}, u32[]{:S(2)}) collective-permute-start(bf16[2,32,2048]{2,1,0:T(8,128)(2,1)S(1)} %copy-done.65), channel_id=1, source_target_pairs={{0,16},{1,17},{2,18},{3,19},{4,20},{5,21},{6,22},{7,23},{8,24},{9,... | collective-permute-start | bytes 786440 | tf_op jit(solution)/shard_map/ppermute | solution.py:55
  (141 other events, 1694.4 us)

commit v4 on v3

--- a/solution.py
+++ b/solution.py
@@ -181,24 +181,19 @@
     return send(low(chip_part(keep, got, 1 - first_axis()[0])), B_ROUTE)
 
 
-def over_first_in_two(keep, got, corner):
-    b, a = first_axis()
-    return send(low(chip_part(keep, got, 1 - b, 1 - a if corner else a)), B_ROUTE)
-
-
 def of_first(first, i):
     return lax.dynamic_index_in_dim(first, i, 0)
 
 
 def over_second(keep, got, first):
     b, a = first_axis()
-    far = first[0] if isinstance(first, tuple) else of_first(first, 1 - a)
+    far = of_first(first, 1 - a)
     return send(low(chip_part(keep, got, b, 1 - a) + f32(far)), A_ROUTE)
 
 
 def own_part(keep, got, first, second):
     b, a = first_axis()
-    mine = first[1] if isinstance(first, tuple) else of_first(first, a)
+    mine = of_first(first, a)
     return (chip_part(keep, got, b, a) + f32(mine) + f32(second))[0]
 
 
@@ -605,7 +600,15 @@
     act = low(act)
     out_acc[...] += dot(act, down_w, NN)
     g_up = low(slope * dot(g_out, down_w, NT))
-    up_bias_grad[...] = jnp.sum(f32(g_up), 0, keepdims=True)
+    column = jnp.transpose(
+        jnp.broadcast_to(jnp.sum(f32(g_up), 0, keepdims=True), (8, STEP))
+    )[:, :1]
+    lane = lax.broadcasted_iota(jnp.int32, (rk, VEC), 1) - (4 + 2 * last)
+    for i in range(STEP // hk):
+        pair = [column[i * hk + q * rk : i * hk + (q + 1) * rk] for q in range(2)]
+        up_bias_grad[i * rk : (i + 1) * rk, :] = jnp.where(
+            lane == 0, pair[0], jnp.where(lane == 1, pair[1], 0.0)
+        )
     u_acc[...] += dot(g_up, up_w, NT)
     d_up = low(dot(xs[...], g_up, NN))
     at = pl.ds(pl.multiple_of(j * STEP, STEP), STEP)
@@ -646,8 +649,7 @@
     tall = lambda a, b: pl.BlockSpec((a, b), lambda j: (0, 0), pipeline_mode=pl.Buffered(1))
     acc = jax.ShapeDtypeStruct((BLK, D), jnp.float32)
     lows = jax.ShapeDtypeStruct((BLK, D), jnp.bfloat16)
-    width = 2 * HALF + (D if last else 0)
-    grads = jax.ShapeDtypeStruct((D // 2, width), jnp.bfloat16)
+    grads = jax.ShapeDtypeStruct((D // 2, 2 * HALF), jnp.bfloat16)
     return pl.pallas_call(
         functools.partial(mlp_body, last, spot_of, alternate),
         grid=(HALF // STEP,),
@@ -661,9 +663,9 @@
         + [pl.BlockSpec((1, D // CHUNKS, HALF), lambda j: (j, 0, 1))] * 8
         + [tall(BLK, D)] * (2 if last else 0),
         out_specs=[tall(D // 2, 2 * HALF)] * 2
-        + [pl.BlockSpec((1, STEP), lambda j: (0, j))]
+        + [pl.BlockSpec((D // (HALF // STEP), VEC), lambda j: (j, 0))]
         + ([tall(BLK, D)] * 3 + [whole(8, D)] if last else [tall(BLK, D)] * 2),
-        out_shape=[grads, grads, jax.ShapeDtypeStruct((1, HALF), jnp.float32)]
+        out_shape=[grads, grads, jax.ShapeDtypeStruct((D, VEC), jnp.float32)]
         + (
             [lows, acc, lows, jax.ShapeDtypeStruct((8, D), jnp.float32)]
             if last
@@ -715,6 +717,11 @@
             a = refs[ins[0]][...]
             if kind == "transposed":
                 a = low(jnp.transpose(a))
+            elif kind == "vectors":
+                sums, gate = refs[ins[1]], refs[ins[2]]
+                a = jnp.concatenate([a[0:1], sums[0:1], gate[...], sums[1:2]], 0)
+                a = jnp.concatenate([a, jnp.zeros((VEC - 4, D), jnp.float32)], 0)
+                a = low(jnp.transpose(a) + refs[ins[3]][...] + refs[ins[4]][...])
             put(
                 [
                     (a[i * rk : (i + 1) * rk], a[(i + 1) * rk : (i + 2) * rk])
@@ -724,7 +731,7 @@
             )
 
 
-def weight_grads(core_of, plan):
+def weight_grads(core_of, plan, at=0, total=None, into=None):
     args, steps, columns, width, flops = [], [], [], 0, 0
     for kind, *arrays in plan:
         steps.append((kind, tuple(range(len(args), len(args) + len(arrays)))))
@@ -733,19 +740,35 @@
         if kind == "dot":
             n = sum(a.shape[1] for a in arrays[1:])
             flops += 2 * BLK * D * n
+        elif kind == "vectors":
+            n = VEC
         else:
             n = arrays[0].shape[1 if kind == "rows" else 0]
         width += n
+    padded = -(-width // 512) * 512 if into else width
+    total = total or width
+    n = len(args)
+
+    def body(*refs):
+        outs = refs[n + 2 :] if into else refs[n:]
+        weight_grads_body(core_of, steps, columns, *refs[:n], *outs)
+
+    whole = [pl.BlockSpec(a.shape, lambda i, r=a.ndim: (0,) * r) for a in args]
+    kept = [pl.BlockSpec(memory_space=pl.ANY)] * 2 if into else []
     return pl.pallas_call(
-        functools.partial(weight_grads_body, core_of, steps, columns),
-        out_shape=[jax.ShapeDtypeStruct((D // 2, width), jnp.bfloat16)] * 2,
+        body,
+        grid=(1,),
+        in_specs=whole + kept,
+        out_specs=[pl.BlockSpec((D // 2, padded), lambda i: (0, at // padded))] * 2,
+        out_shape=[jax.ShapeDtypeStruct((D // 2, total), jnp.bfloat16)] * 2,
+        input_output_aliases={n: 0, n + 1: 1} if into else {},
         scratch_shapes=[pltpu.VMEM((D, BLK), jnp.bfloat16)],
-        compiler_params=pltpu.CompilerParams(vmem_limit_bytes=48 * 2**20),
+        compiler_params=pltpu.CompilerParams(vmem_limit_bytes=56 * 2**20),
         cost_estimate=pl.CostEstimate(
             flops=flops, bytes_accessed=4 * D * width, transcendentals=0
         ),
         name="weight_grads",
-    )(*args)
+    )(*args, *(into or ()))
 
 
 def natural(keep, away):
@@ -754,29 +777,30 @@
     return jnp.stack(parts, 3).reshape(-1, keep.shape[1])
 
 
-def out_weight_grad(core_of, mixed, branch, keep, away):
-    def body(x, g, keep_in, away_in, keep_out, away_out, split):
-        weight_grads_body(
-            core_of, [("dot", (0, 1))], [0], x, g, keep_out, away_out, split
-        )
-
-    whole = pl.BlockSpec((BLK, D), lambda i: (0, 0))
-    here = pl.BlockSpec(memory_space=pl.ANY)
-    last = pl.BlockSpec((D // 2, D), lambda i: (0, keep.shape[1] // D - 1))
+def finish_mlp(end_a, end_b):
+    rows = end_a[0].shape[0]
+
+    def body(a0, a1, b0, b1, up, down):
+        halves = a0[...] + f32(a1[...]), b0[...] + f32(b1[...])
+        lane = lax.broadcasted_iota(jnp.int32, (rows, 128), 1) < 64
+        for i in range(0, CHUNKS, 2):
+            a, b = (half[:, i * 64 : i * 64 + 128] for half in halves)
+            up[:, i * 128 : (i + 1) * 128] = jnp.where(lane, a, pltpu.roll(b, 64, 1))
+            up[:, (i + 1) * 128 : (i + 2) * 128] = jnp.where(lane, pltpu.roll(a, 64, 1), b)
+        at = 0
+        for half in halves:
+            for q in range(HALF // D):
+                down[at : at + rows, :] = half[:, HALF + q * D : HALF + (q + 1) * D]
+                at += rows
+
     return pl.pallas_call(
         body,
-        grid=(1,),
-        in_specs=[whole, whole, here, here],
-        out_specs=[last, last],
-        out_shape=[jax.ShapeDtypeStruct(keep.shape, keep.dtype)] * 2,
-        input_output_aliases={2: 0, 3: 1},
-        scratch_shapes=[pltpu.VMEM((D, BLK), jnp.bfloat16)],
-        compiler_params=pltpu.CompilerParams(vmem_limit_bytes=32 * 2**20),
-        cost_estimate=pl.CostEstimate(
-            flops=2 * BLK * D * D, bytes_accessed=4 * 2**20, transcendentals=0
-        ),
-        name="out_weight_grad",
-    )(mixed, branch, keep, away)
+        out_shape=[
+            jax.ShapeDtypeStruct((rows, 2 * HALF), jnp.float32),
+            jax.ShapeDtypeStruct((4 * rows, D), jnp.float32),
+        ],
+        name="finish_mlp",
+    )(*end_a, *end_b)
 
 
 def pack_first(attn_gain, mlp_gain, gate, down_bias, up_bias, *matrices):
@@ -1043,33 +1067,35 @@
         )
     output, grad_hidden, grad_branch, mlp_sums = before
 
-    keep_b, away_b = out_weight_grad(core_of, mixed, grad_branch, keep_b, away_b)
     grad_mixed = low(dot(grad_branch, out_full, NT))
     if fast:
+        second_a = over_second(keep_a, got_a, first_a)
         got_b, grad_mixed = join(to_core(away_b), grad_mixed)
-        second_a = over_second(keep_a, got_a, first_a)
-        corner_b = over_first_in_two(keep_b, got_b, True)
+        first_b = over_first(keep_b, got_b)
     gq, gkv, gprev, gstate, gbias = attention_back(
         query, kv, prev, skv, bias_rows, lse, grad_mixed
     )
     gbias = gbias.reshape(HEADS, BLK)
     if fast:
-        second_a, corner_b, gprev, gstate = join(second_a, corner_b, gprev, gstate)
-        side_b = over_first_in_two(keep_b, got_b, False)
+        second_a, first_b, gprev, gstate = join(second_a, first_b, gprev, gstate)
     read, sent = readout(gstate, skv_full)
     if fast:
-        sibling, gbias = send(sent, CORE_ROUTE), exchange(gbias, CORE_ROUTE)
+        sibling = send(sent, CORE_ROUTE)
         near = later_near(keep_gate, sent, sibling)
     first = weight_grads(
-        core_of, [("dot", state_low, gstate[0], gstate[1]), ("dot", normed_low, gq)]
+        core_of,
+        [
+            ("dot", mixed, grad_branch),
+            ("dot", state_low, gstate[0], gstate[1]),
+            ("dot", normed_low, gq),
+        ],
     )
     if fast:
-        near, side_b, first, gbias = join(near, side_b, first, gbias)
-        first_b = (corner_b, side_b)
-        gnext = from_behind(tie(gprev, near), "seq", -1)
-        pair_a = over_pairs(keep_a, got_a, first_a, second_a)
+        pair_a = over_pairs(keep_a, got_a, first_a, tie(second_a, first[0]))
+        near, first = join(near, first)
+        gprev = tie(gprev, near)
+        gnext = from_behind(gprev, "seq", -1)
         got_c = to_core(first[1])
-        gbias = exchange(gbias, X_ROUTE)
         after = later_sum(keep_gate, near, sibling)
     else:
         gnext = from_behind(gprev, "seq", -1)
@@ -1077,110 +1103,93 @@
     grad_update = low((1.0 - keep_gate) * after)
     grad_smix = low(dot(grad_update, update_full, NT))
     if fast:
-        grad_smix, second_b = join(grad_smix, over_second(keep_b, got_b, first_b))
+        got_c, grad_smix = join(got_c, grad_smix)
+        gbias = exchange(tie(gbias, grad_smix), CORE_ROUTE)
     gsum, gquery = state_attention_back(kv, squery_full, state_lse, grad_smix, gkv)
     if fast:
         gsum, after = join(gsum, after)
     state_init_grad = jnp.where(is_first, read + keep_gate * after, 0.0)
-    second = weight_grads(
+    last = weight_grads(
         core_of,
         [
             ("dot", state_mix, grad_update),
             ("rows", gquery),
             ("transposed", state_init_grad),
         ],
+        0,
+        4 * D + 512,
     )
     if fast:
-        gnext, pair_a, got_c, second, gbias = join(gnext, pair_a, got_c, second, gbias)
-        first_c = over_first(first[0], got_c)
-        pair_b = over_pairs(keep_b, got_b, first_b, second_b)
-        got_d = to_core(second[1])
-        gbias = exchange(gbias, Y_ROUTE)
+        gnext, last, gbias, pair_a = join(gnext, last, gbias, pair_a)
+        second_b = over_second(keep_b, got_b, tie(first_b, gnext))
+        first_c = over_first(first[0], tie(got_c, gnext))
+        gbias = exchange(gbias, X_ROUTE)
     gk, gv = (low(gsum[i] + f32(gnext[i])) for i in range(2))
-    key_grads = weight_grads(core_of, [("dot", normed_low, gk, gv)])
-    if fast:
-        gk, got_e = tie((gk, key_grads[1]), key_grads[0])
-        got_e = to_core(got_e)
+    last = weight_grads(core_of, [("dot", normed_low, gk, gv)], 2 * D, 4 * D + 512, last)
     embedded_grad, embedded_low, gain_grad = embedding_back(
         gq, gk, gv, query_full, kv_full, embedded, grad_hidden, vector_rows
     )
-    if fast:
-        first_c, got_d, got_e, embedded_low, gbias = join(
-            first_c, got_d, got_e, embedded_low, gbias
-        )
-        second_c = over_second(first[0], got_c, first_c)
-        first_d, first_e = over_first(second[0], got_d), over_first(key_grads[0], got_e)
-        position_table_grad = exchange(exchange(gbias, Z_NEAR), Z_FAR)
-        after, mlp_sums, bias_a, bias_b = join(after, mlp_sums, bias_a, bias_b, gain_grad)[:4]
-    else:
-        position_table_grad = lax.psum(gbias, AX)
     gate_bias_grad = jnp.sum(after * (state_prev - update), 0) * keep_gate * (1.0 - keep_gate)
-    up_bias_grad = jnp.concatenate([b.reshape(CHUNKS, -1) for b in (bias_a, bias_b)], 1)
-    vector_grads = jnp.concatenate(
-        [gain_grad[:1], mlp_sums[:1], gate_bias_grad[None], mlp_sums[1:2]]
-        + [up_bias_grad.reshape(-1, folds, rows).transpose(1, 0, 2).reshape(folds, D)]
-        + [jnp.zeros((VEC - 4 - folds, D), jnp.float32)],
-        0,
-    )
     last = weight_grads(
-        core_of, [("dot", embedded_low, one_hot), ("transposed", vector_grads)]
+        core_of,
+        [
+            ("dot", embedded_low, one_hot),
+            ("vectors", gain_grad, mlp_sums, gate_bias_grad[None], bias_a, bias_b),
+        ],
+        4 * D,
+        4 * D + 512,
+        last,
     )
     if fast:
-        second_c, first_d, first_e, pair_b, got_f, position_table_grad = join(
-            second_c, first_d, first_e, pair_b, to_core(last[1]), position_table_grad
-        )
-        second_d = over_second(second[0], got_d, first_d)
-        second_e = over_second(key_grads[0], got_e, first_e)
-        first_f = over_first(last[0], got_f)
+        second_b, first_c, last, gbias = join(second_b, first_c, last, gbias)
+        got_d = to_core(last[1])
+        pair_b = over_pairs(keep_b, got_b, first_b, second_b)
+        first_d = over_first(last[0], got_d)
+        second_c = over_second(first[0], got_c, first_c)
+        end_a = within_pair(*pair_a)
+        gbias = exchange(gbias, Y_ROUTE)
+        second_c, first_d, pair_b, end_a, gbias = join(second_c, first_d, pair_b, end_a, gbias)
+        second_d = over_second(last[0], got_d, first_d)
         pair_c = over_pairs(first[0], got_c, first_c, second_c)
         end_b = within_pair(*pair_b)
-        second_d, second_e, first_f, pair_c, end_b = join(
-            second_d, second_e, first_f, pair_c, end_b
-        )
-        end_e = over_z(key_grads[0], got_e, first_e, second_e)
-        second_f = over_second(last[0], got_f, first_f)
-        pair_d = over_pairs(second[0], got_d, first_d, second_d)
-        end_e, second_f, pair_d = join(end_e, second_f, pair_d)
-        end_f = over_z(last[0], got_f, first_f, second_f)
-        end_c, end_d = within_pair(*pair_c), within_pair(*pair_d)
-        end_a = within_pair(*pair_a)
-        sums = [finish(s) for s in (end_a, end_b, end_c, end_d, end_e, end_f)]
-        up_sum = jnp.concatenate([s[:, :HALF].reshape(rows, CHUNKS, -1) for s in sums[:2]], 2)
-        up_sum = up_sum.reshape(rows, ff)
-        down_sum = jnp.concatenate([unfold(s[:, HALF : 2 * HALF]) for s in sums[:2]], 0)
-        out_sum = sums[1][:, 2 * HALF :]
-        first, second, key_sum, last = sums[2:]
+        gbias = exchange(gbias, Z_NEAR)
+        second_d, end_b, gbias = join(second_d, end_b, gbias)
+        up_sum, down_sum = finish_mlp(end_a, end_b)
+        end_d = over_z(last[0], got_d, first_d, second_d)
+        pair_c, up_sum = join(pair_c, up_sum)
+        end_c = within_pair(*pair_c)
+        position_table_grad = exchange(gbias, Z_FAR)
+        first, last = finish(end_c), finish(end_d)
     else:
         pairs = [natural(keep_a, away_a), natural(keep_b, away_b)]
-        out_sum = scatter_any(pairs[1][:, 2 * HALF :])
         up_sum = jnp.concatenate([s[:, :HALF].reshape(D, CHUNKS, -1) for s in pairs], 2)
         up_sum = scatter_any(up_sum.reshape(D, ff))
         down_sum = jnp.concatenate(
             [
-                s[:, HALF : 2 * HALF].reshape(CHUNKS, D // CHUNKS, -1, D).transpose(0, 2, 1, 3)
+                s[:, HALF:].reshape(CHUNKS, D // CHUNKS, -1, D).transpose(0, 2, 1, 3)
                 for s in pairs
             ],
             1,
         )
         down_sum = scatter_any(down_sum.reshape(ff, D))
-        first, second, key_sum, last = (
-            scatter_any(natural(*s)) for s in (first, second, key_grads, last)
-        )
-    vector_sum = last[:, VOCAB:]
+        first, last = (scatter_any(natural(*s)) for s in (first, last))
+        position_table_grad = lax.psum(gbias, AX)
+    main = 4 * D + VOCAB
+    vector_sum = last[:, main:]
     return (
         output,
         embedded_grad,
-        last[:, :VOCAB],
+        last[:, 4 * D : main],
         vector_sum[:, 0],
-        first[:, 2 * D :],
-        key_sum[:, :D],
-        key_sum[:, D:],
-        out_sum,
+        first[:, 3 * D :],
+        last[:, 2 * D : 3 * D],
+        last[:, 3 * D : 4 * D],
         first[:, :D],
         first[:, D : 2 * D],
-        second[:, :D],
-        second[:, D : D + NSTATE],
-        second[:, D + NSTATE :],
+        first[:, 2 * D : 3 * D],
+        last[:, :D],
+        last[:, D : D + NSTATE],
+        last[:, D + NSTATE : 2 * D],
         vector_sum[:, 2],
         position_table_grad,
         vector_sum[:, 1],

time: 558 us -> 533 us (0.955)
  waiting for transfers between devices: 149 us -> 179 us
  starting transfers between devices: 101 us -> 71.1 us
  local copies, waits for them, and re-layouts: 51.3 us -> 31.8 us
  other arithmetic: 66.4 us -> 52.1 us
  Pallas kernels: 160 us -> 171 us
    ppermute x84 -> x72, waiting for transfers between devices: 149 us -> 179 us  [send(): return lax.ppermute(v, AX, pairs)]
    ppermute x84 -> x72, starting transfers between devices: 96.9 us -> 66.7 us  [send(): return lax.ppermute(v, AX, pairs)]
    pallas_call x5, Pallas kernels: 18.5 us -> 29.5 us  [the longest x4 27 us: weight_grads(): pl.pallas_call(body, grid=(1,), in_specs=whole + kept, out_specs=[pl.Bloc...]
    unnamed x161 -> x134, local copies, waits for them, and re-layouts: 27.7 us -> 17.7 us
    convert_element_type x22 -> x17, other arithmetic: 41.1 us -> 32.4 us  [low(): return v.astype(jnp.bfloat16)]
    add x6 -> x4, other arithmetic: 12.1 us -> 10 us  [own_part(): return (chip_part(keep, got, b, a) + f32(mine) + f32(second))[0]]
  transfers between devices with their start and end apart: 86 -> 74, of which waited for: 24 -> 31; matrix products, arithmetic and copies ran while one was open for 18% -> 14% of each run, Pallas kernels for 28% -> 31%
where the time goes in v4:
time: 533 us; the launch traced here: 525 us
  waiting for transfers between devices  179 us (34%)
  Pallas kernels  171 us (32%)
  starting transfers between devices  71.1 us (13%)
  other arithmetic  52.1 us (10%)
  local copies, waits for them, and re-layouts  31.8 us (6%)
  matrix products  18.1 us (3%)
    ppermute x72, waiting for transfers between devices, send(): return lax.ppermute(v, AX, pairs)  179 us
    ppermute x72, starting transfers between devices, send(): return lax.ppermute(v, AX, pairs)  66.7 us
    pallas_call x2, Pallas kernels, mlp_half(): pl.pallas_call(functools.partial(mlp_body, last, spot_of, alternate), gri...  50.1 us
    convert_element_type x17, other arithmetic, low(): return v.astype(jnp.bfloat16)  32.4 us
    pallas_call x4, Pallas kernels, weight_grads(): pl.pallas_call(body, grid=(1,), in_specs=whole + kept, out_specs=[pl.Bloc...  27 us
    pallas_call x1, Pallas kernels, attention_back(): pl.pallas_call(attention_back_body, grid=(HEADS,), in_specs=[head_block(0...  22.5 us
    dot_general x8, matrix products, dot(): lax.dot_general(a, b, (dims, ((), ())), preferred_element_type=jnp.float32)  18.1 us
    unnamed x134, local copies, waits for them, and re-layouts  17.7 us
  transfers between devices with their start and end apart: 74, of which 31 were waited for; matrix products, arithmetic and copies ran while one was open for 14% of the time, Pallas kernels for 31%

profile of v4, /device:TPU:0, one launch (start us, length us, event | category | flops | bytes accessed | tf_op | source)
XLA Modules:
  0.0 525.2 jit_solution(11418265487683140198)
XLA Ops:
  14.5 14.9 %collective-permute-done.1.refs_2_ = bf16[32,3968]{1,0:T(8,128)(2,1)S(1)} collective-permute-done((bf16[32,3968]{1,0:T(8,128)(2,1)}, bf16[32,3968]{1,0:T(8,128)(2,1)S(1)}, u32[]{:S(2)}, u32[]{:S(2)}) %collective-permute-start.1) | collective-permute-done | bytes 253984 | tf_op jit(solution)/shard_map/ppermute | solution.py:55
  43.7 19.6 %collective-permute-done.6.refs_2_ = bf16[32,4608]{1,0:T(8,128)(2,1)S(1)} collective-permute-done((bf16[32,4608]{1,0:T(8,128)(2,1)}, bf16[32,4608]{1,0:T(8,128)(2,1)S(1)}, u32[]{:S(2)}, u32[]{:S(2)}) %collective-permute-start.6) | collective-permute-done | bytes 294944 | tf_op jit(solution)/shard_map/ppermute | solution.py:55
  67.0 8.7 %collective-permute-done.14.refs_1_ = bf16[32,4096]{1,0:T(8,128)(2,1)} collective-permute-done((bf16[32,4096]{1,0:T(8,128)(2,1)}, bf16[32,4096]{1,0:T(8,128)(2,1)}, u32[]{:S(2)}, u32[]{:S(2)}) %collective-permute-start.14) | collective-permute-done | bytes 262176 | tf_op jit(solution)/shard_map/ppermute | solution.py:55
  84.1 5.4 %assemble.2 = (bf16[4,2,2,2,32,384]{5,4,3,2,1,0:T(8,128)(2,1)}, bf16[4,2,2,2,32,2048]{5,4,3,2,1,0:T(8,128)(2,1)}, bf16[4,2,2,2,32,512]{5,4,3,2,1,0:T(8,128)(2,1)S(1)}, bf16[4,2,2,2,32,1024]{5,4,3,2,1,0:T(8,128)(2,1)S(1)}) custom-call(bf16[4,32,3968]{2,1,0:T(8,128)(2,1)S(1)} %copy-done.9, bf16[4,32,3968]{2,1,0:T(8,128)(2,1)S(1)} %copy-done.20, ...), custom_call_target="tpu_custom_call" | custom-call | tf_op jit(solution)/shard_map/assemble/pallas_call | solution.py:110
  97.7 7.0 %state_attention.1 = (bf16[512,1024]{1,0:T(8,128)(2,1)S(1)}, f32[8,1,512]{2,1,0:T(1,128)S(1)}) custom-call(bf16[512,2048]{1,0:T(8,128)(2,1)S(1)} %convolution_convert_fusion.1.k.v, bf16[512,2048]{1,0:T(8,128)(2,1)S(1)} %convolution_convert_fusion.1.k.v, bf16[1024,512]{1,0:T(8,128)(2,1)S(1)} %bitcast.139), custom_call_target="tpu_custom_call" | custom-call | flops 1073741824 | bytes 4194304 | tf_op jit(solution)/shard_map/state_attention/pallas_call | solution.py:481
  118.7 6.3 %collective-permute-done.25.refs_1_ = bf16[32,4096]{1,0:T(8,128)(2,1)} collective-permute-done((bf16[32,4096]{1,0:T(8,128)(2,1)}, bf16[32,4096]{1,0:T(8,128)(2,1)}, u32[]{:S(2)}, u32[]{:S(2)}) %collective-permute-start.25) | collective-permute-done | bytes 262176 | tf_op jit(solution)/shard_map/ppermute | solution.py:55
  127.2 12.7 %collective-permute-done.20.refs_3_ = bf16[4,32,4608]{2,1,0:T(8,128)(2,1)} collective-permute-done((bf16[4,32,4608]{2,1,0:T(8,128)(2,1)}, bf16[4,32,4608]{2,1,0:T(8,128)(2,1)}, u32[]{:S(2)}, u32[]{:S(2)}) %collective-permute-start.20) | collective-permute-done | bytes 1179680 | tf_op jit(solution)/shard_map/ppermute | solution.py:55
  139.9 5.1 collective-permute-start.26
  155.4 6.5 %assemble.3 = (bf16[4,2,2,2,32,1024]{5,4,3,2,1,0:T(8,128)(2,1)S(1)}, bf16[4,2,2,2,32,512]{5,4,3,2,1,0:T(8,128)(2,1)S(1)}, bf16[4,2,2,2,32,2048]{5,4,3,2,1,0:T(8,128)(2,1)}, bf16[4,2,2,2,32,1024]{5,4,3,2,1,0:T(8,128)(2,1)}) custom-call(bf16[4,32,4608]{2,1,0:T(8,128)(2,1)S(1)} %copy-done.5, bf16[4,32,4608]{2,1,0:T(8,128)(2,1)} %collective-permute-done.8.refs_1_, ...), custom_call_target="tpu_custom_call" | custom-call | tf_op jit(solution)/shard_map/assemble/pallas_call | solution.py:110
  180.3 14.0 %attention.1 = (bf16[512,1024]{1,0:T(8,128)(2,1)S(1)}, f32[8,1,512]{2,1,0:T(1,128)S(1)}) custom-call(bf16[512,1024]{1,0:T(8,128)(2,1)S(1)} %convolution_convert_fusion.4.q, bf16[512,2048]{1,0:T(8,128)(2,1)S(1)} %convolution_convert_fusion.1.k.v, bf16[512,2048]{1,0:T(8,128)(2,1)S(1)} %convolution_convert_fusion.1.k.v, ...), custom_call_target="tpu_custom_call" | custom-call | flops 3221225472 | bytes 9437184 | tf_op jit(solution)/shard_map/attention/pallas_call | solution.py:387
  200.0 23.7 %mlp_half.2 = (bf16[512,4096]{1,0:T(8,128)(2,1)}, bf16[512,4096]{1,0:T(8,128)(2,1)}, f32[1024,128]{1,0:T(8,128)}, f32[512,1024]{1,0:T(8,128)}, f32[512,1024]{1,0:T(8,128)}) custom-call(f32[512,1024]{1,0:T(8,128)} %convolution_add_fusion.refs_0_, bf16[512,1024]{1,0:T(8,128)(2,1)} %refs_1_.3, f32[8,1024]{1,0:T(8,128)} %copy-done.21, ...), custom_call_target="tpu_custom_call" | custom-call | flops 12884901888 | bytes 31457280 | tf_op jit(solution)/shard_map/mlp_half/pallas_call | solution.py:653
  245.2 26.4 %mlp_half.3 = (bf16[512,4096]{1,0:T(8,128)(2,1)}, bf16[512,4096]{1,0:T(8,128)(2,1)}, f32[1024,128]{1,0:T(8,128)}, bf16[512,1024]{1,0:T(8,128)(2,1)}, f32[512,102...) custom-call(f32[512,1024]{1,0:T(8,128)} %convolution_add_fusion.refs_0_, bf16[512,1024]{1,0:T(8,128)(2,1)} %refs_1_.3, ...), custom_call_target="tpu_custom_call" | custom-call | flops 12884901888 | bytes 31457280 | tf_op jit(solution)/shard_map/mlp_half/pallas_call | solution.py:653
  286.2 22.5 %attention_back.1 = (bf16[512,1024]{1,0:T(8,128)(2,1)S(1)}, f32[2,512,1024]{2,1,0:T(8,128)}, bf16[2,512,1024]{2,1,0:T(8,128)(2,1)}, bf16[2,512,1024]{2,1,0:T(8,128)(2,1)}, f32[8,1,512]{2,1,0:T(1,128)S(1)}) custom-call(bf16[512,1024]{1,0:T(8,128)(2,1)S(1)} %convolution_convert_fusion.4.q, bf16[512,2048]{1,0:T(8,128)(2,1)} %copy-done, ...), custom_call_target="tpu_custom_call" | custom-call | flops 8053063680 | bytes 18874368 | tf_op jit(solution)/shard_map/attention_back/pallas_call | solution.py:442
  310.7 8.5 %collective-permute-done.48 = bf16[2,4,32,4096]{3,2,1,0:T(8,128)(2,1)} collective-permute-done((bf16[2,4,32,4096]{3,2,1,0:T(8,128)(2,1)}, bf16[2,4,32,4096]{3,2,1,0:T(8,128)(2,1)}, u32[]{:S(2)}, u32[]{:S(2)}) %collective-permute-start.48) | collective-permute-done | bytes 2097184 | tf_op jit(solution)/shard_map/ppermute | solution.py:55
  328.6 11.2 %weight_grads.4 = (bf16[512,4096]{1,0:T(8,128)(2,1)}, bf16[512,4096]{1,0:T(8,128)(2,1)}) custom-call(bf16[512,1024]{1,0:T(8,128)(2,1)} %copy-done.29, bf16[512,1024]{1,0:T(8,128)(2,1)} %get-tuple-element.259.refs_1_, bf16[512,1024]{1,0:T(8,128)(2,1)} %copy-done.46, bf16[512,1024]{1,0:T(8,128)(2,1)} %get-tuple-element.350.refs_3_, ...), custom_call_target="tpu_custom_call" | custom-call | flops 4294967296 | bytes 16777216 | tf_op jit(solution)/shard_map/weight_grads/pallas_call | solution.py:758
  354.6 10.5 %state_attention_back.1 = (f32[2,512,1024]{2,1,0:T(8,128)S(1)}, bf16[1024,512]{1,0:T(8,128)(2,1)S(1)}) custom-call(bf16[512,2048]{1,0:T(8,128)(2,1)S(1)} %copy-done.1, bf16[512,2048]{1,0:T(8,128)(2,1)S(1)} %copy-done.1, bf16[1024,512]{1,0:T(8,128)(2,1)S(1)} %bitcast.140, f32[8,1,512]{2,1,0:T(1,128)S(1)} %get-tuple-element.262.lse, ...), custom_call_target="tpu_custom_call" | custom-call | flops 2684354560 | bytes 14680064 | tf_op jit(solution)/shard_map/state_attention_back/pallas_call | solution.py:512
  367.8 6.1 %weight_grads.5 = (bf16[512,4608]{1,0:T(8,128)(2,1)}, bf16[512,4608]{1,0:T(8,128)(2,1)}) custom-call(bf16[512,1024]{1,0:T(8,128)(2,1)} %copy-done.13, bf16[512,1024]{1,0:T(8,128)(2,1)} %copy-done.44, bf16[1024,512]{1,0:T(8,128)(2,1)} %copy-done.14, f32[512,1024]{1,0:T(8,128)} %get-tuple-element.348.refs_3_), custom_call_target="tpu_custom_call" | custom-call | flops 1073741824 | bytes 8388608 | tf_op jit(solution)/shard_map/weight_grads/pallas_call | solution.py:758
  387.6 6.4 %weight_grads.6 = (bf16[512,4608]{1,0:T(8,128)(2,1)}, bf16[512,4608]{1,0:T(8,128)(2,1)}) custom-call(bf16[512,1024]{1,0:T(8,128)(2,1)} %copy-done.40, bf16[512,1024]{1,0:T(8,128)(2,1)} %get-tuple-element.343.k.refs_1_, bf16[512,1024]{1,0:T(8,128)(2,1)} %get-tuple-element.342.v.refs_2_, ...), custom_call_target="tpu_custom_call", output_to_operand_aliasing={{0}: (3, {}), {1}: (4, {})} | custom-call | flops 2147483648 | bytes 8388608 | tf_op jit(solution)/shard_map/weight_grads/pallas_call | solution.py:758
  394.1 9.4 %embedding_back.1 = (f32[512,1024]{1,0:T(8,128)}, bf16[512,1024]{1,0:T(8,128)(2,1)S(1)}, f32[8,1024]{1,0:T(8,128)S(1)}) custom-call(bf16[512,1024]{1,0:T(8,128)(2,1)S(1)} %copy-done.17, bf16[512,1024]{1,0:T(8,128)(2,1)S(1)} %copy-done.3, bf16[512,1024]{1,0:T(8,128)(2,1)S(1)} %copy-done.2, bf16[1024,1024]{1,0:T(8,128)(2,1)} %bitcast.141, ...), custom_call_target="tpu_custom_call" | custom-call | flops 3221225472 | bytes 18874368 | tf_op jit(solution)/shard_map/embedding_back/pallas_call | solution.py:895
  408.4 6.0 %collective-permute-done.57 = bf16[2,4,32,4096]{3,2,1,0:T(8,128)(2,1)} collective-permute-done((bf16[2,4,32,4096]{3,2,1,0:T(8,128)(2,1)S(1)}, bf16[2,4,32,4096]{3,2,1,0:T(8,128)(2,1)}, u32[]{:S(2)}, u32[]{:S(2)}) %collective-permute-start.57) | collective-permute-done | bytes 2097184 | tf_op jit(solution)/shard_map/ppermute | solution.py:55
  435.2 21.5 %collective-permute-done.64 = f32[8,512]{1,0:T(8,128)S(1)} collective-permute-done((f32[8,512]{1,0:T(8,128)S(1)}, f32[8,512]{1,0:T(8,128)S(1)}, u32[]{:S(2)}, u32[]{:S(2)}) %collective-permute-start.64) | collective-permute-done | bytes 16416 | tf_op jit(solution)/shard_map/ppermute | solution.py:55
  484.5 7.4 %collective-permute-done.71 = bf16[2,32,4096]{2,1,0:T(8,128)(2,1)} collective-permute-done((bf16[2,32,4096]{2,1,0:T(8,128)(2,1)}, bf16[2,32,4096]{2,1,0:T(8,128)(2,1)}, u32[]{:S(2)}, u32[]{:S(2)}) %collective-permute-start.71) | collective-permute-done | bytes 524320 | tf_op jit(solution)/shard_map/ppermute | solution.py:55
  498.6 11.4 %collective-permute-done.72 = bf16[32,4096]{1,0:T(8,128)(2,1)S(1)} collective-permute-done((bf16[32,4096]{1,0:T(8,128)(2,1)S(1)}, bf16[32,4096]{1,0:T(8,128)(2,1)S(1)}, u32[]{:S(2)}, u32[]{:S(2)}) %collective-permute-start.72) | collective-permute-done | bytes 262176 | tf_op jit(solution)/shard_map/ppermute | solution.py:55
  515.2 5.9 %collective-permute-done.69 = bf16[32,4608]{1,0:T(8,128)(2,1)S(1)} collective-permute-done((bf16[32,4608]{1,0:T(8,128)(2,1)S(1)}, bf16[32,4608]{1,0:T(8,128)(2,1)S(1)}, u32[]{:S(2)}, u32[]{:S(2)}) %collective-permute-start.69) | collective-permute-done | bytes 294944 | tf_op jit(solution)/shard_map/ppermute | solution.py:55
  (353 shorter events, 246.0 us)
Async XLA Ops:
  32.5 30.8 %collective-permute-start.4 = (bf16[4,32,3968]{2,1,0:T(8,128)(2,1)}, bf16[4,32,3968]{2,1,0:T(8,128)(2,1)S(1)}, u32[]{:S(2)}, u32[]{:S(2)}) collective-permute-start(bf16[4,32,3968]{2,1,0:T(8,128)(2,1)} %stack_z.4.refs_0_), channel_id=1, source_target_pairs={{0,4},{1,3},{2,6},{3,1},{4,0},{5,7},{6,2},{7,5},{8,12},{9,11},{10,... | collective-permute-start | bytes 3047432 | tf_op jit(solution)/shard_map/ppermute | solution.py:55
  34.1 29.2 %collective-permute-start.3 = (bf16[4,32,3968]{2,1,0:T(8,128)(2,1)}, bf16[4,32,3968]{2,1,0:T(8,128)(2,1)S(1)}, u32[]{:S(2)}, u32[]{:S(2)}) collective-permute-start(bf16[4,32,3968]{2,1,0:T(8,128)(2,1)} %stack_z.4.refs_0_), channel_id=1, source_target_pairs={{0,2},{1,5},{2,0},{3,7},{4,6},{5,1},{6,4},{7,3},{8,10},{9,13},{10,... | collective-permute-start | bytes 3047432 | tf_op jit(solution)/shard_map/ppermute | solution.py:55
  35.6 27.7 %collective-permute-start.6 = (bf16[32,4608]{1,0:T(8,128)(2,1)}, bf16[32,4608]{1,0:T(8,128)(2,1)S(1)}, u32[]{:S(2)}, u32[]{:S(2)}) collective-permute-start(bf16[32,4608]{1,0:T(8,128)(2,1)} %get-tuple-element.184.refs_0_), channel_id=1, source_target_pairs={{0,16},{1,17},{2,18},{3,19},{4,20},{5,21},{6,22},{7,23},{8,24},{9,... | collective-permute-start | bytes 884744 | tf_op jit(solution)/shard_map/ppermute | solution.py:55
  78.7 28.6 %collective-permute-start.15 = (bf16[32,4096]{1,0:T(8,128)(2,1)}, bf16[32,4096]{1,0:T(8,128)(2,1)}, u32[]{:S(2)}, u32[]{:S(2)}) collective-permute-start(bf16[32,4096]{1,0:T(8,128)(2,1)} %get-tuple-element.191.refs_0_), channel_id=1, source_target_pairs={{0,16},{1,17},{2,18},{3,19},{4,20},{5,21},{6,22},{7,23},{8,24},{9,... | collective-permute-start | bytes 786440 | tf_op jit(solution)/shard_map/ppermute | solution.py:55
  78.7 32.7 %collective-permute-start.21 = (bf16[4,32,4608]{2,1,0:T(8,128)(2,1)}, bf16[4,32,4608]{2,1,0:T(8,128)(2,1)}, u32[]{:S(2)}, u32[]{:S(2)}) collective-permute-start(bf16[4,32,4608]{2,1,0:T(8,128)(2,1)} %stack_z.5.refs_0_), channel_id=1, source_target_pairs={{0,1},{1,0},{2,3},{3,2},{4,5},{5,4},{6,7},{7,6},{8,9},{9,8},{10,11... | collective-permute-start | bytes 3538952 | tf_op jit(solution)/shard_map/ppermute | solution.py:55
  79.2 28.2 %collective-permute-start.9 = (bf16[4,32,4608]{2,1,0:T(8,128)(2,1)}, bf16[4,32,4608]{2,1,0:T(8,128)(2,1)}, u32[]{:S(2)}, u32[]{:S(2)}) collective-permute-start(bf16[4,32,4608]{2,1,0:T(8,128)(2,1)} %stack_z.5.refs_0_), channel_id=1, source_target_pairs={{0,4},{1,5},{2,6},{3,7},{4,0},{5,1},{6,2},{7,3},{8,12},{9,13},{10,... | collective-permute-start | bytes 3538952 | tf_op jit(solution)/shard_map/ppermute | solution.py:55
  79.7 27.9 %collective-permute-start.8 = (bf16[4,32,4608]{2,1,0:T(8,128)(2,1)}, bf16[4,32,4608]{2,1,0:T(8,128)(2,1)}, u32[]{:S(2)}, u32[]{:S(2)}) collective-permute-start(bf16[4,32,4608]{2,1,0:T(8,128)(2,1)} %stack_z.5.refs_0_), channel_id=1, source_target_pairs={{0,2},{1,3},{2,0},{3,1},{4,6},{5,7},{6,4},{7,5},{8,10},{9,11},{10,... | collective-permute-start | bytes 3538952 | tf_op jit(solution)/shard_map/ppermute | solution.py:55
  107.6 32.3 %collective-permute-start.24 = (bf16[512,2048]{1,0:T(8,128)(2,1)S(1)}, bf16[512,2048]{1,0:T(8,128)(2,1)}, u32[]{:S(2)}, u32[]{:S(2)}) collective-permute-start(bf16[512,2048]{1,0:T(8,128)(2,1)S(1)} %convolution_convert_fusion.1.k.v), channel_id=1, source_target_pairs={{0,1},{1,2},{2,3},{4,5},{5,6},{6,7},{8,9},{9,10},{10,11},{12,13},{... | collective-permute-start | bytes 6291464 | tf_op jit(solution)/shard_map/ppermute | solution.py:294
  111.3 28.6 %collective-permute-start.20 = (bf16[4,32,4608]{2,1,0:T(8,128)(2,1)}, bf16[4,32,4608]{2,1,0:T(8,128)(2,1)}, u32[]{:S(2)}, u32[]{:S(2)}) collective-permute-start(bf16[4,32,4608]{2,1,0:T(8,128)(2,1)} %collective-permute-done.8.refs_1_), channel_id=1, source_target_pairs={{0,4},{1,5},{2,6},{3,7},{4,0},{5,1},{6,2},{7,3},{8,12},{9,13},{10,... | collective-permute-start | bytes 3538952 | tf_op jit(solution)/shard_map/ppermute | solution.py:55
  145.1 29.2 %collective-permute-start.30 = (bf16[32,4096]{1,0:T(8,128)(2,1)}, bf16[32,4096]{1,0:T(8,128)(2,1)}, u32[]{:S(2)}, u32[]{:S(2)}) collective-permute-start(bf16[32,4096]{1,0:T(8,128)(2,1)} %get-tuple-element.207.refs_0_), channel_id=1, source_target_pairs={{0,16},{1,17},{2,18},{3,19},{4,20},{5,21},{6,22},{7,23},{8,24},{9,... | collective-permute-start | bytes 786440 | tf_op jit(solution)/shard_map/ppermute | solution.py:55
  147.4 49.5 %collective-permute-start.33 = (bf16[4,32,4096]{2,1,0:T(8,128)(2,1)}, bf16[4,32,4096]{2,1,0:T(8,128)(2,1)}, u32[]{:S(2)}, u32[]{:S(2)}) collective-permute-start(bf16[4,32,4096]{2,1,0:T(8,128)(2,1)} %stack_z.6.refs_4_.refs_12_), channel_id=1, source_target_pairs={{0,1},{1,0},{2,3},{3,2},{4,5},{5,4},{6,7},{7,6},{8,9},{9,8},{10,11... | collective-permute-start | bytes 3145736 | tf_op jit(solution)/shard_map/ppermute | solution.py:55
  147.6 26.7 %collective-permute-start.29 = (bf16[4,32,4096]{2,1,0:T(8,128)(2,1)}, bf16[4,32,4096]{2,1,0:T(8,128)(2,1)}, u32[]{:S(2)}, u32[]{:S(2)}) collective-permute-start(bf16[4,32,4096]{2,1,0:T(8,128)(2,1)} %stack_z.6.refs_4_.refs_12_), channel_id=1, source_target_pairs={{0,4},{1,3},{2,6},{3,1},{4,0},{5,7},{6,2},{7,5},{8,12},{9,11},{10,... | collective-permute-start | bytes 3145736 | tf_op jit(solution)/shard_map/ppermute | solution.py:55
  149.1 25.2 %collective-permute-start.28 = (bf16[4,32,4096]{2,1,0:T(8,128)(2,1)}, bf16[4,32,4096]{2,1,0:T(8,128)(2,1)}, u32[]{:S(2)}, u32[]{:S(2)}) collective-permute-start(bf16[4,32,4096]{2,1,0:T(8,128)(2,1)} %stack_z.6.refs_4_.refs_12_), channel_id=1, source_target_pairs={{0,2},{1,5},{2,0},{3,7},{4,6},{5,1},{6,4},{7,3},{8,10},{9,13},{10,... | collective-permute-start | bytes 3145736 | tf_op jit(solution)/shard_map/ppermute | solution.py:55
  198.1 25.7 %collective-permute-start.38 = (bf16[4,32,4096]{2,1,0:T(8,128)(2,1)S(1)}, bf16[4,32,4096]{2,1,0:T(8,128)(2,1)S(1)}, u32[]{:S(2)}, u32[]{:S(2)}) collective-permute-start(bf16[4,32,4096]{2,1,0:T(8,128)(2,1)S(1)} %copy-done.47), channel_id=1, source_target_pairs={{0,4},{1,3},{2,6},{3,1},{4,0},{5,7},{6,2},{7,5},{8,12},{9,11},{10,... | collective-permute-start | bytes 3145736 | tf_op jit(solution)/shard_map/ppermute | solution.py:55
  243.0 28.6 %collective-permute-start.44 = (bf16[2,4,32,4096]{3,2,1,0:T(8,128)(2,1)S(1)}, bf16[2,4,32,4096]{3,2,1,0:T(8,128)(2,1)}, u32[]{:S(2)}, u32[]{:S(2)}) collective-permute-start(bf16[2,4,32,4096]{3,2,1,0:T(8,128)(2,1)S(1)} %fusion.4), channel_id=1, source_target_pairs={{0,4},{1,3},{2,6},{3,1},{4,0},{5,7},{6,2},{7,5},{8,12},{9,11},{10,... | collective-permute-start | bytes 6291464 | tf_op jit(solution)/shard_map/ppermute | solution.py:55
  281.6 37.6 %collective-permute-start.48 = (bf16[2,4,32,4096]{3,2,1,0:T(8,128)(2,1)}, bf16[2,4,32,4096]{3,2,1,0:T(8,128)(2,1)}, u32[]{:S(2)}, u32[]{:S(2)}) collective-permute-start(bf16[2,4,32,4096]{3,2,1,0:T(8,128)(2,1)} %fusion.5), channel_id=1, source_target_pairs={{0,4},{1,3},{2,6},{3,1},{4,0},{5,7},{6,2},{7,5},{8,12},{9,11},{10,... | collective-permute-start | bytes 6291464 | tf_op jit(solution)/shard_map/ppermute | solution.py:55
  284.5 26.2 %collective-permute-start.47 = (bf16[1,4,32,4096]{3,2,1,0:T(8,128)(2,1)S(1)}, bf16[1,4,32,4096]{3,2,1,0:T(8,128)(2,1)S(1)}, u32[]{:S(2)}, u32[]{:S(2)}) collective-permute-start(bf16[1,4,32,4096]{3,2,1,0:T(8,128)(2,1)S(1)} %fusion.12), channel_id=1, source_target_pairs={{0,2},{1,5},{2,0},{3,7},{4,6},{5,1},{6,4},{7,3},{8,10},{9,13},{10,... | collective-permute-start | bytes 3145736 | tf_op jit(solution)/shard_map/ppermute | solution.py:55
  345.0 28.9 %collective-permute-start.53 = (bf16[2,512,1024]{2,1,0:T(8,128)(2,1)}, bf16[2,512,1024]{2,1,0:T(8,128)(2,1)}, u32[]{:S(2)}, u32[]{:S(2)}) collective-permute-start(bf16[2,512,1024]{2,1,0:T(8,128)(2,1)} %get-tuple-element.279), channel_id=1, source_target_pairs={{1,0},{2,1},{3,2},{5,4},{6,5},{7,6},{9,8},{10,9},{11,10},{13,12},{... | collective-permute-start | bytes 6291464 | tf_op jit(solution)/shard_map/ppermute | solution.py:294
  347.2 26.7 %collective-permute-start.55 = (bf16[2,32,4096]{2,1,0:T(8,128)(2,1)}, bf16[2,32,4096]{2,1,0:T(8,128)(2,1)}, u32[]{:S(2)}, u32[]{:S(2)}) collective-permute-start(bf16[2,32,4096]{2,1,0:T(8,128)(2,1)} %fusion.23), channel_id=1, source_target_pairs={{0,16},{1,17},{2,18},{3,19},{4,20},{5,21},{6,22},{7,23},{8,24},{9,... | collective-permute-start | bytes 1572872 | tf_op jit(solution)/shard_map/ppermute | solution.py:55
  376.9 37.4 %collective-permute-start.57 = (bf16[2,4,32,4096]{3,2,1,0:T(8,128)(2,1)S(1)}, bf16[2,4,32,4096]{3,2,1,0:T(8,128)(2,1)}, u32[]{:S(2)}, u32[]{:S(2)}) collective-permute-start(bf16[2,4,32,4096]{3,2,1,0:T(8,128)(2,1)S(1)} %fusion.6), channel_id=1, source_target_pairs={{0,4},{1,3},{2,6},{3,1},{4,0},{5,7},{6,2},{7,5},{8,12},{9,11},{10,... | collective-permute-start | bytes 6291464 | tf_op jit(solution)/shard_map/ppermute | solution.py:55
  380.9 27.5 %collective-permute-start.56 = (bf16[1,4,32,4096]{3,2,1,0:T(8,128)(2,1)S(1)}, bf16[1,4,32,4096]{3,2,1,0:T(8,128)(2,1)}, u32[]{:S(2)}, u32[]{:S(2)}) collective-permute-start(bf16[1,4,32,4096]{3,2,1,0:T(8,128)(2,1)S(1)} %fusion.10), channel_id=1, source_target_pairs={{0,2},{1,5},{2,0},{3,7},{4,6},{5,1},{6,4},{7,3},{8,10},{9,13},{10,... | collective-permute-start | bytes 3145736 | tf_op jit(solution)/shard_map/ppermute | solution.py:55
  416.7 40.1 %collective-permute-start.60 = (bf16[1,4,32,4096]{3,2,1,0:T(8,128)(2,1)S(1)}, bf16[1,4,32,4096]{3,2,1,0:T(8,128)(2,1)S(1)}, u32[]{:S(2)}, u32[]{:S(2)}) collective-permute-start(bf16[1,4,32,4096]{3,2,1,0:T(8,128)(2,1)S(1)} %fusion.9), channel_id=1, source_target_pairs={{0,2},{1,5},{2,0},{3,7},{4,6},{5,1},{6,4},{7,3},{8,10},{9,13},{10,... | collective-permute-start | bytes 3145736 | tf_op jit(solution)/shard_map/ppermute | solution.py:55
  425.8 30.9 %collective-permute-start.61 = (bf16[2,4,32,4608]{3,2,1,0:T(8,128)(2,1)S(1)}, bf16[2,4,32,4608]{3,2,1,0:T(8,128)(2,1)S(1)}, u32[]{:S(2)}, u32[]{:S(2)}) collective-permute-start(bf16[2,4,32,4608]{3,2,1,0:T(8,128)(2,1)S(1)} %fusion), channel_id=1, source_target_pairs={{0,4},{1,3},{2,6},{3,1},{4,0},{5,7},{6,2},{7,5},{8,12},{9,11},{10,... | collective-permute-start | bytes 7077896 | tf_op jit(solution)/shard_map/ppermute | solution.py:55
  429.7 27.0 %collective-permute-start.62 = (bf16[2,32,4096]{2,1,0:T(8,128)(2,1)S(1)}, bf16[2,32,4096]{2,1,0:T(8,128)(2,1)S(1)}, u32[]{:S(2)}, u32[]{:S(2)}) collective-permute-start(bf16[2,32,4096]{2,1,0:T(8,128)(2,1)S(1)} %fusion.24), channel_id=1, source_target_pairs={{0,16},{1,17},{2,18},{3,19},{4,20},{5,21},{6,22},{7,23},{8,24},{9,... | collective-permute-start | bytes 1572872 | tf_op jit(solution)/shard_map/ppermute | solution.py:55
  (116 other events, 1470.7 us)

commit v5 on v4

--- a/solution.py
+++ b/solution.py
@@ -1156,7 +1156,6 @@
         second_d, end_b, gbias = join(second_d, end_b, gbias)
         up_sum, down_sum = finish_mlp(end_a, end_b)
         end_d = over_z(last[0], got_d, first_d, second_d)
-        pair_c, up_sum = join(pair_c, up_sum)
         end_c = within_pair(*pair_c)
         position_table_grad = exchange(gbias, Z_FAR)
         first, last = finish(end_c), finish(end_d)

time: 533 us -> 537 us (level)
    unnamed x134 -> x138, local copies, waits for them, and re-layouts: 17.7 us -> 17.9 us
  transfers between devices with their start and end apart: 74 -> 74, of which waited for: 31 -> 28; matrix products, arithmetic and copies ran while one was open for 14% -> 14% of each run, Pallas kernels for 31% -> 31%
where the time goes in v5:
time: 537 us; the launch traced here: 529 us
  waiting for transfers between devices  178 us (33%)
  Pallas kernels  171 us (32%)
  starting transfers between devices  70.6 us (13%)
  other arithmetic  57.2 us (11%)
  local copies, waits for them, and re-layouts  32.9 us (6%)
  matrix products  18.1 us (3%)
    ppermute x72, waiting for transfers between devices, send(): return lax.ppermute(v, AX, pairs)  178 us
    ppermute x72, starting transfers between devices, send(): return lax.ppermute(v, AX, pairs)  66.2 us
    pallas_call x2, Pallas kernels, mlp_half(): pl.pallas_call(functools.partial(mlp_body, last, spot_of, alternate), gri...  50.1 us
    convert_element_type x17, other arithmetic, low(): return v.astype(jnp.bfloat16)  35 us
    pallas_call x4, Pallas kernels, weight_grads(): pl.pallas_call(body, grid=(1,), in_specs=whole + kept, out_specs=[pl.Bloc...  27 us
    pallas_call x1, Pallas kernels, attention_back(): pl.pallas_call(attention_back_body, grid=(HEADS,), in_specs=[head_block(0...  22.5 us
    dot_general x8, matrix products, dot(): lax.dot_general(a, b, (dims, ((), ())), preferred_element_type=jnp.float32)  18.1 us
    unnamed x138, local copies, waits for them, and re-layouts  17.9 us
  transfers between devices with their start and end apart: 74, of which 28 were waited for; matrix products, arithmetic and copies ran while one was open for 14% of the time, Pallas kernels for 31%

profile of v5, /device:TPU:0, one launch (start us, length us, event | category | flops | bytes accessed | tf_op | source)
XLA Modules:
  0.0 529.4 jit_solution(4596843096082756326)
XLA Ops:
  14.5 14.9 %collective-permute-done.1.refs_2_ = bf16[32,3968]{1,0:T(8,128)(2,1)S(1)} collective-permute-done((bf16[32,3968]{1,0:T(8,128)(2,1)}, bf16[32,3968]{1,0:T(8,128)(2,1)S(1)}, u32[]{:S(2)}, u32[]{:S(2)}) %collective-permute-start.1) | collective-permute-done | bytes 253984 | tf_op jit(solution)/shard_map/ppermute | solution.py:55
  43.7 19.6 %collective-permute-done.6.refs_2_ = bf16[32,4608]{1,0:T(8,128)(2,1)S(1)} collective-permute-done((bf16[32,4608]{1,0:T(8,128)(2,1)}, bf16[32,4608]{1,0:T(8,128)(2,1)S(1)}, u32[]{:S(2)}, u32[]{:S(2)}) %collective-permute-start.6) | collective-permute-done | bytes 294944 | tf_op jit(solution)/shard_map/ppermute | solution.py:55
  67.0 8.7 %collective-permute-done.14.refs_1_ = bf16[32,4096]{1,0:T(8,128)(2,1)} collective-permute-done((bf16[32,4096]{1,0:T(8,128)(2,1)}, bf16[32,4096]{1,0:T(8,128)(2,1)}, u32[]{:S(2)}, u32[]{:S(2)}) %collective-permute-start.14) | collective-permute-done | bytes 262176 | tf_op jit(solution)/shard_map/ppermute | solution.py:55
  84.1 5.4 %assemble.2 = (bf16[4,2,2,2,32,384]{5,4,3,2,1,0:T(8,128)(2,1)}, bf16[4,2,2,2,32,2048]{5,4,3,2,1,0:T(8,128)(2,1)}, bf16[4,2,2,2,32,512]{5,4,3,2,1,0:T(8,128)(2,1)S(1)}, bf16[4,2,2,2,32,1024]{5,4,3,2,1,0:T(8,128)(2,1)S(1)}) custom-call(bf16[4,32,3968]{2,1,0:T(8,128)(2,1)S(1)} %copy-done.9, bf16[4,32,3968]{2,1,0:T(8,128)(2,1)S(1)} %copy-done.20, ...), custom_call_target="tpu_custom_call" | custom-call | tf_op jit(solution)/shard_map/assemble/pallas_call | solution.py:110
  97.7 7.0 %state_attention.1 = (bf16[512,1024]{1,0:T(8,128)(2,1)S(1)}, f32[8,1,512]{2,1,0:T(1,128)S(1)}) custom-call(bf16[512,2048]{1,0:T(8,128)(2,1)S(1)} %convolution_convert_fusion.1.k.v, bf16[512,2048]{1,0:T(8,128)(2,1)S(1)} %convolution_convert_fusion.1.k.v, bf16[1024,512]{1,0:T(8,128)(2,1)S(1)} %bitcast.143), custom_call_target="tpu_custom_call" | custom-call | flops 1073741824 | bytes 4194304 | tf_op jit(solution)/shard_map/state_attention/pallas_call | solution.py:481
  118.7 6.3 %collective-permute-done.25.refs_1_ = bf16[32,4096]{1,0:T(8,128)(2,1)} collective-permute-done((bf16[32,4096]{1,0:T(8,128)(2,1)}, bf16[32,4096]{1,0:T(8,128)(2,1)}, u32[]{:S(2)}, u32[]{:S(2)}) %collective-permute-start.25) | collective-permute-done | bytes 262176 | tf_op jit(solution)/shard_map/ppermute | solution.py:55
  127.2 12.7 %collective-permute-done.20.refs_3_ = bf16[4,32,4608]{2,1,0:T(8,128)(2,1)} collective-permute-done((bf16[4,32,4608]{2,1,0:T(8,128)(2,1)}, bf16[4,32,4608]{2,1,0:T(8,128)(2,1)}, u32[]{:S(2)}, u32[]{:S(2)}) %collective-permute-start.20) | collective-permute-done | bytes 1179680 | tf_op jit(solution)/shard_map/ppermute | solution.py:55
  139.9 5.1 collective-permute-start.26
  155.4 6.5 %assemble.3 = (bf16[4,2,2,2,32,1024]{5,4,3,2,1,0:T(8,128)(2,1)S(1)}, bf16[4,2,2,2,32,512]{5,4,3,2,1,0:T(8,128)(2,1)S(1)}, bf16[4,2,2,2,32,2048]{5,4,3,2,1,0:T(8,128)(2,1)}, bf16[4,2,2,2,32,1024]{5,4,3,2,1,0:T(8,128)(2,1)}) custom-call(bf16[4,32,4608]{2,1,0:T(8,128)(2,1)S(1)} %copy-done.5, bf16[4,32,4608]{2,1,0:T(8,128)(2,1)} %collective-permute-done.8.refs_1_, ...), custom_call_target="tpu_custom_call" | custom-call | tf_op jit(solution)/shard_map/assemble/pallas_call | solution.py:110
  180.3 14.0 %attention.1 = (bf16[512,1024]{1,0:T(8,128)(2,1)S(1)}, f32[8,1,512]{2,1,0:T(1,128)S(1)}) custom-call(bf16[512,1024]{1,0:T(8,128)(2,1)S(1)} %convolution_convert_fusion.4.q, bf16[512,2048]{1,0:T(8,128)(2,1)S(1)} %convolution_convert_fusion.1.k.v, bf16[512,2048]{1,0:T(8,128)(2,1)S(1)} %convolution_convert_fusion.1.k.v, ...), custom_call_target="tpu_custom_call" | custom-call | flops 3221225472 | bytes 9437184 | tf_op jit(solution)/shard_map/attention/pallas_call | solution.py:387
  200.0 23.7 %mlp_half.2 = (bf16[512,4096]{1,0:T(8,128)(2,1)}, bf16[512,4096]{1,0:T(8,128)(2,1)}, f32[1024,128]{1,0:T(8,128)}, f32[512,1024]{1,0:T(8,128)}, f32[512,1024]{1,0:T(8,128)}) custom-call(f32[512,1024]{1,0:T(8,128)} %convolution_add_fusion.refs_0_, bf16[512,1024]{1,0:T(8,128)(2,1)} %refs_1_.3, f32[8,1024]{1,0:T(8,128)} %copy-done.21, ...), custom_call_target="tpu_custom_call" | custom-call | flops 12884901888 | bytes 31457280 | tf_op jit(solution)/shard_map/mlp_half/pallas_call | solution.py:653
  245.2 26.4 %mlp_half.3 = (bf16[512,4096]{1,0:T(8,128)(2,1)}, bf16[512,4096]{1,0:T(8,128)(2,1)}, f32[1024,128]{1,0:T(8,128)}, bf16[512,1024]{1,0:T(8,128)(2,1)}, f32[512,102...) custom-call(f32[512,1024]{1,0:T(8,128)} %convolution_add_fusion.refs_0_, bf16[512,1024]{1,0:T(8,128)(2,1)} %refs_1_.3, ...), custom_call_target="tpu_custom_call" | custom-call | flops 12884901888 | bytes 31457280 | tf_op jit(solution)/shard_map/mlp_half/pallas_call | solution.py:653
  286.2 22.5 %attention_back.1 = (bf16[512,1024]{1,0:T(8,128)(2,1)S(1)}, f32[2,512,1024]{2,1,0:T(8,128)}, bf16[2,512,1024]{2,1,0:T(8,128)(2,1)}, bf16[2,512,1024]{2,1,0:T(8,128)(2,1)}, f32[8,1,512]{2,1,0:T(1,128)S(1)}) custom-call(bf16[512,1024]{1,0:T(8,128)(2,1)S(1)} %convolution_convert_fusion.4.q, bf16[512,2048]{1,0:T(8,128)(2,1)} %copy-done, ...), custom_call_target="tpu_custom_call" | custom-call | flops 8053063680 | bytes 18874368 | tf_op jit(solution)/shard_map/attention_back/pallas_call | solution.py:442
  310.7 8.5 %collective-permute-done.48 = bf16[2,4,32,4096]{3,2,1,0:T(8,128)(2,1)} collective-permute-done((bf16[2,4,32,4096]{3,2,1,0:T(8,128)(2,1)}, bf16[2,4,32,4096]{3,2,1,0:T(8,128)(2,1)}, u32[]{:S(2)}, u32[]{:S(2)}) %collective-permute-start.48) | collective-permute-done | bytes 2097184 | tf_op jit(solution)/shard_map/ppermute | solution.py:55
  328.6 11.2 %weight_grads.4 = (bf16[512,4096]{1,0:T(8,128)(2,1)}, bf16[512,4096]{1,0:T(8,128)(2,1)}) custom-call(bf16[512,1024]{1,0:T(8,128)(2,1)} %copy-done.29, bf16[512,1024]{1,0:T(8,128)(2,1)} %get-tuple-element.256.refs_1_, bf16[512,1024]{1,0:T(8,128)(2,1)} %copy-done.49, bf16[512,1024]{1,0:T(8,128)(2,1)} %get-tuple-element.344.refs_3_, ...), custom_call_target="tpu_custom_call" | custom-call | flops 4294967296 | bytes 16777216 | tf_op jit(solution)/shard_map/weight_grads/pallas_call | solution.py:758
  354.6 10.5 %state_attention_back.1 = (f32[2,512,1024]{2,1,0:T(8,128)S(1)}, bf16[1024,512]{1,0:T(8,128)(2,1)S(1)}) custom-call(bf16[512,2048]{1,0:T(8,128)(2,1)S(1)} %copy-done.1, bf16[512,2048]{1,0:T(8,128)(2,1)S(1)} %copy-done.1, bf16[1024,512]{1,0:T(8,128)(2,1)S(1)} %bitcast.144, f32[8,1,512]{2,1,0:T(1,128)S(1)} %get-tuple-element.259.lse, ...), custom_call_target="tpu_custom_call" | custom-call | flops 2684354560 | bytes 14680064 | tf_op jit(solution)/shard_map/state_attention_back/pallas_call | solution.py:512
  367.8 6.1 %weight_grads.5 = (bf16[512,4608]{1,0:T(8,128)(2,1)}, bf16[512,4608]{1,0:T(8,128)(2,1)}) custom-call(bf16[512,1024]{1,0:T(8,128)(2,1)} %copy-done.13, bf16[512,1024]{1,0:T(8,128)(2,1)} %copy-done.45, bf16[1024,512]{1,0:T(8,128)(2,1)} %copy-done.14, f32[512,1024]{1,0:T(8,128)} %get-tuple-element.342.refs_3_), custom_call_target="tpu_custom_call" | custom-call | flops 1073741824 | bytes 8388608 | tf_op jit(solution)/shard_map/weight_grads/pallas_call | solution.py:758
  387.6 6.4 %weight_grads.6 = (bf16[512,4608]{1,0:T(8,128)(2,1)}, bf16[512,4608]{1,0:T(8,128)(2,1)}) custom-call(bf16[512,1024]{1,0:T(8,128)(2,1)} %copy-done.41, bf16[512,1024]{1,0:T(8,128)(2,1)} %get-tuple-element.337.k.refs_1_, bf16[512,1024]{1,0:T(8,128)(2,1)} %get-tuple-element.336.v.refs_2_, ...), custom_call_target="tpu_custom_call", output_to_operand_aliasing={{0}: (3, {}), {1}: (4, {})} | custom-call | flops 2147483648 | bytes 8388608 | tf_op jit(solution)/shard_map/weight_grads/pallas_call | solution.py:758
  394.1 9.4 %embedding_back.1 = (f32[512,1024]{1,0:T(8,128)}, bf16[512,1024]{1,0:T(8,128)(2,1)S(1)}, f32[8,1024]{1,0:T(8,128)S(1)}) custom-call(bf16[512,1024]{1,0:T(8,128)(2,1)S(1)} %copy-done.17, bf16[512,1024]{1,0:T(8,128)(2,1)S(1)} %copy-done.3, bf16[512,1024]{1,0:T(8,128)(2,1)S(1)} %copy-done.2, bf16[1024,1024]{1,0:T(8,128)(2,1)} %bitcast.145, ...), custom_call_target="tpu_custom_call" | custom-call | flops 3221225472 | bytes 18874368 | tf_op jit(solution)/shard_map/embedding_back/pallas_call | solution.py:895
  408.4 6.0 %collective-permute-done.57 = bf16[2,4,32,4096]{3,2,1,0:T(8,128)(2,1)} collective-permute-done((bf16[2,4,32,4096]{3,2,1,0:T(8,128)(2,1)S(1)}, bf16[2,4,32,4096]{3,2,1,0:T(8,128)(2,1)}, u32[]{:S(2)}, u32[]{:S(2)}) %collective-permute-start.57) | collective-permute-done | bytes 2097184 | tf_op jit(solution)/shard_map/ppermute | solution.py:55
  435.0 21.7 %collective-permute-done.64 = f32[8,512]{1,0:T(8,128)S(1)} collective-permute-done((f32[8,512]{1,0:T(8,128)S(1)}, f32[8,512]{1,0:T(8,128)S(1)}, u32[]{:S(2)}, u32[]{:S(2)}) %collective-permute-start.64) | collective-permute-done | bytes 16416 | tf_op jit(solution)/shard_map/ppermute | solution.py:55
  473.0 9.0 %collective-permute-done.67 = f32[8,512]{1,0:T(8,128)S(1)} collective-permute-done((f32[8,512]{1,0:T(8,128)S(1)}, f32[8,512]{1,0:T(8,128)S(1)}, u32[]{:S(2)}, u32[]{:S(2)}) %collective-permute-start.67) | collective-permute-done | bytes 16416 | tf_op jit(solution)/shard_map/ppermute | solution.py:55
  482.0 6.9 %collective-permute-done.71 = bf16[2,32,4096]{2,1,0:T(8,128)(2,1)} collective-permute-done((bf16[2,32,4096]{2,1,0:T(8,128)(2,1)}, bf16[2,32,4096]{2,1,0:T(8,128)(2,1)}, u32[]{:S(2)}, u32[]{:S(2)}) %collective-permute-start.71) | collective-permute-done | bytes 524320 | tf_op jit(solution)/shard_map/ppermute | solution.py:55
  504.9 18.8 %collective-permute-done.73 = f32[8,512]{1,0:T(8,128)S(1)} collective-permute-done((f32[8,512]{1,0:T(8,128)S(1)}, f32[8,512]{1,0:T(8,128)S(1)}, u32[]{:S(2)}, u32[]{:S(2)}) %collective-permute-start.73) | collective-permute-done | bytes 16416 | tf_op jit(solution)/shard_map/ppermute | solution.py:55
  (355 shorter events, 240.1 us)
Async XLA Ops:
  32.5 30.8 %collective-permute-start.4 = (bf16[4,32,3968]{2,1,0:T(8,128)(2,1)}, bf16[4,32,3968]{2,1,0:T(8,128)(2,1)S(1)}, u32[]{:S(2)}, u32[]{:S(2)}) collective-permute-start(bf16[4,32,3968]{2,1,0:T(8,128)(2,1)} %stack_z.4.refs_0_), channel_id=1, source_target_pairs={{0,4},{1,3},{2,6},{3,1},{4,0},{5,7},{6,2},{7,5},{8,12},{9,11},{10,... | collective-permute-start | bytes 3047432 | tf_op jit(solution)/shard_map/ppermute | solution.py:55
  34.1 29.2 %collective-permute-start.3 = (bf16[4,32,3968]{2,1,0:T(8,128)(2,1)}, bf16[4,32,3968]{2,1,0:T(8,128)(2,1)S(1)}, u32[]{:S(2)}, u32[]{:S(2)}) collective-permute-start(bf16[4,32,3968]{2,1,0:T(8,128)(2,1)} %stack_z.4.refs_0_), channel_id=1, source_target_pairs={{0,2},{1,5},{2,0},{3,7},{4,6},{5,1},{6,4},{7,3},{8,10},{9,13},{10,... | collective-permute-start | bytes 3047432 | tf_op jit(solution)/shard_map/ppermute | solution.py:55
  35.6 27.7 %collective-permute-start.6 = (bf16[32,4608]{1,0:T(8,128)(2,1)}, bf16[32,4608]{1,0:T(8,128)(2,1)S(1)}, u32[]{:S(2)}, u32[]{:S(2)}) collective-permute-start(bf16[32,4608]{1,0:T(8,128)(2,1)} %get-tuple-element.181.refs_0_), channel_id=1, source_target_pairs={{0,16},{1,17},{2,18},{3,19},{4,20},{5,21},{6,22},{7,23},{8,24},{9,... | collective-permute-start | bytes 884744 | tf_op jit(solution)/shard_map/ppermute | solution.py:55
  78.7 28.6 %collective-permute-start.15 = (bf16[32,4096]{1,0:T(8,128)(2,1)}, bf16[32,4096]{1,0:T(8,128)(2,1)}, u32[]{:S(2)}, u32[]{:S(2)}) collective-permute-start(bf16[32,4096]{1,0:T(8,128)(2,1)} %get-tuple-element.188.refs_0_), channel_id=1, source_target_pairs={{0,16},{1,17},{2,18},{3,19},{4,20},{5,21},{6,22},{7,23},{8,24},{9,... | collective-permute-start | bytes 786440 | tf_op jit(solution)/shard_map/ppermute | solution.py:55
  78.7 32.7 %collective-permute-start.21 = (bf16[4,32,4608]{2,1,0:T(8,128)(2,1)}, bf16[4,32,4608]{2,1,0:T(8,128)(2,1)}, u32[]{:S(2)}, u32[]{:S(2)}) collective-permute-start(bf16[4,32,4608]{2,1,0:T(8,128)(2,1)} %stack_z.5.refs_0_), channel_id=1, source_target_pairs={{0,1},{1,0},{2,3},{3,2},{4,5},{5,4},{6,7},{7,6},{8,9},{9,8},{10,11... | collective-permute-start | bytes 3538952 | tf_op jit(solution)/shard_map/ppermute | solution.py:55
  79.2 28.2 %collective-permute-start.9 = (bf16[4,32,4608]{2,1,0:T(8,128)(2,1)}, bf16[4,32,4608]{2,1,0:T(8,128)(2,1)}, u32[]{:S(2)}, u32[]{:S(2)}) collective-permute-start(bf16[4,32,4608]{2,1,0:T(8,128)(2,1)} %stack_z.5.refs_0_), channel_id=1, source_target_pairs={{0,4},{1,5},{2,6},{3,7},{4,0},{5,1},{6,2},{7,3},{8,12},{9,13},{10,... | collective-permute-start | bytes 3538952 | tf_op jit(solution)/shard_map/ppermute | solution.py:55
  79.7 27.9 %collective-permute-start.8 = (bf16[4,32,4608]{2,1,0:T(8,128)(2,1)}, bf16[4,32,4608]{2,1,0:T(8,128)(2,1)}, u32[]{:S(2)}, u32[]{:S(2)}) collective-permute-start(bf16[4,32,4608]{2,1,0:T(8,128)(2,1)} %stack_z.5.refs_0_), channel_id=1, source_target_pairs={{0,2},{1,3},{2,0},{3,1},{4,6},{5,7},{6,4},{7,5},{8,10},{9,11},{10,... | collective-permute-start | bytes 3538952 | tf_op jit(solution)/shard_map/ppermute | solution.py:55
  107.6 32.3 %collective-permute-start.24 = (bf16[512,2048]{1,0:T(8,128)(2,1)S(1)}, bf16[512,2048]{1,0:T(8,128)(2,1)}, u32[]{:S(2)}, u32[]{:S(2)}) collective-permute-start(bf16[512,2048]{1,0:T(8,128)(2,1)S(1)} %convolution_convert_fusion.1.k.v), channel_id=1, source_target_pairs={{0,1},{1,2},{2,3},{4,5},{5,6},{6,7},{8,9},{9,10},{10,11},{12,13},{... | collective-permute-start | bytes 6291464 | tf_op jit(solution)/shard_map/ppermute | solution.py:294
  111.3 28.6 %collective-permute-start.20 = (bf16[4,32,4608]{2,1,0:T(8,128)(2,1)}, bf16[4,32,4608]{2,1,0:T(8,128)(2,1)}, u32[]{:S(2)}, u32[]{:S(2)}) collective-permute-start(bf16[4,32,4608]{2,1,0:T(8,128)(2,1)} %collective-permute-done.8.refs_1_), channel_id=1, source_target_pairs={{0,4},{1,5},{2,6},{3,7},{4,0},{5,1},{6,2},{7,3},{8,12},{9,13},{10,... | collective-permute-start | bytes 3538952 | tf_op jit(solution)/shard_map/ppermute | solution.py:55
  145.1 29.2 %collective-permute-start.30 = (bf16[32,4096]{1,0:T(8,128)(2,1)}, bf16[32,4096]{1,0:T(8,128)(2,1)}, u32[]{:S(2)}, u32[]{:S(2)}) collective-permute-start(bf16[32,4096]{1,0:T(8,128)(2,1)} %get-tuple-element.204.refs_0_), channel_id=1, source_target_pairs={{0,16},{1,17},{2,18},{3,19},{4,20},{5,21},{6,22},{7,23},{8,24},{9,... | collective-permute-start | bytes 786440 | tf_op jit(solution)/shard_map/ppermute | solution.py:55
  147.4 49.5 %collective-permute-start.33 = (bf16[4,32,4096]{2,1,0:T(8,128)(2,1)}, bf16[4,32,4096]{2,1,0:T(8,128)(2,1)}, u32[]{:S(2)}, u32[]{:S(2)}) collective-permute-start(bf16[4,32,4096]{2,1,0:T(8,128)(2,1)} %stack_z.6.refs_4_.refs_12_), channel_id=1, source_target_pairs={{0,1},{1,0},{2,3},{3,2},{4,5},{5,4},{6,7},{7,6},{8,9},{9,8},{10,11... | collective-permute-start | bytes 3145736 | tf_op jit(solution)/shard_map/ppermute | solution.py:55
  147.6 26.7 %collective-permute-start.29 = (bf16[4,32,4096]{2,1,0:T(8,128)(2,1)}, bf16[4,32,4096]{2,1,0:T(8,128)(2,1)}, u32[]{:S(2)}, u32[]{:S(2)}) collective-permute-start(bf16[4,32,4096]{2,1,0:T(8,128)(2,1)} %stack_z.6.refs_4_.refs_12_), channel_id=1, source_target_pairs={{0,4},{1,3},{2,6},{3,1},{4,0},{5,7},{6,2},{7,5},{8,12},{9,11},{10,... | collective-permute-start | bytes 3145736 | tf_op jit(solution)/shard_map/ppermute | solution.py:55
  243.0 28.6 %collective-permute-start.44 = (bf16[2,4,32,4096]{3,2,1,0:T(8,128)(2,1)S(1)}, bf16[2,4,32,4096]{3,2,1,0:T(8,128)(2,1)}, u32[]{:S(2)}, u32[]{:S(2)}) collective-permute-start(bf16[2,4,32,4096]{3,2,1,0:T(8,128)(2,1)S(1)} %fusion.4), channel_id=1, source_target_pairs={{0,4},{1,3},{2,6},{3,1},{4,0},{5,7},{6,2},{7,5},{8,12},{9,11},{10,... | collective-permute-start | bytes 6291464 | tf_op jit(solution)/shard_map/ppermute | solution.py:55
  281.6 37.6 %collective-permute-start.48 = (bf16[2,4,32,4096]{3,2,1,0:T(8,128)(2,1)}, bf16[2,4,32,4096]{3,2,1,0:T(8,128)(2,1)}, u32[]{:S(2)}, u32[]{:S(2)}) collective-permute-start(bf16[2,4,32,4096]{3,2,1,0:T(8,128)(2,1)} %fusion.5), channel_id=1, source_target_pairs={{0,4},{1,3},{2,6},{3,1},{4,0},{5,7},{6,2},{7,5},{8,12},{9,11},{10,... | collective-permute-start | bytes 6291464 | tf_op jit(solution)/shard_map/ppermute | solution.py:55
  345.0 28.9 %collective-permute-start.53 = (bf16[2,512,1024]{2,1,0:T(8,128)(2,1)}, bf16[2,512,1024]{2,1,0:T(8,128)(2,1)}, u32[]{:S(2)}, u32[]{:S(2)}) collective-permute-start(bf16[2,512,1024]{2,1,0:T(8,128)(2,1)} %get-tuple-element.276), channel_id=1, source_target_pairs={{1,0},{2,1},{3,2},{5,4},{6,5},{7,6},{9,8},{10,9},{11,10},{13,12},{... | collective-permute-start | bytes 6291464 | tf_op jit(solution)/shard_map/ppermute | solution.py:294
  347.2 26.7 %collective-permute-start.55 = (bf16[2,32,4096]{2,1,0:T(8,128)(2,1)}, bf16[2,32,4096]{2,1,0:T(8,128)(2,1)}, u32[]{:S(2)}, u32[]{:S(2)}) collective-permute-start(bf16[2,32,4096]{2,1,0:T(8,128)(2,1)} %fusion.23), channel_id=1, source_target_pairs={{0,16},{1,17},{2,18},{3,19},{4,20},{5,21},{6,22},{7,23},{8,24},{9,... | collective-permute-start | bytes 1572872 | tf_op jit(solution)/shard_map/ppermute | solution.py:55
  376.9 37.4 %collective-permute-start.57 = (bf16[2,4,32,4096]{3,2,1,0:T(8,128)(2,1)S(1)}, bf16[2,4,32,4096]{3,2,1,0:T(8,128)(2,1)}, u32[]{:S(2)}, u32[]{:S(2)}) collective-permute-start(bf16[2,4,32,4096]{3,2,1,0:T(8,128)(2,1)S(1)} %fusion.6), channel_id=1, source_target_pairs={{0,4},{1,3},{2,6},{3,1},{4,0},{5,7},{6,2},{7,5},{8,12},{9,11},{10,... | collective-permute-start | bytes 6291464 | tf_op jit(solution)/shard_map/ppermute | solution.py:55
  380.9 27.5 %collective-permute-start.56 = (bf16[1,4,32,4096]{3,2,1,0:T(8,128)(2,1)S(1)}, bf16[1,4,32,4096]{3,2,1,0:T(8,128)(2,1)}, u32[]{:S(2)}, u32[]{:S(2)}) collective-permute-start(bf16[1,4,32,4096]{3,2,1,0:T(8,128)(2,1)S(1)} %fusion.10), channel_id=1, source_target_pairs={{0,2},{1,5},{2,0},{3,7},{4,6},{5,1},{6,4},{7,3},{8,10},{9,13},{10,... | collective-permute-start | bytes 3145736 | tf_op jit(solution)/shard_map/ppermute | solution.py:55
  416.7 40.1 %collective-permute-start.60 = (bf16[1,4,32,4096]{3,2,1,0:T(8,128)(2,1)S(1)}, bf16[1,4,32,4096]{3,2,1,0:T(8,128)(2,1)S(1)}, u32[]{:S(2)}, u32[]{:S(2)}) collective-permute-start(bf16[1,4,32,4096]{3,2,1,0:T(8,128)(2,1)S(1)} %fusion.9), channel_id=1, source_target_pairs={{0,2},{1,5},{2,0},{3,7},{4,6},{5,1},{6,4},{7,3},{8,10},{9,13},{10,... | collective-permute-start | bytes 3145736 | tf_op jit(solution)/shard_map/ppermute | solution.py:55
  425.8 31.0 %collective-permute-start.61 = (bf16[2,4,32,4608]{3,2,1,0:T(8,128)(2,1)S(1)}, bf16[2,4,32,4608]{3,2,1,0:T(8,128)(2,1)S(1)}, u32[]{:S(2)}, u32[]{:S(2)}) collective-permute-start(bf16[2,4,32,4608]{3,2,1,0:T(8,128)(2,1)S(1)} %fusion), channel_id=1, source_target_pairs={{0,4},{1,3},{2,6},{3,1},{4,0},{5,7},{6,2},{7,5},{8,12},{9,11},{10,... | collective-permute-start | bytes 7077896 | tf_op jit(solution)/shard_map/ppermute | solution.py:55
  429.6 27.2 %collective-permute-start.62 = (bf16[2,32,4096]{2,1,0:T(8,128)(2,1)S(1)}, bf16[2,32,4096]{2,1,0:T(8,128)(2,1)S(1)}, u32[]{:S(2)}, u32[]{:S(2)}) collective-permute-start(bf16[2,32,4096]{2,1,0:T(8,128)(2,1)S(1)} %fusion.24), channel_id=1, source_target_pairs={{0,16},{1,17},{2,18},{3,19},{4,20},{5,21},{6,22},{7,23},{8,24},{9,... | collective-permute-start | bytes 1572872 | tf_op jit(solution)/shard_map/ppermute | solution.py:55
  493.7 30.6 %collective-permute-start.68 = (bf16[32,4608]{1,0:T(8,128)(2,1)}, bf16[32,4608]{1,0:T(8,128)(2,1)S(1)}, u32[]{:S(2)}, u32[]{:S(2)}) collective-permute-start(bf16[32,4608]{1,0:T(8,128)(2,1)} %get-tuple-element.338), channel_id=1, source_target_pairs={{0,8},{1,9},{2,10},{3,11},{4,12},{5,13},{6,14},{7,15},{8,16},{9,17... | collective-permute-start | bytes 884744 | tf_op jit(solution)/shard_map/ppermute | solution.py:55
  495.7 28.6 %collective-permute-start.70 = (bf16[32,4608]{1,0:T(8,128)(2,1)}, bf16[32,4608]{1,0:T(8,128)(2,1)S(1)}, u32[]{:S(2)}, u32[]{:S(2)}) collective-permute-start(bf16[32,4608]{1,0:T(8,128)(2,1)} %get-tuple-element.339), channel_id=1, source_target_pairs={{0,24},{1,25},{2,26},{3,27},{4,28},{5,29},{6,30},{7,31},{8,0},{9,1... | collective-permute-start | bytes 884744 | tf_op jit(solution)/shard_map/ppermute | solution.py:55
  497.5 26.8 %collective-permute-start.69 = (bf16[32,4608]{1,0:T(8,128)(2,1)S(1)}, bf16[32,4608]{1,0:T(8,128)(2,1)S(1)}, u32[]{:S(2)}, u32[]{:S(2)}) collective-permute-start(bf16[32,4608]{1,0:T(8,128)(2,1)S(1)} %get-tuple-element.340), channel_id=1, source_target_pairs={{0,16},{1,17},{2,18},{3,19},{4,20},{5,21},{6,22},{7,23},{8,24},{9,... | collective-permute-start | bytes 884744 | tf_op jit(solution)/shard_map/ppermute | solution.py:55
  (118 other events, 1483.5 us)
